TPU v7x, 512 devices: a whole 4x8x8 slice. The times are simulated.
512 devices in a mesh: group: 32 (over z, y_hi, core), tp: 16 (over y_lo, x).
Axes of the slice: x: 4, y: 8 (y_hi: 2, y_lo: 4; y = y_hi * 4 + y_lo), z: 8, core: 2. Of those that a mesh axis runs over, the one named last changes fastest.
Arguments:
- hidden: bfloat16 [64, 8, 5120], P('group', None, 'tp'), may hold values from -6 to 6
- query_weight: bfloat16 [5120, 4096], P('tp'), may hold values from -0.078125 to 0.078125
- key_value_weight: bfloat16 [5120, 1024], P('tp'), may hold values from -0.078125 to 0.078125
- query_codes: bfloat16 [5120, 4096], P('tp', 'group'), may hold values from -127 to 127
- query_scales: float32 [5120, 32], P('tp', 'group'), may hold values from 2e-05 to 0.0002
- key_value_codes: bfloat16 [16, 320, 1024], P('tp', 'group'), may hold values from -127 to 127
- key_value_scales: float32 [16, 320, 8], P('tp', 'group'), may hold values from 2e-05 to 0.0002
- key_cache: bfloat16 [4, 16, 64, 16, 512], P(None, 'tp', 'group'), may hold values from -150 to 150
- value_cache: bfloat16 [4, 16, 64, 16, 512], P(None, 'tp', 'group'), may hold values from -6 to 6
- lengths: int32 [64], P('group'), may hold values from 1 to 1024
- counts: int32 [64], P('group'), may hold values from 4 to 8
- learner: int32 [64, 8, 1], P('group'), may hold values from 0 to 31; in each aligned block of 16 rows (0 to 15, 16 to 31, ..., all dimensions but the last counted through in order) at most 2 rows name the same one
- token_ids: int32 [64, 8], P('group'), may hold values from 0 to 151935
Outputs:
- trajectory_rows: bfloat16 [32, 64, 4096], P('group', None, 'tp')
- trajectory_ids: int32 [32, 64], P('group')
Inputs may be any that keep to these rules, and one draw needn't show every extreme that they name: In the 16 rows of one rollout group, at most 2 name the same learner, and exactly 2 do so in some group.
All inputs are finite; a program needn't handle non-finite values.
Results may differ from a plain program's by a relative error of at most 0.012.
The roundings to bfloat16 on the way count: a program that leaves them out, or rounds other values in their place, can miss the bound.
Values may be sent and summed in bfloat16 or wider, within the bound.
No kernel may reach another device: no remote copies, remote signals or barrier semaphores. Data moves between devices by JAX's collectives and lax.ppermute only.
A program may use at most 64 MiB of HBM per device.

v0:
```python
import math

import jax
import jax.numpy as jnp
from jax import lax
from jax.sharding import PartitionSpec as P

HEADS = 32
KV_HEADS = 4
HEAD = 128


NEG_FILL = -1e30


def dequantize(codes, scales):
    height, columns = codes.shape
    blocks = scales.shape[-1]
    wide = codes.astype(jnp.float32).reshape(height, blocks, columns // blocks) * scales[:, :, None]
    return wide.reshape(height, columns).astype(jnp.bfloat16)


def per_device(
    hidden,
    query_weight,
    key_value_weight,
    query_codes,
    query_scales,
    key_value_codes,
    key_value_scales,
    key_cache,
    value_cache,
    lengths,
    counts,
    learner,
    token_ids,
):
    games, steps, features = hidden.shape
    token_rows = hidden.reshape(games * steps, features)
    n_group = lax.axis_size("group")
    n_tp = lax.axis_size("tp")
    tp_index = lax.axis_index("tp")
    members = HEADS // KV_HEADS
    query_local = dequantize(query_codes, query_scales)
    query_term = jnp.dot(
        token_rows,
        lax.all_gather(query_local, "group", axis=1, tiled=True),
        preferred_element_type=jnp.float32,
    )
    pair_local = dequantize(key_value_codes[0], key_value_scales[0])
    pair_term = jnp.dot(
        token_rows,
        lax.all_gather(pair_local, "group", axis=0, tiled=True),
        preferred_element_type=jnp.float32,
    )
    query_part = jnp.dot(token_rows, query_weight, preferred_element_type=jnp.float32) + query_term
    pair_part = (
        jnp.dot(token_rows, key_value_weight, preferred_element_type=jnp.float32) + pair_term
    )
    query_sum, pair_sum = lax.psum((query_part, pair_part), "tp")
    query_round = query_sum.astype(jnp.bfloat16)
    pair_round = pair_sum.astype(jnp.bfloat16)
    queries = query_round.reshape(games, steps, KV_HEADS, members, HEAD)
    pair_heads = pair_round.reshape(games, steps, 2, KV_HEADS, HEAD)
    new_keys = pair_heads[:, :, 0]
    new_values = pair_heads[:, :, 1]
    rounds_count = key_cache.shape[0]
    block_size = key_cache.shape[3]
    key_rows = key_cache.reshape(rounds_count, games, block_size, KV_HEADS, HEAD)
    value_rows = value_cache.reshape(rounds_count, games, block_size, KV_HEADS, HEAD)
    factor = 1.0 / math.sqrt(HEAD)

    def cache_scores(key_block):
        scores = (
            jnp.einsum(
                "gscrd,ugbcd->gscrub", queries, key_block, preferred_element_type=jnp.float32
            )
            * factor
        )
        round_ids = lax.iota(jnp.int32, key_block.shape[0])
        position = (round_ids[:, None] * n_tp + tp_index) * block_size + lax.iota(
            jnp.int32, block_size
        )[None, :]
        valid = position[None, :, :] < lengths[:, None, None]
        return (scores, valid[:, None, None, None, :, :])

    new_scores = (
        jnp.einsum("gscrd,gtcd->gscrt", queries, new_keys, preferred_element_type=jnp.float32)
        * factor
    )
    causal = lax.iota(jnp.int32, steps)[None, :] <= lax.iota(jnp.int32, steps)[:, None]
    new_valid = causal[None, :, None, None, :] & (tp_index == 0)
    new_top = jnp.max(jnp.where(new_valid, new_scores, NEG_FILL), axis=4)
    scores, valid = cache_scores(key_rows)
    local_top = jnp.maximum(new_top, jnp.max(jnp.where(valid, scores, NEG_FILL), axis=(4, 5)))
    row_top = lax.pmax(local_top, "tp")
    new_weight = jnp.where(new_valid, jnp.exp(new_scores - row_top[..., None]), 0.0).astype(
        jnp.bfloat16
    )
    new_total = jnp.sum(new_weight.astype(jnp.float32), axis=4)
    new_mixed = jnp.einsum(
        "gscrt,gtcd->gscrd", new_weight, new_values, preferred_element_type=jnp.float32
    )
    scores, valid = cache_scores(key_rows)
    weight = jnp.where(valid, jnp.exp(scores - row_top[..., None, None]), 0.0).astype(jnp.bfloat16)
    block_total = jnp.sum(weight.astype(jnp.float32), axis=(4, 5))
    block_mixed = jnp.einsum(
        "gscrub,ugbcd->gscrd", weight, value_rows, preferred_element_type=jnp.float32
    )
    block_total, block_mixed = (block_total, block_mixed)
    total = new_total + block_total
    mixed = new_mixed + block_mixed
    mixed_heads = mixed.reshape(games, steps, HEADS, HEAD)
    total_heads = total.reshape(games, steps, HEADS)
    mixed_whole, total_whole = lax.psum((mixed_heads, total_heads), "tp")
    share = HEADS // n_tp
    mixed_mine = lax.dynamic_slice_in_dim(mixed_whole, tp_index * share, share, 2)
    total_mine = lax.dynamic_slice_in_dim(total_whole, tp_index * share, share, 2)
    attended = (mixed_mine / total_mine[..., None]).astype(jnp.bfloat16).reshape(games * steps, -1)
    capacity = max(2, 2 * games * steps // n_group)
    is_live = (lax.iota(jnp.int32, steps)[None, :] < counts[:, None]).reshape(games * steps)
    target = learner.reshape(games * steps)
    match = ((target[:, None] == lax.iota(jnp.int32, n_group)[None, :]) & is_live[:, None]).astype(
        jnp.int32
    )
    earlier = jnp.cumsum(match, axis=0) - match
    order_rank = jnp.sum(earlier * match, axis=1)
    slot_index = target * capacity + order_rank
    placed = (lax.iota(jnp.int32, n_group * capacity)[:, None] == slot_index[None, :]) & is_live[
        None, :
    ]
    packed = jnp.dot(
        placed.astype(jnp.bfloat16), attended, preferred_element_type=jnp.float32
    ).astype(jnp.bfloat16)
    packed = packed.reshape(n_group, capacity, attended.shape[1])
    flat_ids = token_ids.reshape(games * steps)
    packed_ids = jnp.where(
        jnp.any(placed, axis=1), jnp.sum(jnp.where(placed, flat_ids[None, :], 0), axis=1), -1
    )
    packed_ids = packed_ids.reshape(n_group, capacity)
    rows_back, ids_back = (
        lax.all_to_all(packed, "group", split_axis=0, concat_axis=1, tiled=True),
        lax.all_to_all(packed_ids, "group", split_axis=0, concat_axis=1, tiled=True),
    )
    return (rows_back, ids_back)


def solution(mesh):
    placed = (
        P("group", None, "tp"),
        P("tp", None),
        P("tp", None),
        P("tp", "group"),
        P("tp", "group"),
        P("tp", "group", None),
        P("tp", "group", None),
        P(None, "tp", "group", None, None),
        P(None, "tp", "group", None, None),
        P("group"),
        P("group"),
        P("group", None, None),
        P("group", None),
    )
    return jax.shard_map(
        per_device,
        mesh=mesh,
        in_specs=placed,
        out_specs=(P("group", None, "tp"), P("group", None)),
        check_vma=False,
    )
```

profile of v0, /device:TPU:1, one launch (start us, length us, event | category | flops | bytes accessed | tf_op | source)
XLA Modules:
  0.0 470.9 jit_solution(16273196277991290665)
XLA Ops:
  7.2 0.8 reduce.1
  8.1 1.6 multiply_convert_fusion
  10.3 1.3 reduce.7
  12.6 0.8 broadcast_in_dim.82
  14.5 17.2 %all-to-all-start.1 = ((s32[32,1,2]{2,1,0:T(1,128)}), s32[32,1,2]{2,1,0:T(1,128)S(1)}, u32[]{:S(2)}, u32[]{:S(2)}) async-start(s32[32,1,2]{2,1,0:T(1,128)} %bitcast.24), calls=%async_computation.1 | async-start | bytes 32768 | tf_op jit(solution)/shard_map/all_to_all | solution.py:143
  31.8 0.8 copy.53
  32.6 0.8 fusion.10
  33.4 65.5 %all-gather = bf16[32,10,1024]{2,1,0:T(8,128)(2,1)} all-gather(bf16[1,10,1024]{2,1,0:T(8,128)(2,1)S(1)} %fusion.10), channel_id=1, replica_groups=mesh['group'=32,'tp'=16] {'group'}, dimensions={0}, use_global_device_ids=true | all-gather | bytes 675840 | tf_op jit(solution)/shard_map/all_gather | solution.py:53
  98.9 1.4 reshape.177
  100.3 1.3 fusion.16
  101.8 0.9 reshape.170
  102.7 1.6 reshape.171
  105.0 14.5 %all-gather.3.cloned.1.call-done = bf16[320,4096]{1,0:T(8,128)(2,1)} async-done(((bf16[320,128]{1,0:T(8,128)(2,1)}), bf16[320,4096]{1,0:T(8,128)(2,1)}) %all-gather.3.cloned.1.call-update) | async-done | bytes 2621456 | tf_op jit(solution)/shard_map/all_gather | solution.py:47
  119.5 2.2 fusion
  121.7 65.0 %all-reduce.5 = (bf16[16,4096]{1,0:T(8,128)(2,1)S(1)}, bf16[16,1024]{1,0:T(8,128)(2,1)S(1)}) all-reduce(f32[16,4096]{1,0:T(8,128)S(1)} %fusion, f32[16,1024]{1,0:T(8,128)S(1)} %fusion.4), channel_id=1, replica_groups=mesh['group'=32,'tp'=16] {'tp'}, use_global_device_ids=true, to_apply=%region_3.4 | all-reduce | flops 81920 | bytes 491520 | tf_op jit(solution)/shard_map/psum | solution.py:60
  187.4 1.5 select_reduce_fusion
  188.9 60.6 %pmax.7 = f32[2,8,4,8]{3,1,2,0:T(8,128)S(1)} all-reduce(f32[2,8,4,8]{3,1,2,0:T(8,128)S(1)} %max.5), channel_id=1, replica_groups=mesh['group'=32,'tp'=16] {'tp'}, use_global_device_ids=true, to_apply=%region_6.7 | all-reduce | flops 512 | bytes 4096 | tf_op jit(solution)/shard_map/pmax | solution.py:96
  249.5 1.7 convolution_bitcast_fusion.1
  252.2 1.6 convert_reduce_fusion
  254.1 31.7 %psum.31 = f32[2,8,32]{2,1,0:T(8,128)S(1)} all-reduce(f32[2,8,32]{2,1,0:T(8,128)S(1)} %add.83), channel_id=1, replica_groups=mesh['group'=32,'tp'=16] {'tp'}, use_global_device_ids=true, to_apply=%region_10.11 | all-reduce | flops 512 | bytes 4096 | tf_op jit(solution)/shard_map/psum | solution.py:115
  285.8 141.6 %all-reduce.4.cloned.1.call-done = f32[2,8,32,128]{3,2,1,0:T(8,128)} async-done(((f32[2,8,32,128]{3,2,1,0:T(8,128)}), f32[2,8,32,128]{3,2,1,0:T(8,128)}) %all-reduce.4.cloned.1.call-update) | async-done | bytes 262160 | tf_op jit(solution)/shard_map/psum | solution.py:115
  427.4 0.9 fusion.25
  429.2 22.2 %all-to-all-start = ((bf16[32,2,256]{2,1,0:T(2,128)(2,1)}), bf16[32,2,256]{2,1,0:T(2,128)(2,1)S(1)}, u32[]{:S(2)}, u32[]{:S(2)}) async-start(bf16[32,2,256]{2,1,0:T(2,128)(2,1)} %reshape.174), calls=%async_computation | async-start | bytes 65536 | tf_op jit(solution)/shard_map/all_to_all | solution.py:142
  452.7 10.7 %all-to-all-done = bf16[32,2,256]{2,1,0:T(2,128)(2,1)S(1)} async-done(((bf16[32,2,256]{2,1,0:T(2,128)(2,1)}), bf16[32,2,256]{2,1,0:T(2,128)(2,1)S(1)}, u32[]{:S(2)}, u32[]{:S(2)}) %all-to-all-start) | async-done | bytes 32800 | tf_op jit(solution)/shard_map/all_to_all | solution.py:142
  (46 shorter events, 8.6 us)
Async XLA Ops:
  7.2 97.3 %copy-start = (bf16[320,4096]{1,0:T(8,128)(2,1)S(1)}, bf16[320,4096]{1,0:T(8,128)(2,1)}, u32[]{:S(2)}) copy-start(bf16[320,4096]{1,0:T(8,128)(2,1)} %param.14) | copy-start | bytes 7864324
  7.2 93.1 %copy-start.1 = (bf16[2,8,320]{2,1,0:T(8,128)(2,1)S(1)}, bf16[2,8,320]{2,1,0:T(8,128)(2,1)}, u32[]{:S(2)}) copy-start(bf16[2,8,320]{2,1,0:T(8,128)(2,1)} %param.13) | copy-start | bytes 30724
  7.2 112.3 %all-gather.3.cloned.1.call-start = ((), (), s32[]{:S(2)}) async-start(), calls=%async_computation.2 | async-start | bytes 2703360 | tf_op jit(solution)/shard_map/all_gather | solution.py:47
  14.5 414.8 %all-to-all-start.1 = ((s32[32,1,2]{2,1,0:T(1,128)}), s32[32,1,2]{2,1,0:T(1,128)S(1)}, u32[]{:S(2)}, u32[]{:S(2)}) async-start(s32[32,1,2]{2,1,0:T(1,128)} %bitcast.24), calls=%async_computation.1 | async-start | bytes 32768 | tf_op jit(solution)/shard_map/all_to_all | solution.py:143
  31.7 395.7 %all-reduce.4.cloned.1.call-start = ((), (), s32[]{:S(2)}) async-start(), calls=%async_computation.3 | async-start | bytes 524288 | tf_op jit(solution)/shard_map/psum | solution.py:115
  32.6 71.8 %copy-start.2 = (s32[2]{0:T(128)S(1)}, s32[2]{0:T(128)}, u32[]{:S(2)}) copy-start(s32[2]{0:T(128)} %param.22) | copy-start | bytes 28
  429.2 34.2 %all-to-all-start = ((bf16[32,2,256]{2,1,0:T(2,128)(2,1)}), bf16[32,2,256]{2,1,0:T(2,128)(2,1)S(1)}, u32[]{:S(2)}, u32[]{:S(2)}) async-start(bf16[32,2,256]{2,1,0:T(2,128)(2,1)} %reshape.174), calls=%async_computation | async-start | bytes 65536 | tf_op jit(solution)/shard_map/all_to_all | solution.py:142
Sparse Core Ops, SparseCore 0:
  11.2 108.2 all-gather.2
  252.4 174.9 all-reduce.3
where the time goes:
time: 472 us; the launch traced here: 471 us
  blocking collectives  223 us (47%)
  waiting for transfers between devices  167 us (35%)
  starting transfers between devices  39.5 us (8%)
  between operations  14.2 us (3%)
  local copies, waits for them, and re-layouts  9.73 us (2%)
  other arithmetic  9.33 us (2%)
  matrix products  8.69 us (2%)
    psum x1, waiting for transfers between devices, per_device(): mixed_whole, total_whole = lax.psum((mixed_heads, total_heads), 'tp')  142 us
    all_gather x1, blocking collectives, per_device(): lax.all_gather(pair_local, 'group', axis=0, tiled=True)  65.5 us
    psum x1, blocking collectives, per_device(): query_sum, pair_sum = lax.psum((query_part, pair_part), 'tp')  65 us
    pmax x1, blocking collectives, per_device(): row_top = lax.pmax(local_top, 'tp')  60.6 us
    psum x1, blocking collectives, per_device(): mixed_whole, total_whole = lax.psum((mixed_heads, total_heads), 'tp')  31.7 us
    all_to_all x1, starting transfers between devices, per_device(): lax.all_to_all(packed, 'group', split_axis=0, concat_axis=1, tiled=True)  22.2 us
    all_to_all x1, starting transfers between devices, per_device(): lax.all_to_all(packed_ids, 'group', split_axis=0, concat_axis=1, tiled=True)  17.2 us
    all_gather x1, waiting for transfers between devices, per_device(): lax.all_gather(query_local, 'group', axis=1, tiled=True)  14.5 us
  transfers between devices with their start and end apart: 4, of which 3 were waited for; matrix products, arithmetic and copies ran while one was open for 5% of the time, Pallas kernels for 0%

commit v1 on v0

v1 whole, which is shorter than its diff:
```python
import math

import jax
import jax.numpy as jnp
from jax import lax
from jax.sharding import PartitionSpec as P

HEADS = 32
KV_HEADS = 4
HEAD = 128
CORES = 2


NEG_FILL = -1e30


def dequantize(codes, scales):
    height, columns = codes.shape
    blocks = scales.shape[-1]
    wide = codes.astype(jnp.float32).reshape(height, blocks, columns // blocks) * scales[:, :, None]
    return wide.reshape(height, columns).astype(jnp.bfloat16)


def per_device(
    hidden,
    query_weight,
    key_value_weight,
    query_codes,
    query_scales,
    key_value_codes,
    key_value_scales,
    key_cache,
    value_cache,
    lengths,
    counts,
    learner,
    token_ids,
):
    games, steps, features = hidden.shape
    rows = games * steps
    n_group = lax.axis_size("group")
    n_tp = lax.axis_size("tp")
    chips = n_group // CORES
    group_index = lax.axis_index("group")
    chip = group_index // CORES
    core = group_index % CORES
    sharing = n_tp // KV_HEADS
    same_core = [[CORES * u + k for u in range(chips)] for k in range(CORES)]
    swap = [(g, g ^ 1) for g in range(n_group)]
    turn = [
        ((CORES * u + k) * n_tp + t, (CORES * t + k) * n_tp + u)
        for u in range(chips)
        for k in range(CORES)
        for t in range(n_tp)
    ]
    wide = HEADS // n_tp * HEAD
    pair_rows = key_value_codes.shape[1]

    query_mine = dequantize(query_codes, query_scales)
    query_other = lax.ppermute(query_mine, "group", swap)

    rounds, _, _, block, _ = key_cache.shape
    both = jnp.stack([key_cache, value_cache]).reshape(2, rounds, games, block, KV_HEADS, HEAD)
    both = jnp.transpose(both, (4, 0, 1, 2, 3, 5))
    both = jnp.broadcast_to(both[:, None], (KV_HEADS, sharing) + both.shape[1:])
    both = both.reshape((n_tp,) + both.shape[2:])
    cache = lax.all_to_all(both, "tp", split_axis=0, concat_axis=0, tiled=True)

    pair_mine = dequantize(key_value_codes[0], key_value_scales[0])
    pair_heads = pair_mine.reshape(pair_rows, 2, KV_HEADS, HEAD).transpose(2, 0, 1, 3)
    pair_heads = pair_heads.reshape(KV_HEADS, pair_rows, 2 * HEAD)
    is_live = (lax.iota(jnp.int32, steps)[None, :] < counts[:, None]).reshape(rows)
    target = jnp.where(is_live, learner.reshape(rows), -1)
    flat_ids = token_ids.reshape(rows)
    facts = jnp.stack([flat_ids // 4096, flat_ids // 64 % 64, flat_ids % 64, target])
    facts = facts.astype(jnp.bfloat16)
    x_part = jnp.pad(hidden.reshape(rows, features), ((0, 0), (0, 64)))
    facts_part = jnp.pad(facts, ((0, pair_rows - 4), (0, 128 - rows)))
    pair_part = jnp.concatenate(
        [pair_heads, jnp.broadcast_to(facts_part, (KV_HEADS,) + facts_part.shape)], axis=2
    )
    pair_part = jnp.pad(pair_part, ((0, 0), (0, 16 - pair_rows), (0, 0)))
    load = jnp.concatenate([jnp.broadcast_to(x_part, (KV_HEADS,) + x_part.shape), pair_part], axis=1)
    load = jnp.broadcast_to(load[:, None], (KV_HEADS, chips // KV_HEADS) + load.shape[1:])
    load = load.reshape((chips,) + load.shape[2:])
    came = lax.all_to_all(
        load, "group", split_axis=0, concat_axis=0, tiled=True, axis_index_groups=same_core
    )
    x_all = came[:, :rows, :features].reshape(chips * rows, features)
    delta_mine = came[:, rows:]
    delta_other = lax.ppermute(delta_mine, "group", swap)
    delta = jnp.stack([delta_mine, delta_other])

    query_delta = jnp.where(
        core == 0,
        jnp.concatenate([query_mine, query_other], axis=1),
        jnp.concatenate([query_other, query_mine], axis=1),
    )
    head = chip // (chips // KV_HEADS)
    query_base = lax.dynamic_slice_in_dim(query_weight, chip * wide, wide, 1)
    pair_base = jnp.concatenate(
        [
            lax.dynamic_slice_in_dim(key_value_weight, head * HEAD, HEAD, 1),
            lax.dynamic_slice_in_dim(key_value_weight, (KV_HEADS + head) * HEAD, HEAD, 1),
        ],
        axis=1,
    )
    spot = lax.iota(jnp.int32, CORES * chips * 16)
    owner = spot // 16 % chips * CORES + (spot // 16 // chips + core) % 2
    source = jnp.where(spot % 16 < pair_rows, owner * pair_rows + spot % 16, -1)
    spread = (lax.iota(jnp.int32, features)[:, None] == source[None, :]).astype(jnp.bfloat16)
    x_spread = jnp.dot(x_all, spread, preferred_element_type=jnp.float32).astype(jnp.bfloat16)
    pair_delta = delta[..., : 2 * HEAD].reshape(CORES * chips * 16, 2 * HEAD)
    query_part = jnp.dot(x_all, query_base, preferred_element_type=jnp.float32) + jnp.dot(
        x_all, query_delta, preferred_element_type=jnp.float32
    )
    pair_part = jnp.dot(x_all, pair_base, preferred_element_type=jnp.float32) + jnp.dot(
        x_spread, pair_delta, preferred_element_type=jnp.float32
    )
    part = jnp.concatenate([query_part, pair_part], axis=1).reshape(chips, rows, wide + 2 * HEAD)
    parts = lax.all_to_all(part, "tp", split_axis=0, concat_axis=0, tiled=True)
    mine = jnp.sum(parts, axis=0).astype(jnp.bfloat16)
    mine = lax.ppermute(mine, ("group", "tp"), turn)

    all_facts = delta[:, :, :4, 2 * HEAD : 2 * HEAD + rows].astype(jnp.int32)
    all_facts = jnp.where(core == 0, all_facts, all_facts[::-1])
    all_facts = all_facts.transpose(2, 1, 0, 3).reshape(4, n_group, rows)
    all_ids = all_facts[0] * 4096 + all_facts[1] * 64 + all_facts[2]
    hits = all_facts[3] == group_index
    hit_rank = jnp.cumsum(hits.astype(jnp.int32), axis=1) - 1
    capacity = max(2, 2 * rows // n_group)
    chosen = hits[:, None, :] & (hit_rank[:, None, :] == lax.iota(jnp.int32, capacity)[None, :, None])
    ids_back = jnp.where(
        jnp.any(chosen, axis=2), jnp.sum(jnp.where(chosen, all_ids[:, None, :], 0), axis=2), -1
    ).reshape(1, n_group * capacity)

    per = HEADS // n_tp
    queries = mine[:, :wide].reshape(games, steps, per, HEAD)
    new_keys = mine[:, wide : wide + HEAD].reshape(games, steps, HEAD)
    new_values = mine[:, wide + HEAD :].reshape(games, steps, HEAD)
    key_rows = cache[:, 0]
    value_rows = cache[:, 1]
    factor = 1.0 / math.sqrt(HEAD)
    scores = (
        jnp.einsum("gshd,trgbd->gshtrb", queries, key_rows, preferred_element_type=jnp.float32)
        * factor
    )
    position = (
        (lax.iota(jnp.int32, rounds)[None, :, None] * n_tp + lax.iota(jnp.int32, n_tp)[:, None, None])
        * block
        + lax.iota(jnp.int32, block)[None, None, :]
    )
    valid = (position[None] < lengths[:, None, None, None])[:, None, None]
    new_scores = (
        jnp.einsum("gshd,gjd->gshj", queries, new_keys, preferred_element_type=jnp.float32) * factor
    )
    causal = lax.iota(jnp.int32, steps)[None, :] <= lax.iota(jnp.int32, steps)[:, None]
    new_valid = causal[None, :, None, :]
    top = jnp.maximum(
        jnp.max(jnp.where(valid, scores, NEG_FILL), axis=(3, 4, 5)),
        jnp.max(jnp.where(new_valid, new_scores, NEG_FILL), axis=3),
    )
    weight = jnp.where(valid, jnp.exp(scores - top[..., None, None, None]), 0.0).astype(jnp.bfloat16)
    new_weight = jnp.where(new_valid, jnp.exp(new_scores - top[..., None]), 0.0).astype(jnp.bfloat16)
    total = jnp.sum(weight.astype(jnp.float32), axis=(3, 4, 5)) + jnp.sum(
        new_weight.astype(jnp.float32), axis=3
    )
    mixed = jnp.einsum(
        "gshtrb,trgbd->gshd", weight, value_rows, preferred_element_type=jnp.float32
    ) + jnp.einsum("gshj,gjd->gshd", new_weight, new_values, preferred_element_type=jnp.float32)
    attended = (mixed / total[..., None]).astype(jnp.bfloat16).reshape(rows, wide)

    match = (target[:, None] == lax.iota(jnp.int32, n_group)[None, :]).astype(jnp.int32)
    earlier = jnp.cumsum(match, axis=0) - match
    order_rank = jnp.sum(earlier * match, axis=1)
    slot_index = jnp.where(is_live, target * capacity + order_rank, -1)
    placed = lax.iota(jnp.int32, n_group * capacity)[:, None] == slot_index[None, :]
    packed = jnp.dot(
        placed.astype(jnp.bfloat16), attended, preferred_element_type=jnp.float32
    ).astype(jnp.bfloat16)
    packed = packed.reshape(n_group, capacity, wide)
    rows_back = lax.all_to_all(packed, "group", split_axis=0, concat_axis=1, tiled=True)
    return (rows_back, ids_back)


def solution(mesh):
    placed = (
        P("group", None, "tp"),
        P("tp", None),
        P("tp", None),
        P("tp", "group"),
        P("tp", "group"),
        P("tp", "group", None),
        P("tp", "group", None),
        P(None, "tp", "group", None, None),
        P(None, "tp", "group", None, None),
        P("group"),
        P("group"),
        P("group", None, None),
        P("group", None),
    )
    return jax.shard_map(
        per_device,
        mesh=mesh,
        in_specs=placed,
        out_specs=(P("group", None, "tp"), P("group", None)),
        check_vma=False,
    )
```

time: 472 us -> 134 us (0.28)
  blocking collectives: 223 us -> 0 us
  waiting for transfers between devices: 167 us -> 43.1 us
  starting transfers between devices: 39.5 us -> 53.1 us
  between operations: 14.2 us -> 1.05 us
  local copies, waits for them, and re-layouts: 9.73 us -> 17.7 us
    psum x1 -> x0, waiting for transfers between devices: 142 us -> none  [per_device(): mixed_whole, total_whole = lax.psum((mixed_heads, total_heads), 'tp')]
    psum x2 -> x0, blocking collectives: 96.6 us -> none  [the longest x1 65 us: per_device(): query_sum, pair_sum = lax.psum((query_part, pair_part), 'tp')]
    all_gather x1 -> x0, blocking collectives: 65.5 us -> none  [per_device(): lax.all_gather(pair_local, 'group', axis=0, tiled=True)]
    pmax x1 -> x0, blocking collectives: 60.6 us -> none  [per_device(): row_top = lax.pmax(local_top, 'tp')]
    all_to_all x1 -> x3, waiting for transfers between devices: 0.01 us -> 31.8 us  [the longest x1 18.6 us: per_device(): cache = lax.all_to_all(both, 'tp', split_axis=0, concat_axis=0, tiled=True)]
    all_gather x1 -> x0, waiting for transfers between devices: 14.5 us -> none  [per_device(): lax.all_gather(query_local, 'group', axis=1, tiled=True)]
    all_to_all x1 -> x3, starting transfers between devices: 17.2 us -> 29.3 us  [the longest x1 16.2 us: per_device(): lax.all_to_all(load, 'group', split_axis=0, concat_axis=0, tiled=True, ax...]
    ppermute x0 -> x3, starting transfers between devices: none -> 7.99 us  [the longest x1 4.48 us: per_device(): delta_other = lax.ppermute(delta_mine, 'group', swap)]
  transfers between devices with their start and end apart: 4 -> 7, of which waited for: 3 -> 4; matrix products, arithmetic and copies ran while one was open for 5% -> 13% of each run, Pallas kernels for 0% -> 0%
where the time goes in v1:
time: 134 us; the launch traced here: 133 us
  starting transfers between devices  53.1 us (40%)
  waiting for transfers between devices  43.1 us (32%)
  local copies, waits for them, and re-layouts  17.7 us (13%)
  other arithmetic  11.5 us (9%)
  matrix products  6.79 us (5%)
    all_to_all x1, waiting for transfers between devices, per_device(): cache = lax.all_to_all(both, 'tp', split_axis=0, concat_axis=0, tiled=True)  18.6 us
    all_to_all x1, starting transfers between devices, per_device(): lax.all_to_all(load, 'group', split_axis=0, concat_axis=0, tiled=True, ax...  16.2 us
    all_to_all x1, starting transfers between devices, per_device(): lax.all_to_all(packed, 'group', split_axis=0, concat_axis=1, tiled=True)  15.7 us
    all_to_all x1, waiting for transfers between devices, per_device(): lax.all_to_all(packed, 'group', split_axis=0, concat_axis=1, tiled=True)  11.3 us
    all_to_all x1, waiting for transfers between devices, per_device(): parts = lax.all_to_all(part, 'tp', split_axis=0, concat_axis=0, tiled=True)  10.3 us
    all_to_all x1, starting transfers between devices, per_device(): parts = lax.all_to_all(part, 'tp', split_axis=0, concat_axis=0, tiled=True)  8.42 us
    all_to_all x1, starting transfers between devices, per_device(): cache = lax.all_to_all(both, 'tp', split_axis=0, concat_axis=0, tiled=True)  4.68 us
    ppermute x1, starting transfers between devices, per_device(): delta_other = lax.ppermute(delta_mine, 'group', swap)  4.48 us
  transfers between devices with their start and end apart: 7, of which 4 were waited for; matrix products, arithmetic and copies ran while one was open for 13% of the time, Pallas kernels for 0%

profile of v1, /device:TPU:1, one launch (start us, length us, event | category | flops | bytes accessed | tf_op | source)
XLA Modules:
  0.0 133.2 jit_solution(6030994432875710395)
XLA Ops:
  0.7 0.9 iota_compare_fusion.11
  6.6 16.2 %all-to-all-start = ((bf16[16,32,384]{2,1,0:T(8,128)(2,1)}), bf16[16,32,384]{2,1,0:T(8,128)(2,1)S(1)}, u32[]{:S(2)}, u32[]{:S(2)}) async-start(bf16[16,32,384]{2,1,0:T(8,128)(2,1)} %bitcast.3), calls=%async_computation | async-start | bytes 786432 | tf_op jit(solution)/shard_map/all_to_all | solution.py:86
  23.5 1.6 %multiply_convert_fusion = bf16[320,128]{1,0:T(8,128)(2,1)} fusion(bf16[320,128]{1,0:T(8,128)(2,1)} %param.16, f32[320]{0:T(512)S(1)} %reduce.2), kind=kLoop, calls=%fused_computation.35 | loop fusion | flops 122880 | bytes 165120 | tf_op jit(solution)/shard_map/convert_element_type | solution.py:21
  25.2 2.9 %collective-permute-start = (bf16[320,128]{1,0:T(8,128)(2,1)}, bf16[320,128]{1,0:T(8,128)(2,1)}, u32[]{:S(2)}, u32[]{:S(2)}) collective-permute-start(bf16[320,128]{1,0:T(8,128)(2,1)} %multiply_convert_fusion), channel_id=1, source_target_pairs={{0,16},{16,0},{32,48},{48,32},{64,80},{80,64},{96,112},{112,96},{1... | collective-permute-start | bytes 245768 | tf_op jit(solution)/shard_map/ppermute | solution.py:60
  28.2 1.6 %stack.30 = bf16[1,4,2,16,4,128]{5,4,3,2,1,0:T(4,128)(2,1)} reshape(bf16[4,1,2,16,512]{4,3,2,1,0:T(8,128)(2,1)} %param.20) | data formatting | bytes 262144 | tf_op jit(solution)/shard_map/stack | solution.py:63
  31.7 1.6 %constant_dynamic-slice_fusion.1 = (bf16[320,128]{1,0:T(8,128)(2,1)S(1)}, bf16[320,128]{1,0:T(8,128)(2,1)}) fusion(bf16[320,1024]{1,0:T(8,128)(2,1)} %param.15, s32[]{:T(128)S(6)} %select_n.214, s32[]{:T(128)S(6)} %select_n.215), kind=kLoop, calls=%fused_computation.138 | loop fusion | bytes 327688 | tf_op jit(solution)/shard_map/dynamic_slice | solution.py:103
  33.3 2.9 %all-to-all-done = bf16[16,32,384]{2,1,0:T(8,128)(2,1)S(1)} async-done(((bf16[16,32,384]{2,1,0:T(8,128)(2,1)}), bf16[16,32,384]{2,1,0:T(8,128)(2,1)S(1)}, u32[]{:S(2)}, u32[]{:S(2)}) %all-to-all-start) | async-done | bytes 393248 | tf_op jit(solution)/shard_map/all_to_all | solution.py:86
  36.2 4.5 %collective-permute-start.1 = (bf16[16,16,384]{2,0,1:T(8,128)(2,1)S(1)}, bf16[16,16,384]{2,0,1:T(8,128)(2,1)S(1)}, u32[]{:S(2)}, u32[]{:S(2)}) collective-permute-start(bf16[16,16,384]{2,0,1:T(8,128)(2,1)S(1)} %copy.128), channel_id=1, source_target_pairs={{0,16},{16,0},{32,48},{48,32},{64,80},{80,64},{96,112},{112,96},{1... | collective-permute-start | bytes 589832 | tf_op jit(solution)/shard_map/ppermute | solution.py:91
  41.1 2.0 %convolution_add_fusion = f32[256,256]{0,1:T(8,128)} fusion(f32[256,256]{0,1:T(8,128)S(1)} %fusion.18, bf16[256,320]{1,0:T(8,128)(2,1)S(1)} %bitcast.89, bf16[320,128]{1,0:T(8,128)(2,1)} %collective-permute-done, bf16[320,128]{1,0:T(8,128)(2,1)} %multiply_convert_fusion, pred[]{:T(512)S(6)} %eq.89), kind=kOutput, calls=%fused_computation.4 | convolution fusion | flops 42745856 | bytes 851969 | tf_op jit(solution)/shard_map/dot_general | solution.py:114
  44.0 1.3 fusion.1
  45.3 1.1 pad_maximum_fusion
  46.4 1.0 copy.89
  47.4 8.4 %all-to-all-start.1 = ((f32[16,16,512]{2,1,0:T(8,128)}), f32[16,16,512]{2,1,0:T(8,128)S(1)}, u32[]{:S(2)}, u32[]{:S(2)}) async-start(f32[16,16,512]{2,1,0:T(8,128)} %bitcast.85), calls=%async_computation.1 | async-start | bytes 1048576 | tf_op jit(solution)/shard_map/all_to_all | solution.py:121
  55.8 1.2 maximum_bitcast_fusion
  58.7 1.3 add_select_fusion.5
  60.0 10.3 %all-to-all-done.1 = f32[16,16,512]{2,1,0:T(8,128)S(1)} async-done(((f32[16,16,512]{2,1,0:T(8,128)}), f32[16,16,512]{2,1,0:T(8,128)S(1)}, u32[]{:S(2)}, u32[]{:S(2)}) %all-to-all-start.1) | async-done | bytes 524320 | tf_op jit(solution)/shard_map/all_to_all | solution.py:121
  70.3 2.2 %broadcast_in_dim.112 = bf16[4,4,2,4,2,16,128]{6,5,3,4,2,1,0:T(8,128)(2,1)} broadcast(bf16[4,2,4,2,16,128]{5,4,2,3,1,0:T(8,128)(2,1)} %copy.90), dimensions={0,2,3,4,5,6} | broadcast | bytes 1310720 | tf_op jit(solution)/shard_map/broadcast_in_dim | solution.py:65
  72.5 4.7 %all-to-all-start.2 = ((bf16[16,2,4,2,16,128]{5,4,2,3,1,0:T(8,128)(2,1)}), bf16[16,2,4,2,16,128]{5,4,2,3,1,0:T(8,128)(2,1)}, u32[]{:S(2)}, u32[]{:S(2)}) async-start(bf16[16,2,4,2,16,128]{5,4,2,3,1,0:T(8,128)(2,1)} %bitcast.84), calls=%async_computation.2 | async-start | bytes 2097152 | tf_op jit(solution)/shard_map/all_to_all | solution.py:67
  79.9 0.8 select_reduce_fusion.2
  80.7 18.6 %all-to-all-done.2 = bf16[16,2,4,2,16,128]{5,4,2,3,1,0:T(8,128)(2,1)} async-done(((bf16[16,2,4,2,16,128]{5,4,2,3,1,0:T(8,128)(2,1)}), bf16[16,2,4,2,16,128]{5,4,2,3,1,0:T(8,128)(2,1)}, u32[]{:S(2)}, u32[]{:S(2)}) %all-to-all-start.2) | async-done | bytes 1048608 | tf_op jit(solution)/shard_map/all_to_all | solution.py:67
  99.3 1.4 %fusion.75 = (bf16[16,1,4,2,16,128]{5,4,2,3,1,0:T(8,128)(2,1)S(1)}, bf16[16,1,4,2,16,128]{5,4,2,3,1,0:T(8,128)(2,1)S(1)}) fusion(bf16[16,2,4,2,16,128]{5,4,2,3,1,0:T(8,128)(2,1)} %all-to-all-done.2), kind=kLoop, calls=%fused_computation.153 | loop fusion | bytes 2097152 | tf_op jit(solution)/shard_map/slice | solution.py:141
  100.8 1.4 %select_reduce_fusion = (f32[2,8,2]{1,2,0:T(2,128)S(1)}, f32[2,8,2,16,4,16]{5,1,4,3,2,0:T(8,128)S(1)}) fusion(pred[2,16,4,16]{3,2,1,0:T(4,128)(4,1)S(1)} %broadcast_compare_fusion, bf16[16,1,4,2,16,128]{5,4,2,3,1,0:T(8,128)(2,1)S(1)} %get-tuple-element.4, bf16[16,512]{1,0:T(8,128)(2,1)S(1)} %collective-permute-done.2), kind=kOutput, calls=%fused_computation.14 | convolution fusion | flops 8486880 | bytes 680064 | tf_op jit(solution)/shard_map/gshd,trgbd->gshtrb/dot_general | solution.py:145
  104.8 15.7 %all-to-all-start.3 = ((bf16[32,2,256]{2,1,0:T(2,128)(2,1)}), bf16[32,2,256]{2,1,0:T(2,128)(2,1)S(1)}, u32[]{:S(2)}, u32[]{:S(2)}) async-start(bf16[32,2,256]{2,1,0:T(2,128)(2,1)} %reshape.527), calls=%async_computation.3 | async-start | bytes 65536 | tf_op jit(solution)/shard_map/all_to_all | solution.py:182
  121.2 11.3 %all-to-all-done.3 = bf16[32,2,256]{2,1,0:T(2,128)(2,1)S(1)} async-done(((bf16[32,2,256]{2,1,0:T(2,128)(2,1)}), bf16[32,2,256]{2,1,0:T(2,128)(2,1)S(1)}, u32[]{:S(2)}, u32[]{:S(2)}) %all-to-all-start.3) | async-done | bytes 32800 | tf_op jit(solution)/shard_map/all_to_all | solution.py:182
  (93 shorter events, 17.3 us)
Async XLA Ops:
  0.6 40.1 %copy-start = (bf16[320,4096]{1,0:T(8,128)(2,1)S(1)}, bf16[320,4096]{1,0:T(8,128)(2,1)}, u32[]{:S(2)}) copy-start(bf16[320,4096]{1,0:T(8,128)(2,1)} %param.14) | copy-start | bytes 7864324
  0.6 30.3 %copy-start.7 = (s32[2,8,1]{1,2,0:T(1,128)S(1)}, s32[2,8,1]{1,2,0:T(1,128)}, u32[]{:S(2)}) copy-start(s32[2,8,1]{1,2,0:T(1,128)} %param.24) | copy-start | bytes 196
  0.7 29.1 %copy-start.4 = (bf16[4,1,2,16,512]{4,3,2,1,0:T(8,128)(2,1)S(1)}, bf16[4,1,2,16,512]{4,3,2,1,0:T(8,128)(2,1)}, u32[]{:S(2)}) copy-start(bf16[4,1,2,16,512]{4,3,2,1,0:T(8,128)(2,1)} %param.21) | copy-start | bytes 393220
  6.6 29.6 %all-to-all-start = ((bf16[16,32,384]{2,1,0:T(8,128)(2,1)}), bf16[16,32,384]{2,1,0:T(8,128)(2,1)S(1)}, u32[]{:S(2)}, u32[]{:S(2)}) async-start(bf16[16,32,384]{2,1,0:T(8,128)(2,1)} %bitcast.3), calls=%async_computation | async-start | bytes 786432 | tf_op jit(solution)/shard_map/all_to_all | solution.py:86
  25.2 15.9 %collective-permute-start = (bf16[320,128]{1,0:T(8,128)(2,1)}, bf16[320,128]{1,0:T(8,128)(2,1)}, u32[]{:S(2)}, u32[]{:S(2)}) collective-permute-start(bf16[320,128]{1,0:T(8,128)(2,1)} %multiply_convert_fusion), channel_id=1, source_target_pairs={{0,16},{16,0},{32,48},{48,32},{64,80},{80,64},{96,112},{112,96},{1... | collective-permute-start | bytes 245768 | tf_op jit(solution)/shard_map/ppermute | solution.py:60
  28.2 8.0 %copy-start.8 = (pred[16]{0:T(512)(128)(4,1)}, pred[16]{0:T(512)(128)(4,1)S(1)}, u32[]{:S(2)}) copy-start(pred[16]{0:T(512)(128)(4,1)S(1)} %lt.104) | copy-start | bytes 52
  31.7 11.7 %copy-start.10 = (s32[16]{0:T(128)}, s32[16]{0:T(128)S(1)}, u32[]{:S(2)}) copy-start(s32[16]{0:T(128)S(1)} %reshape.513) | copy-start | bytes 196
  33.3 24.5 %copy-start.6 = (s32[16]{0:T(128)}, s32[16]{0:T(128)S(1)}, u32[]{:S(2)}) copy-start(s32[16]{0:T(128)S(1)} %broadcast_select_fusion.1) | copy-start | bytes 196
  36.2 6.9 %copy-start.3 = (bf16[320,128]{1,0:T(8,128)(2,1)S(1)}, bf16[320,128]{1,0:T(8,128)(2,1)}, u32[]{:S(2)}) copy-start(bf16[320,128]{1,0:T(8,128)(2,1)} %get-tuple-element.7) | copy-start | bytes 245764
  36.2 7.1 %collective-permute-start.1 = (bf16[16,16,384]{2,0,1:T(8,128)(2,1)S(1)}, bf16[16,16,384]{2,0,1:T(8,128)(2,1)S(1)}, u32[]{:S(2)}, u32[]{:S(2)}) collective-permute-start(bf16[16,16,384]{2,0,1:T(8,128)(2,1)S(1)} %copy.128), channel_id=1, source_target_pairs={{0,16},{16,0},{32,48},{48,32},{64,80},{80,64},{96,112},{112,96},{1... | collective-permute-start | bytes 589832 | tf_op jit(solution)/shard_map/ppermute | solution.py:91
  43.3 0.7 copy-start.1
  47.4 31.2 %copy-start.2 = (bf16[16,16,384]{2,0,1:T(8,128)(2,1)S(1)}, bf16[16,16,384]{2,0,1:T(8,128)(2,1)}, u32[]{:S(2)}) copy-start(bf16[16,16,384]{2,0,1:T(8,128)(2,1)} %copy-done.1) | copy-start | bytes 589828
  47.4 22.9 %all-to-all-start.1 = ((f32[16,16,512]{2,1,0:T(8,128)}), f32[16,16,512]{2,1,0:T(8,128)S(1)}, u32[]{:S(2)}, u32[]{:S(2)}) async-start(f32[16,16,512]{2,1,0:T(8,128)} %bitcast.85), calls=%async_computation.1 | async-start | bytes 1048576 | tf_op jit(solution)/shard_map/all_to_all | solution.py:121
  72.5 26.9 %all-to-all-start.2 = ((bf16[16,2,4,2,16,128]{5,4,2,3,1,0:T(8,128)(2,1)}), bf16[16,2,4,2,16,128]{5,4,2,3,1,0:T(8,128)(2,1)}, u32[]{:S(2)}, u32[]{:S(2)}) async-start(bf16[16,2,4,2,16,128]{5,4,2,3,1,0:T(8,128)(2,1)} %bitcast.84), calls=%async_computation.2 | async-start | bytes 2097152 | tf_op jit(solution)/shard_map/all_to_all | solution.py:67
  79.2 0.7 collective-permute-start.2
  100.8 3.0 %copy-start.5 = (pred[8,8]{0,1:T(8,128)(4,1)S(1)}, pred[8,8]{0,1:T(8,128)(4,1)}, u32[]{:S(2)}) copy-start(pred[8,8]{0,1:T(8,128)(4,1)} %iota_compare_fusion.10) | copy-start | bytes 196
  100.8 3.0 %copy-start.9 = (s32[16]{0:T(128)S(1)}, s32[16]{0:T(128)}, u32[]{:S(2)}) copy-start(s32[16]{0:T(128)} %add_select_fusion.5) | copy-start | bytes 196
  104.8 27.8 %all-to-all-start.3 = ((bf16[32,2,256]{2,1,0:T(2,128)(2,1)}), bf16[32,2,256]{2,1,0:T(2,128)(2,1)S(1)}, u32[]{:S(2)}, u32[]{:S(2)}) async-start(bf16[32,2,256]{2,1,0:T(2,128)(2,1)} %reshape.527), calls=%async_computation.3 | async-start | bytes 65536 | tf_op jit(solution)/shard_map/all_to_all | solution.py:182

commit v2 on v1

v2 whole, which is shorter than its diff:
```python
import functools
import math

import jax
import jax.numpy as jnp
from jax import lax
from jax.experimental import pallas as pl
from jax.experimental.pallas import tpu as pltpu
from jax.sharding import PartitionSpec as P

HEADS = 32
KV_HEADS = 4
HEAD = 128
CORES = 2
TILE = 16
LANES = 128


NEG_FILL = -1e30

VMEM = pl.BlockSpec(memory_space=pltpu.VMEM)
SMEM = pl.BlockSpec(memory_space=pltpu.SMEM)
PARAMS = pltpu.CompilerParams(vmem_limit_bytes=32 * 1024 * 1024)


def column(row):
    n = row.shape[1]
    across = lax.broadcasted_iota(jnp.int32, (n, n), 1)
    down = lax.broadcasted_iota(jnp.int32, (n, n), 0)
    return jnp.sum(jnp.where(across == down, row, jnp.zeros_like(row)), axis=1, keepdims=True)


def load_kernel(counts_ref, hidden_ref, codes_ref, scales_ref, learner_ref, ids_ref, load_ref):
    chips = load_ref.shape[0]
    rows, features = hidden_ref.shape
    pair_rows = codes_ref.shape[0]
    games, steps = ids_ref.shape
    load_ref[...] = jnp.zeros_like(load_ref)
    load_ref[:, :rows, :features] = jnp.broadcast_to(hidden_ref[...], (chips, rows, features))
    per_head = chips // KV_HEADS
    for block in range(2 * KV_HEADS):
        scale = column(scales_ref[block : block + 1, :])
        codes = codes_ref[:, block * HEAD : (block + 1) * HEAD].astype(jnp.float32)
        delta = (codes * scale).astype(jnp.bfloat16)
        head, part = block % KV_HEADS, block // KV_HEADS
        load_ref[
            head * per_head : (head + 1) * per_head,
            rows : rows + pair_rows,
            part * HEAD : (part + 1) * HEAD,
        ] = jnp.broadcast_to(delta, (per_head, pair_rows, HEAD))
    step = lax.broadcasted_iota(jnp.int32, (1, steps), 1)
    ids = ids_ref[...]
    named = [
        jnp.where(step < counts_ref[game], learner_ref[game], -1) for game in range(games)
    ]
    facts = jnp.concatenate([ids >> 12, (ids >> 6) & 63, ids & 63] + named, axis=0)
    facts = facts.astype(jnp.float32).astype(jnp.bfloat16)
    load_ref[:, rows : rows + 4 * games, 2 * HEAD : 2 * HEAD + steps] = jnp.broadcast_to(
        facts, (chips,) + facts.shape
    )


def pieces_kernel(place_ref, codes_ref, scales_ref, key_ref, value_ref, delta_ref, *piece_refs):
    scale = column(scales_ref[...])
    delta_ref[...] = (codes_ref[...].astype(jnp.float32) * scale).astype(jnp.bfloat16)
    for shift, piece_ref in enumerate(piece_refs):
        head = lax.rem(place_ref[0] + shift, KV_HEADS)
        lanes = pl.ds(pl.multiple_of(head * HEAD, HEAD), HEAD)
        piece_ref[0] = key_ref[:, 0, :, :, lanes]
        piece_ref[1] = value_ref[:, 0, :, :, lanes]


def part_kernel(
    place_ref,
    came_ref,
    other_ref,
    delta_mine_ref,
    delta_other_ref,
    query_ref,
    key_ref,
    value_ref,
    piece0_ref,
    piece1_ref,
    piece2_ref,
    piece3_ref,
    part_ref,
    shard_ref,
):
    chips, rows = part_ref.shape[:2]
    features = query_ref.shape[0]
    wide = query_ref.shape[1]
    core = place_ref[2]
    pair_rows = features // (chips * CORES)

    def dot(a, b):
        return jnp.dot(a, b, preferred_element_type=jnp.float32)

    inputs = came_ref[:, :rows, :features].reshape(chips * rows, features)
    mine, other = delta_mine_ref[...], delta_other_ref[...]
    first = jnp.where(core == 0, mine, other)
    second = jnp.where(core == 0, other, mine)
    queries = dot(inputs, query_ref[...])
    part_ref[:, :, :HEAD] = (queries[:, :HEAD] + dot(inputs, first)).reshape(chips, rows, HEAD)
    part_ref[:, :, HEAD:wide] = (queries[:, HEAD:] + dot(inputs, second)).reshape(chips, rows, HEAD)
    spot = lax.broadcasted_iota(jnp.int32, (1, chips * TILE), 1)
    feature = lax.broadcasted_iota(jnp.int32, (features, chips * TILE), 0)
    pairs = jnp.zeros((chips * rows, 2 * HEAD), jnp.float32)
    for turn, delta_ref in enumerate((came_ref, other_ref)):
        owner = (spot // TILE) * CORES + (core + turn) % CORES
        source = jnp.where(spot % TILE < pair_rows, owner * pair_rows + spot % TILE, -1)
        spread = (feature == source).astype(jnp.float32).astype(jnp.bfloat16)
        spread = dot(inputs, spread).astype(jnp.bfloat16)
        delta = delta_ref[:, rows:, : 2 * HEAD] if turn == 0 else delta_ref[:, :, : 2 * HEAD]
        pairs = pairs + dot(spread, delta.reshape(chips * TILE, 2 * HEAD))
    part_ref[:, :, wide : wide + HEAD] = (pairs[:, :HEAD] + dot(inputs, key_ref[...])).reshape(
        chips, rows, HEAD
    )
    part_ref[:, :, wide + HEAD :] = (pairs[:, HEAD:] + dot(inputs, value_ref[...])).reshape(
        chips, rows, HEAD
    )
    for shift, piece_ref in enumerate((piece0_ref, piece1_ref, piece2_ref, piece3_ref)):
        shard_ref[shift] = piece_ref[...]


def attend_kernel(
    place_ref,
    lengths_ref,
    mine_ref,
    placed_ref,
    shard0_ref,
    shard1_ref,
    shard2_ref,
    shard3_ref,
    packed_ref,
):
    shards = (shard0_ref, shard1_ref, shard2_ref, shard3_ref)
    count, _, rounds, games, block, _ = shard0_ref.shape
    rows = mine_ref.shape[0]
    steps = rows // games
    heads = mine_ref.shape[1] // HEAD - 2
    n_tp = count * len(shards)
    factor = 1.0 / math.sqrt(HEAD)
    mine = mine_ref[...].astype(jnp.float32)
    spot = lax.broadcasted_iota(jnp.int32, (1, count * rounds * block), 1)
    positions = []
    for shift in range(len(shards)):
        across = lax.rem(place_ref[1] - shift + len(shards), len(shards))
        down = (place_ref[0] - spot // (rounds * block) + count) % count
        tp = down * len(shards) + across
        positions.append((spot // block % rounds * n_tp + tp) * block + spot % block)
    contract = (((1,), (1,)), ((), ()))
    games_out = []
    for game in range(games):
        band = mine[game * steps : (game + 1) * steps]
        queries = jnp.concatenate(
            [band[:, h * HEAD : (h + 1) * HEAD] for h in range(heads)], axis=0
        ).astype(jnp.bfloat16)
        new_keys = band[:, heads * HEAD : (heads + 1) * HEAD].astype(jnp.bfloat16)
        new_values = band[:, (heads + 1) * HEAD :].astype(jnp.bfloat16)
        new_scores = factor * lax.dot_general(
            queries, new_keys, contract, preferred_element_type=jnp.float32
        )
        later = lax.broadcasted_iota(jnp.int32, new_scores.shape, 1)
        step = lax.broadcasted_iota(jnp.int32, new_scores.shape, 0) % steps
        new_valid = later <= step
        top = jnp.max(jnp.where(new_valid, new_scores, NEG_FILL), axis=1, keepdims=True)
        kept = []
        for shard_ref, position in zip(shards, positions):
            keys = shard_ref[:, 0, :, game].reshape(count * rounds * block, HEAD)
            scores = factor * lax.dot_general(
                queries, keys, contract, preferred_element_type=jnp.float32
            )
            scores = jnp.where(position < lengths_ref[game], scores, NEG_FILL)
            top = jnp.maximum(top, jnp.max(scores, axis=1, keepdims=True))
            kept.append(scores)
        weight = jnp.where(new_valid, jnp.exp(new_scores - top), 0.0).astype(jnp.bfloat16)
        total = jnp.sum(weight.astype(jnp.float32), axis=1, keepdims=True)
        mixed = jnp.dot(weight, new_values, preferred_element_type=jnp.float32)
        for shard_ref, position, scores in zip(shards, positions, kept):
            values = shard_ref[:, 1, :, game].reshape(count * rounds * block, HEAD)
            weight = jnp.where(
                position < lengths_ref[game], jnp.exp(scores - top), 0.0
            ).astype(jnp.bfloat16)
            total = total + jnp.sum(weight.astype(jnp.float32), axis=1, keepdims=True)
            mixed = mixed + jnp.dot(weight, values, preferred_element_type=jnp.float32)
        out = mixed / total
        games_out.append(
            jnp.concatenate([out[h * steps : (h + 1) * steps] for h in range(heads)], axis=1)
        )
    attended = jnp.concatenate(games_out, axis=0).astype(jnp.bfloat16)
    packed_ref[...] = jnp.dot(
        placed_ref[...], attended, preferred_element_type=jnp.float32
    ).astype(jnp.bfloat16)


def places(counts, learner, n_group, capacity):
    games, steps, _ = learner.shape
    rows = games * steps
    is_live = (lax.iota(jnp.int32, steps)[None, :] < counts[:, None]).reshape(rows)
    target = jnp.where(is_live, learner.reshape(rows), -1)
    match = (target[:, None] == lax.iota(jnp.int32, n_group)[None, :]).astype(jnp.int32)
    earlier = jnp.cumsum(match, axis=0) - match
    order_rank = jnp.sum(earlier * match, axis=1)
    slot_index = jnp.where(is_live, target * capacity + order_rank, -1)
    placed = lax.iota(jnp.int32, n_group * capacity)[:, None] == slot_index[None, :]
    return placed.astype(jnp.bfloat16)


def ids_of(facts, group_index, capacity):
    n_group, kinds, rows = facts.shape[0], 4, facts.shape[1] * facts.shape[2] // 4
    facts = facts.reshape(n_group, kinds, rows).astype(jnp.int32)
    all_ids = facts[:, 0] * 4096 + facts[:, 1] * 64 + facts[:, 2]
    hits = facts[:, 3] == group_index
    hit_rank = jnp.cumsum(hits.astype(jnp.int32), axis=1) - 1
    chosen = hits[:, None, :] & (hit_rank[:, None, :] == lax.iota(jnp.int32, capacity)[None, :, None])
    found = jnp.sum(jnp.where(chosen, all_ids[:, None, :], 0), axis=2)
    return jnp.where(jnp.any(chosen, axis=2), found, -1).reshape(1, n_group * capacity)


def per_device(
    hidden,
    query_weight,
    key_value_weight,
    query_codes,
    query_scales,
    key_value_codes,
    key_value_scales,
    key_cache,
    value_cache,
    lengths,
    counts,
    learner,
    token_ids,
):
    games, steps, features = hidden.shape
    rows = games * steps
    n_group = lax.axis_size("group")
    n_tp = lax.axis_size("tp")
    chips = n_group // CORES
    group_index = lax.axis_index("group")
    tp_index = lax.axis_index("tp")
    chip = group_index // CORES
    core = group_index % CORES
    across = n_tp // KV_HEADS
    same_core = [[CORES * u + k for u in range(chips)] for k in range(CORES)]
    swap = [(g, g ^ 1) for g in range(n_group)]
    turn = [
        ((CORES * u + k) * n_tp + t, (CORES * t + k) * n_tp + u)
        for u in range(chips)
        for k in range(CORES)
        for t in range(n_tp)
    ]
    wide = HEADS // n_tp * HEAD
    capacity = max(2, 2 * rows // n_group)
    rounds, _, _, block, _ = key_cache.shape
    head = chip // (chips // KV_HEADS)
    place = jnp.stack([tp_index // across, tp_index % across, core, chip, head]).astype(jnp.int32)

    load = pl.pallas_call(
        load_kernel,
        out_shape=jax.ShapeDtypeStruct((chips, 2 * TILE, 3 * LANES), jnp.bfloat16),
        in_specs=[SMEM] + [VMEM] * 5,
        out_specs=VMEM,
        compiler_params=PARAMS,
        name="load",
    )(
        counts,
        hidden.reshape(rows, features),
        key_value_codes[0],
        key_value_scales[0].T,
        learner.transpose(0, 2, 1),
        token_ids,
    )
    came = lax.all_to_all(
        load, "group", split_axis=0, concat_axis=0, tiled=True, axis_index_groups=same_core
    )

    piece = jax.ShapeDtypeStruct((2, rounds, games, block, HEAD), jnp.bfloat16)
    query_mine, *pieces = pl.pallas_call(
        pieces_kernel,
        out_shape=[jax.ShapeDtypeStruct(query_codes.shape, jnp.bfloat16)] + [piece] * KV_HEADS,
        in_specs=[SMEM] + [VMEM] * 4,
        out_specs=[VMEM] * (1 + KV_HEADS),
        compiler_params=PARAMS,
        name="pieces",
    )(place, query_codes, query_scales.T, key_cache, value_cache)
    query_other = lax.ppermute(query_mine, "group", swap)
    for shift in range(1, KV_HEADS):
        pairs = [(t, (t + shift * across) % n_tp) for t in range(n_tp)]
        pieces[shift] = lax.ppermute(pieces[shift], "tp", pairs)
    delta_mine = came[:, rows:]
    delta_other = lax.ppermute(delta_mine, "group", swap)

    part, shard = pl.pallas_call(
        part_kernel,
        grid_spec=pltpu.PrefetchScalarGridSpec(
            num_scalar_prefetch=1,
            grid=(1,),
            in_specs=[VMEM] * 4
            + [
                pl.BlockSpec((features, wide), lambda i, place: (0, place[3])),
                pl.BlockSpec((features, HEAD), lambda i, place: (0, place[4])),
                pl.BlockSpec((features, HEAD), lambda i, place: (0, KV_HEADS + place[4])),
            ]
            + [VMEM] * 4,
            out_specs=[VMEM] * 2,
        ),
        out_shape=[
            jax.ShapeDtypeStruct((chips, rows, wide + 2 * HEAD), jnp.float32),
            jax.ShapeDtypeStruct((KV_HEADS,) + piece.shape, jnp.bfloat16),
        ],
        compiler_params=PARAMS,
        name="part",
    )(
        place,
        came,
        delta_other,
        query_mine,
        query_other,
        query_weight,
        key_value_weight,
        key_value_weight,
        *pieces,
    )
    parts = lax.all_to_all(part, "tp", split_axis=0, concat_axis=0, tiled=True)
    shards = [shard]
    for shift in range(1, across):
        pairs = [(t, t // across * across + (t + shift) % across) for t in range(n_tp)]
        shards.append(lax.ppermute(shard, "tp", pairs))
    mine = jnp.sum(parts, axis=0).astype(jnp.bfloat16)
    mine = lax.ppermute(mine, ("group", "tp"), turn)

    packed = pl.pallas_call(
        attend_kernel,
        out_shape=jax.ShapeDtypeStruct((n_group * capacity, wide), jnp.bfloat16),
        in_specs=[SMEM, SMEM] + [VMEM] * 6,
        out_specs=VMEM,
        compiler_params=PARAMS,
        name="attend",
    )(place, lengths, mine, places(counts, learner, n_group, capacity), *shards)
    packed = packed.reshape(n_group, capacity, wide)
    rows_back = lax.all_to_all(packed, "group", split_axis=0, concat_axis=1, tiled=True)

    both = jnp.stack([delta_mine, delta_other])[:, :, : 4 * games, 2 * HEAD : 2 * HEAD + steps]
    both = jnp.where(core == 0, both, both[::-1]).transpose(1, 0, 2, 3)
    ids_back = ids_of(both.reshape(n_group, 4 * games, steps), group_index, capacity)
    return (rows_back, ids_back)


def solution(mesh):
    placed = (
        P("group", None, "tp"),
        P("tp", None),
        P("tp", None),
        P("tp", "group"),
        P("tp", "group"),
        P("tp", "group", None),
        P("tp", "group", None),
        P(None, "tp", "group", None, None),
        P(None, "tp", "group", None, None),
        P("group"),
        P("group"),
        P("group", None, None),
        P("group", None),
    )
    return jax.shard_map(
        per_device,
        mesh=mesh,
        in_specs=placed,
        out_specs=(P("group", None, "tp"), P("group", None)),
        check_vma=False,
    )
```

time: 134 us -> 121 us (0.903)
  starting transfers between devices: 53.1 us -> 72.9 us
  waiting for transfers between devices: 43.1 us -> 25.2 us
  other arithmetic: 11.5 us -> 2.76 us
  matrix products: 6.79 us -> 0 us
  Pallas kernels: 0 us -> 5.51 us
  local copies, waits for them, and re-layouts: 17.7 us -> 12.5 us
    ppermute x0 -> x6, starting transfers between devices: none -> 19.7 us  [the longest x3 10.7 us: per_device(): shards.append(lax.ppermute(shard, 'tp', pairs))]
    all_to_all x1 -> x0, waiting for transfers between devices: 18.6 us -> none  [per_device(): cache = lax.all_to_all(both, 'tp', split_axis=0, concat_axis=0, tiled=True)]
    all_to_all x1, starting transfers between devices: 15.7 us -> 27.5 us  [per_device(): lax.all_to_all(packed, 'group', split_axis=0, concat_axis=1, tiled=True)]
    unnamed x24 -> x28, local copies, waits for them, and re-layouts: 1.08 us -> 9.92 us
    dot_general x8 -> x0, matrix products: 6.79 us -> none  [the longest x1 1.98 us: per_device(): jnp.dot(x_all, query_delta, preferred_element_type=jnp.float32)]
    pallas_call x0 -> x4, Pallas kernels: none -> 5.51 us  [the longest x1 2.06 us: per_device(): pl.pallas_call(part_kernel, grid_spec=pltpu.PrefetchScalarGridSpec(num_sc...]
    all_to_all x1, starting transfers between devices: 8.42 us -> 3.58 us  [per_device(): parts = lax.all_to_all(part, 'tp', split_axis=0, concat_axis=0, tiled=True)]
    all_to_all x1 -> x0, starting transfers between devices: 4.68 us -> none  [per_device(): cache = lax.all_to_all(both, 'tp', split_axis=0, concat_axis=0, tiled=True)]
  transfers between devices with their start and end apart: 7 -> 12, of which waited for: 4 -> 3; matrix products, arithmetic and copies ran while one was open for 13% -> 4% of each run, Pallas kernels for 0% -> 1%
where the time goes in v2:
time: 121 us; the launch traced here: 120 us
  starting transfers between devices  72.9 us (60%)
  waiting for transfers between devices  25.2 us (21%)
  local copies, waits for them, and re-layouts  12.5 us (10%)
  Pallas kernels  5.51 us (5%)
  other arithmetic  2.76 us (2%)
    all_to_all x1, starting transfers between devices, per_device(): lax.all_to_all(packed, 'group', split_axis=0, concat_axis=1, tiled=True)  27.5 us
    all_to_all x1, starting transfers between devices, per_device(): lax.all_to_all(load, 'group', split_axis=0, concat_axis=0, tiled=True, ax...  16.2 us
    all_to_all x1, waiting for transfers between devices, per_device(): parts = lax.all_to_all(part, 'tp', split_axis=0, concat_axis=0, tiled=True)  12.9 us
    all_to_all x1, waiting for transfers between devices, per_device(): lax.all_to_all(packed, 'group', split_axis=0, concat_axis=1, tiled=True)  11.3 us
    ppermute x3, starting transfers between devices, per_device(): shards.append(lax.ppermute(shard, 'tp', pairs))  10.7 us
    unnamed x28, local copies, waits for them, and re-layouts  9.92 us
    ppermute x3, starting transfers between devices, per_device(): pieces[shift] = lax.ppermute(pieces[shift], 'tp', pairs)  9 us
    all_to_all x1, starting transfers between devices, per_device(): parts = lax.all_to_all(part, 'tp', split_axis=0, concat_axis=0, tiled=True)  3.58 us
  transfers between devices with their start and end apart: 12, of which 3 were waited for; matrix products, arithmetic and copies ran while one was open for 4% of the time, Pallas kernels for 1%

profile of v2, /device:TPU:1, one launch (start us, length us, event | category | flops | bytes accessed | tf_op | source)
XLA Modules:
  0.0 119.9 jit_solution(17691416105651192446)
XLA Ops:
  0.7 0.8 copy-done.5
  4.9 1.4 %load.1 = bf16[16,32,384]{2,1,0:T(8,128)(2,1)} custom-call(s32[2]{0:T(128)S(1)} %copy-done.12, bf16[16,320]{1,0:T(8,128)(2,1)S(1)} %bitcast.28, bf16[10,1024]{1,0:T(8,128)(2,1)S(1)} %bitcast.27, f32[8,10]{1,0:T(8,128)S(1)} %bitcast.29, s32[2,1,8]{2,1,0:T(1,128)S(1)} %bitcast.30, s32[2,8]{1,0:T(2,128)S(1)} %copy-done.10), custom_call_target="tpu_custom_call" | custom-call | tf_op jit(solution)/shard_map/load/pallas_call | solution.py:259
  6.3 16.2 %all-to-all-start = ((bf16[16,32,384]{2,1,0:T(8,128)(2,1)}), bf16[16,32,384]{2,1,0:T(8,128)(2,1)S(1)}, u32[]{:S(2)}, u32[]{:S(2)}) async-start(bf16[16,32,384]{2,1,0:T(8,128)(2,1)} %load.1), calls=%async_computation | async-start | bytes 786432 | tf_op jit(solution)/shard_map/all_to_all | solution.py:274
  22.6 0.9 copy-done.2
  23.5 0.9 copy-done.3
  24.4 0.9 copy-done.4
  26.7 2.9 %collective-permute-start.1 = (bf16[320,128]{1,0:T(8,128)(2,1)S(1)}, bf16[320,128]{1,0:T(8,128)(2,1)S(1)}, u32[]{:S(2)}, u32[]{:S(2)}) collective-permute-start(bf16[320,128]{1,0:T(8,128)(2,1)S(1)} %get-tuple-element.9.delta_mine_ref), channel_id=1, source_target_pairs={{0,16},{16,0},{32,48},{48,32},{64,80},{80,64},{96,112},{112,96},{1... | collective-permute-start | bytes 245768 | tf_op jit(solution)/shard_map/ppermute | solution.py:287
  29.5 2.3 %collective-permute-start.2 = (bf16[2,4,2,16,128]{4,3,2,1,0:T(8,128)(2,1)S(1)}, bf16[2,4,2,16,128]{4,3,2,1,0:T(8,128)(2,1)S(1)}, u32[]{:S(2)}, u32[]{:S(2)}) collective-permute-start(bf16[2,4,2,16,128]{4,3,2,1,0:T(8,128)(2,1)S(1)} %get-tuple-element.11), channel_id=1, source_target_pairs={{0,4},{1,5},{2,6},{3,7},{4,8},{5,9},{6,10},{7,11},{8,12},{9,13},{1... | collective-permute-start | bytes 196616 | tf_op jit(solution)/shard_map/ppermute | solution.py:290
  31.9 2.4 %collective-permute-start.3 = (bf16[2,4,2,16,128]{4,3,2,1,0:T(8,128)(2,1)S(1)}, bf16[2,4,2,16,128]{4,3,2,1,0:T(8,128)(2,1)S(1)}, u32[]{:S(2)}, u32[]{:S(2)}) collective-permute-start(bf16[2,4,2,16,128]{4,3,2,1,0:T(8,128)(2,1)S(1)} %get-tuple-element.12), channel_id=1, source_target_pairs={{0,8},{1,9},{2,10},{3,11},{4,12},{5,13},{6,14},{7,15},{8,0},{9,1},... | collective-permute-start | bytes 196616 | tf_op jit(solution)/shard_map/ppermute | solution.py:290
  34.3 4.3 %collective-permute-start.4 = (bf16[2,4,2,16,128]{4,3,2,1,0:T(8,128)(2,1)S(1)}, bf16[2,4,2,16,128]{4,3,2,1,0:T(8,128)(2,1)S(1)}, u32[]{:S(2)}, u32[]{:S(2)}) collective-permute-start(bf16[2,4,2,16,128]{4,3,2,1,0:T(8,128)(2,1)S(1)} %get-tuple-element.13), channel_id=1, source_target_pairs={{0,12},{1,13},{2,14},{3,15},{4,0},{5,1},{6,2},{7,3},{8,4},{9,5},{1... | collective-permute-start | bytes 196616 | tf_op jit(solution)/shard_map/ppermute | solution.py:290
  38.6 0.7 iota_compare_fusion.3
  39.9 1.3 %reduce.3 = s32[2,8]{1,0:T(2,128)S(1)} reduce(s32[2,8,1]{1,2,0:T(1,128)} %param.24, s32[]{:T(128)} %broadcast.59), dimensions={2}, to_apply=%param.24.reduce_sub_computation.3 | reduce | bytes 132 | tf_op args[11]
  41.7 2.5 %collective-permute-start = (bf16[16,16,384]{2,1,0:T(8,128)(2,1)S(1)}, bf16[16,16,384]{2,1,0:T(8,128)(2,1)S(1)}, u32[]{:S(2)}, u32[]{:S(2)}) collective-permute-start(bf16[16,16,384]{2,1,0:T(8,128)(2,1)S(1)} %get-tuple-element.19), channel_id=1, source_target_pairs={{0,16},{16,0},{32,48},{48,32},{64,80},{80,64},{96,112},{112,96},{1... | collective-permute-start | bytes 589832 | tf_op jit(solution)/shard_map/ppermute | solution.py:292
  44.2 1.0 collective-permute-done.other_ref
  45.2 1.7 %copy-done.1 = bf16[320,4096]{1,0:T(8,128)(2,1)S(1)} copy-done((bf16[320,4096]{1,0:T(8,128)(2,1)S(1)}, bf16[320,4096]{1,0:T(8,128)(2,1)}, u32[]{:S(2)}) %copy-start.1) | copy-done | bytes 2621464
  47.0 2.1 %part.1 = (f32[16,16,512]{2,1,0:T(8,128)}, bf16[4,2,4,2,16,128]{5,4,3,2,1,0:T(8,128)(2,1)S(1)}) custom-call(s32[5]{0:T(128)S(1)} %stack.32.place_ref, bf16[16,32,384]{2,1,0:T(8,128)(2,1)S(1)} %all-to-all-done.came_ref, bf16[16,16,384]{2,1,0:T(8,128)(2,1)S(1)} %collective-permute-done.other_ref, bf16[320,128]{1,0:T(8,128)(2,1)S(1)} %get-tuple-element.9.delta_mine_ref, ...), custom_call_target="tpu_custom_call" | custom-call | tf_op jit(solution)/shard_map/part/pallas_call | solution.py:294
  49.0 3.2 %collective-permute-start.6 = (bf16[4,2,4,2,16,128]{5,4,3,2,1,0:T(8,128)(2,1)S(1)}, bf16[4,2,4,2,16,128]{5,4,3,2,1,0:T(8,128)(2,1)S(1)}, u32[]{:S(2)}, u32[]{:S(2)}) collective-permute-start(bf16[4,2,4,2,16,128]{5,4,3,2,1,0:T(8,128)(2,1)S(1)} %get-tuple-element.15.shard0_ref), channel_id=1, source_target_pairs={{0,1},{1,2},{2,3},{3,0},{4,5},{5,6},{6,7},{7,4},{8,9},{9,10},{10,1... | collective-permute-start | bytes 786440 | tf_op jit(solution)/shard_map/ppermute | solution.py:329
  52.3 4.4 %collective-permute-start.7 = (bf16[4,2,4,2,16,128]{5,4,3,2,1,0:T(8,128)(2,1)S(1)}, bf16[4,2,4,2,16,128]{5,4,3,2,1,0:T(8,128)(2,1)S(1)}, u32[]{:S(2)}, u32[]{:S(2)}) collective-permute-start(bf16[4,2,4,2,16,128]{5,4,3,2,1,0:T(8,128)(2,1)S(1)} %get-tuple-element.15.shard0_ref), channel_id=1, source_target_pairs={{0,2},{1,3},{2,0},{3,1},{4,6},{5,7},{6,4},{7,5},{8,10},{9,11},{10,... | collective-permute-start | bytes 786440 | tf_op jit(solution)/shard_map/ppermute | solution.py:329
  56.7 3.1 %collective-permute-start.8 = (bf16[4,2,4,2,16,128]{5,4,3,2,1,0:T(8,128)(2,1)S(1)}, bf16[4,2,4,2,16,128]{5,4,3,2,1,0:T(8,128)(2,1)S(1)}, u32[]{:S(2)}, u32[]{:S(2)}) collective-permute-start(bf16[4,2,4,2,16,128]{5,4,3,2,1,0:T(8,128)(2,1)S(1)} %get-tuple-element.15.shard0_ref), channel_id=1, source_target_pairs={{0,3},{1,0},{2,1},{3,2},{4,7},{5,4},{6,5},{7,6},{8,11},{9,8},{10,9... | collective-permute-start | bytes 786440 | tf_op jit(solution)/shard_map/ppermute | solution.py:329
  59.7 3.6 %all-to-all-start.1 = ((f32[16,16,512]{2,1,0:T(8,128)}), f32[16,16,512]{2,1,0:T(8,128)S(1)}, u32[]{:S(2)}, u32[]{:S(2)}) async-start(f32[16,16,512]{2,1,0:T(8,128)} %get-tuple-element.14), calls=%async_computation.1 | async-start | bytes 1048576 | tf_op jit(solution)/shard_map/all_to_all | solution.py:325
  64.0 12.9 %all-to-all-done.1 = f32[16,16,512]{2,1,0:T(8,128)S(1)} async-done(((f32[16,16,512]{2,1,0:T(8,128)}), f32[16,16,512]{2,1,0:T(8,128)S(1)}, u32[]{:S(2)}, u32[]{:S(2)}) %all-to-all-start.1) | async-done | bytes 524320 | tf_op jit(solution)/shard_map/all_to_all | solution.py:325
  77.7 1.4 %attend.1 = bf16[64,256]{1,0:T(8,128)(2,1)S(1)} custom-call(s32[5]{0:T(128)S(1)} %stack.32.place_ref, s32[2]{0:T(128)S(1)} %copy-done.11, bf16[16,512]{1,0:T(8,128)(2,1)S(1)} %collective-permute-done.5.mine_ref, bf16[64,16]{1,0:T(8,128)(2,1)S(1)} %fusion.placed_ref, bf16[4,2,4,2,16,128]{5,4,3,2,1,0:T(8,128)(2,1)S(1)} %get-tuple-element.15.shard0_ref, ...), custom_call_target="tpu_custom_call" | custom-call | tf_op jit(solution)/shard_map/attend/pallas_call | solution.py:333
  79.8 27.5 %all-to-all-start.2 = ((bf16[32,2,256]{2,1,0:T(2,128)(2,1)}), bf16[32,2,256]{2,1,0:T(2,128)(2,1)S(1)}, u32[]{:S(2)}, u32[]{:S(2)}) async-start(bf16[32,2,256]{2,1,0:T(2,128)(2,1)} %reshape.85), calls=%async_computation.2 | async-start | bytes 65536 | tf_op jit(solution)/shard_map/all_to_all | solution.py:342
  107.9 11.3 %all-to-all-done.2 = bf16[32,2,256]{2,1,0:T(2,128)(2,1)S(1)} async-done(((bf16[32,2,256]{2,1,0:T(2,128)(2,1)}), bf16[32,2,256]{2,1,0:T(2,128)(2,1)S(1)}, u32[]{:S(2)}, u32[]{:S(2)}) %all-to-all-start.2) | async-done | bytes 32800 | tf_op jit(solution)/shard_map/all_to_all | solution.py:342
  (63 shorter events, 9.3 us)
Async XLA Ops:
  0.6 44.6 %copy-start = (bf16[320,1024]{1,0:T(8,128)(2,1)S(1)}, bf16[320,1024]{1,0:T(8,128)(2,1)}, u32[]{:S(2)}) copy-start(bf16[320,1024]{1,0:T(8,128)(2,1)} %value_ref.3) | copy-start | bytes 1966084
  0.6 0.8 copy-start.5
  1.5 0.7 copy-start.6
  2.2 0.7 copy-start.7
  2.9 0.7 copy-start.8
  3.5 0.7 copy-start.10
  6.3 35.4 %all-to-all-start = ((bf16[16,32,384]{2,1,0:T(8,128)(2,1)}), bf16[16,32,384]{2,1,0:T(8,128)(2,1)S(1)}, u32[]{:S(2)}, u32[]{:S(2)}) async-start(bf16[16,32,384]{2,1,0:T(8,128)(2,1)} %load.1), calls=%async_computation | async-start | bytes 786432 | tf_op jit(solution)/shard_map/all_to_all | solution.py:274
  22.6 0.9 copy-start.2
  23.5 0.9 copy-start.3
  24.4 0.9 copy-start.4
  25.3 0.7 copy-start.9
  26.7 17.6 %collective-permute-start.1 = (bf16[320,128]{1,0:T(8,128)(2,1)S(1)}, bf16[320,128]{1,0:T(8,128)(2,1)S(1)}, u32[]{:S(2)}, u32[]{:S(2)}) collective-permute-start(bf16[320,128]{1,0:T(8,128)(2,1)S(1)} %get-tuple-element.9.delta_mine_ref), channel_id=1, source_target_pairs={{0,16},{16,0},{32,48},{48,32},{64,80},{80,64},{96,112},{112,96},{1... | collective-permute-start | bytes 245768 | tf_op jit(solution)/shard_map/ppermute | solution.py:287
  29.5 14.7 %collective-permute-start.2 = (bf16[2,4,2,16,128]{4,3,2,1,0:T(8,128)(2,1)S(1)}, bf16[2,4,2,16,128]{4,3,2,1,0:T(8,128)(2,1)S(1)}, u32[]{:S(2)}, u32[]{:S(2)}) collective-permute-start(bf16[2,4,2,16,128]{4,3,2,1,0:T(8,128)(2,1)S(1)} %get-tuple-element.11), channel_id=1, source_target_pairs={{0,4},{1,5},{2,6},{3,7},{4,8},{5,9},{6,10},{7,11},{8,12},{9,13},{1... | collective-permute-start | bytes 196616 | tf_op jit(solution)/shard_map/ppermute | solution.py:290
  31.9 12.4 %collective-permute-start.3 = (bf16[2,4,2,16,128]{4,3,2,1,0:T(8,128)(2,1)S(1)}, bf16[2,4,2,16,128]{4,3,2,1,0:T(8,128)(2,1)S(1)}, u32[]{:S(2)}, u32[]{:S(2)}) collective-permute-start(bf16[2,4,2,16,128]{4,3,2,1,0:T(8,128)(2,1)S(1)} %get-tuple-element.12), channel_id=1, source_target_pairs={{0,8},{1,9},{2,10},{3,11},{4,12},{5,13},{6,14},{7,15},{8,0},{9,1},... | collective-permute-start | bytes 196616 | tf_op jit(solution)/shard_map/ppermute | solution.py:290
  34.3 9.9 %collective-permute-start.4 = (bf16[2,4,2,16,128]{4,3,2,1,0:T(8,128)(2,1)S(1)}, bf16[2,4,2,16,128]{4,3,2,1,0:T(8,128)(2,1)S(1)}, u32[]{:S(2)}, u32[]{:S(2)}) collective-permute-start(bf16[2,4,2,16,128]{4,3,2,1,0:T(8,128)(2,1)S(1)} %get-tuple-element.13), channel_id=1, source_target_pairs={{0,12},{1,13},{2,14},{3,15},{4,0},{5,1},{6,2},{7,3},{8,4},{9,5},{1... | collective-permute-start | bytes 196616 | tf_op jit(solution)/shard_map/ppermute | solution.py:290
  41.7 3.5 %collective-permute-start = (bf16[16,16,384]{2,1,0:T(8,128)(2,1)S(1)}, bf16[16,16,384]{2,1,0:T(8,128)(2,1)S(1)}, u32[]{:S(2)}, u32[]{:S(2)}) collective-permute-start(bf16[16,16,384]{2,1,0:T(8,128)(2,1)S(1)} %get-tuple-element.19), channel_id=1, source_target_pairs={{0,16},{16,0},{32,48},{48,32},{64,80},{80,64},{96,112},{112,96},{1... | collective-permute-start | bytes 589832 | tf_op jit(solution)/shard_map/ppermute | solution.py:292
  45.2 1.7 %copy-start.1 = (bf16[320,4096]{1,0:T(8,128)(2,1)S(1)}, bf16[320,4096]{1,0:T(8,128)(2,1)}, u32[]{:S(2)}) copy-start(bf16[320,4096]{1,0:T(8,128)(2,1)} %query_ref.1) | copy-start | bytes 7864324
  49.0 28.7 %copy-start.11 = (s32[2]{0:T(128)S(1)}, s32[2]{0:T(128)}, u32[]{:S(2)}) copy-start(s32[2]{0:T(128)} %lengths_ref.1) | copy-start | bytes 28
  49.0 28.6 %collective-permute-start.6 = (bf16[4,2,4,2,16,128]{5,4,3,2,1,0:T(8,128)(2,1)S(1)}, bf16[4,2,4,2,16,128]{5,4,3,2,1,0:T(8,128)(2,1)S(1)}, u32[]{:S(2)}, u32[]{:S(2)}) collective-permute-start(bf16[4,2,4,2,16,128]{5,4,3,2,1,0:T(8,128)(2,1)S(1)} %get-tuple-element.15.shard0_ref), channel_id=1, source_target_pairs={{0,1},{1,2},{2,3},{3,0},{4,5},{5,6},{6,7},{7,4},{8,9},{9,10},{10,1... | collective-permute-start | bytes 786440 | tf_op jit(solution)/shard_map/ppermute | solution.py:329
  52.3 25.4 %collective-permute-start.7 = (bf16[4,2,4,2,16,128]{5,4,3,2,1,0:T(8,128)(2,1)S(1)}, bf16[4,2,4,2,16,128]{5,4,3,2,1,0:T(8,128)(2,1)S(1)}, u32[]{:S(2)}, u32[]{:S(2)}) collective-permute-start(bf16[4,2,4,2,16,128]{5,4,3,2,1,0:T(8,128)(2,1)S(1)} %get-tuple-element.15.shard0_ref), channel_id=1, source_target_pairs={{0,2},{1,3},{2,0},{3,1},{4,6},{5,7},{6,4},{7,5},{8,10},{9,11},{10,... | collective-permute-start | bytes 786440 | tf_op jit(solution)/shard_map/ppermute | solution.py:329
  56.7 21.0 %collective-permute-start.8 = (bf16[4,2,4,2,16,128]{5,4,3,2,1,0:T(8,128)(2,1)S(1)}, bf16[4,2,4,2,16,128]{5,4,3,2,1,0:T(8,128)(2,1)S(1)}, u32[]{:S(2)}, u32[]{:S(2)}) collective-permute-start(bf16[4,2,4,2,16,128]{5,4,3,2,1,0:T(8,128)(2,1)S(1)} %get-tuple-element.15.shard0_ref), channel_id=1, source_target_pairs={{0,3},{1,0},{2,1},{3,2},{4,7},{5,4},{6,5},{7,6},{8,11},{9,8},{10,9... | collective-permute-start | bytes 786440 | tf_op jit(solution)/shard_map/ppermute | solution.py:329
  59.7 17.2 %all-to-all-start.1 = ((f32[16,16,512]{2,1,0:T(8,128)}), f32[16,16,512]{2,1,0:T(8,128)S(1)}, u32[]{:S(2)}, u32[]{:S(2)}) async-start(f32[16,16,512]{2,1,0:T(8,128)} %get-tuple-element.14), calls=%async_computation.1 | async-start | bytes 1048576 | tf_op jit(solution)/shard_map/all_to_all | solution.py:325
  77.0 0.7 collective-permute-start.5
  79.8 39.5 %all-to-all-start.2 = ((bf16[32,2,256]{2,1,0:T(2,128)(2,1)}), bf16[32,2,256]{2,1,0:T(2,128)(2,1)S(1)}, u32[]{:S(2)}, u32[]{:S(2)}) async-start(bf16[32,2,256]{2,1,0:T(2,128)(2,1)} %reshape.85), calls=%async_computation.2 | async-start | bytes 65536 | tf_op jit(solution)/shard_map/all_to_all | solution.py:342
  (1 other events, 0.7 us)

commit v3 on v2

v3 whole, which is shorter than its diff:
```python
import math

import jax
import jax.numpy as jnp
from jax import lax
from jax.experimental import pallas as pl
from jax.experimental.pallas import tpu as pltpu
from jax.sharding import PartitionSpec as P

HEADS = 32
KV_HEADS = 4
HEAD = 128
CORES = 2
TILE = 16
LANES = 128


NEG_FILL = -1e30

VMEM = pl.BlockSpec(memory_space=pltpu.VMEM)
SMEM = pl.BlockSpec(memory_space=pltpu.SMEM)
HBM = pl.BlockSpec(memory_space=pltpu.HBM)
ANY = pl.BlockSpec(memory_space=pl.ANY)
PARAMS = pltpu.CompilerParams(vmem_limit_bytes=24 * 1024 * 1024)


def column(row):
    n = row.shape[1]
    across = lax.broadcasted_iota(jnp.int32, (n, n), 1)
    down = lax.broadcasted_iota(jnp.int32, (n, n), 0)
    return jnp.sum(jnp.where(across == down, row, jnp.zeros_like(row)), axis=1, keepdims=True)


def fetch(pairs, sems):
    copies = [
        pltpu.make_async_copy(source, target, sems.at[i]) for i, (source, target) in enumerate(pairs)
    ]
    for copy in copies:
        copy.start()
    return copies


def load_kernel(
    counts_hbm,
    hidden_hbm,
    codes_hbm,
    scales_hbm,
    learner_hbm,
    ids_hbm,
    load_ref,
    named_ref,
    counts_ref,
    hidden_ref,
    codes_ref,
    scales_ref,
    learner_ref,
    ids_ref,
    sems,
):
    copies = fetch(
        [
            (codes_hbm, codes_ref),
            (scales_hbm, scales_ref),
            (hidden_hbm, hidden_ref),
            (counts_hbm, counts_ref),
            (learner_hbm, learner_ref),
            (ids_hbm, ids_ref),
        ],
        sems,
    )
    chips = load_ref.shape[0]
    rows, features = hidden_ref.shape
    pair_rows = codes_ref.shape[0]
    games, steps = ids_ref.shape
    load_ref[...] = jnp.zeros_like(load_ref)
    for copy in copies:
        copy.wait()
    load_ref[:, :rows, :features] = jnp.broadcast_to(hidden_ref[...], (chips, rows, features))
    per_head = chips // KV_HEADS
    for block in range(2 * KV_HEADS):
        scale = column(scales_ref[block : block + 1, :])
        codes = codes_ref[:, block * HEAD : (block + 1) * HEAD].astype(jnp.float32)
        delta = (codes * scale).astype(jnp.bfloat16)
        head, part = block % KV_HEADS, block // KV_HEADS
        load_ref[
            head * per_head : (head + 1) * per_head,
            rows : rows + pair_rows,
            part * HEAD : (part + 1) * HEAD,
        ] = jnp.broadcast_to(delta, (per_head, pair_rows, HEAD))
    step = lax.broadcasted_iota(jnp.int32, (1, steps), 1)
    ids = ids_ref[...]
    named = [
        jnp.where(step < counts_ref[game], learner_ref[game], -1) for game in range(games)
    ]
    named_ref[...] = jnp.concatenate(named, axis=1)
    facts = jnp.concatenate([ids >> 12, (ids >> 6) & 63, ids & 63] + named, axis=0)
    facts = facts.astype(jnp.float32).astype(jnp.bfloat16)
    load_ref[:, rows : rows + 4 * games, 2 * HEAD : 2 * HEAD + steps] = jnp.broadcast_to(
        facts, (chips,) + facts.shape
    )


def pieces_kernel(
    codes_hbm,
    scales_hbm,
    key_hbm,
    value_hbm,
    delta_ref,
    piece0_ref,
    piece1_ref,
    piece2_ref,
    piece3_ref,
    codes_ref,
    scales_ref,
    sems,
    piece_sems,
):
    copies = fetch([(codes_hbm, codes_ref), (scales_hbm, scales_ref)], sems)
    own = lax.axis_index("tp") // (lax.axis_size("tp") // KV_HEADS)
    moves = []
    for shift, piece_ref in enumerate((piece0_ref, piece1_ref, piece2_ref, piece3_ref)):
        head = lax.rem(own + shift, KV_HEADS)
        lanes = pl.ds(pl.multiple_of(head * HEAD, HEAD), HEAD)
        for part, cache_hbm in enumerate((key_hbm, value_hbm)):
            moves.append((cache_hbm.at[:, 0, :, :, lanes], piece_ref.at[part]))
    moves = fetch(moves, piece_sems)
    for copy in copies:
        copy.wait()
    scale = column(scales_ref[...])
    delta_ref[...] = (codes_ref[...].astype(jnp.float32) * scale).astype(jnp.bfloat16)
    for copy in moves:
        copy.wait()


def swap_kernel(came_ref, query_ref, after1_ref, after2_ref, after3_ref, out_ref):
    chips, depth, width = came_ref.shape
    block = chips * TILE
    for i in range(width // LANES):
        out_ref[i * block : (i + 1) * block] = came_ref[
            :, depth - TILE :, i * LANES : (i + 1) * LANES
        ].reshape(block, LANES)
    out_ref[width // LANES * block :] = query_ref[...]


def part_kernel(
    came_ref,
    other_ref,
    delta_ref,
    query_hbm,
    pair_hbm,
    part_ref,
    query_ref,
    key_ref,
    value_ref,
    sems,
):
    chips, rows = part_ref.shape[:2]
    features, wide = query_ref.shape
    block = chips * TILE
    group_index = lax.axis_index("group")
    chip, core = group_index // CORES, lax.rem(group_index, CORES)
    head = chip // (chips // KV_HEADS)
    pair_rows = features // (chips * CORES)

    def columns(source, start, size):
        return source.at[:, pl.ds(pl.multiple_of(start, HEAD), size)]

    copies = fetch(
        [
            (columns(query_hbm, chip * wide, wide), query_ref),
            (columns(pair_hbm, head * HEAD, HEAD), key_ref),
            (columns(pair_hbm, (KV_HEADS + head) * HEAD, HEAD), value_ref),
        ],
        sems,
    )

    def dot(a, b):
        return jnp.dot(a, b, preferred_element_type=jnp.float32)

    inputs = came_ref[:, :rows, :features].reshape(block, features)
    spot = lax.broadcasted_iota(jnp.int32, (1, block), 1)
    feature = lax.broadcasted_iota(jnp.int32, (features, block), 0)
    keys = jnp.zeros((block, HEAD), jnp.float32)
    values = jnp.zeros((block, HEAD), jnp.float32)
    for turn in range(CORES):
        owner = (spot // TILE) * CORES + lax.rem(core + turn, CORES)
        source = jnp.where(spot % TILE < pair_rows, owner * pair_rows + spot % TILE, -1)
        spread = (feature == source).astype(jnp.float32).astype(jnp.bfloat16)
        spread = dot(inputs, spread).astype(jnp.bfloat16)
        if turn == 0:
            key_delta = came_ref[:, rows:, :HEAD].reshape(block, HEAD)
            value_delta = came_ref[:, rows:, HEAD : 2 * HEAD].reshape(block, HEAD)
        else:
            key_delta = other_ref[:block]
            value_delta = other_ref[block : 2 * block]
        keys = keys + dot(spread, key_delta)
        values = values + dot(spread, value_delta)
    mine, other = delta_ref[...], other_ref[3 * block :]
    first = dot(inputs, jnp.where(core == 0, mine, other))
    second = dot(inputs, jnp.where(core == 0, other, mine))
    for copy in copies:
        copy.wait()
    queries = dot(inputs, query_ref[...])

    def put(i, sums):
        part_ref[:, :, i * HEAD : (i + 1) * HEAD] = sums.reshape(chips, rows, HEAD)

    put(0, queries[:, :HEAD] + first)
    put(1, queries[:, HEAD:] + second)
    put(2, keys + dot(inputs, key_ref[...]))
    put(3, values + dot(inputs, value_ref[...]))


def join_kernel(after_ref, *refs):
    shard_ref = refs[-1]
    for shift, piece_ref in enumerate(refs[:-1]):
        shard_ref[shift] = piece_ref[...]


def facts_kernel(after_ref, named_ref, came_ref, other_ref, placed_ref, ids_ref):
    chips, depth, _ = came_ref.shape
    block = chips * TILE
    slots, rows = placed_ref.shape
    steps = rows // 2
    group_index = lax.axis_index("group")
    core = lax.rem(group_index, CORES)
    capacity = slots // (chips * CORES)

    named = named_ref[...].astype(jnp.float32)
    before = lax.broadcasted_iota(jnp.int32, (rows, rows), 0) < lax.broadcasted_iota(
        jnp.int32, (rows, rows), 1
    )
    rank = jnp.sum(jnp.where((column(named) == named) & before, 1.0, 0.0), axis=0, keepdims=True)
    slot = jnp.where(named >= 0, named * capacity + rank, -1.0)
    index = lax.broadcasted_iota(jnp.int32, (slots, rows), 0).astype(jnp.float32)
    placed_ref[...] = jnp.where(index == slot, 1.0, 0.0).astype(jnp.bfloat16)

    own = came_ref[:, depth - TILE :, 2 * HEAD :].astype(jnp.float32)
    other = other_ref[2 * block : 3 * block].reshape(own.shape).astype(jnp.float32)
    kind = lax.broadcasted_iota(jnp.int32, own.shape, 1)
    lane = lax.broadcasted_iota(jnp.int32, (chips, LANES), 1)
    out_lane = lax.broadcasted_iota(jnp.int32, (chips, slots), 1)
    out_chip = lax.broadcasted_iota(jnp.int32, (chips, slots), 0)
    ids = jnp.zeros((chips, slots), jnp.float32)
    for turn, facts in enumerate((own, other)):
        low = jnp.full((chips, 1), 1e9, jnp.float32)
        high = jnp.full((chips, 1), -1.0, jnp.float32)
        for game in range(rows // steps):

            def pick(i):
                return jnp.sum(jnp.where(kind == 2 * i + game, facts, 0.0), axis=1)

            number = pick(0) * 4096.0 + pick(1) * 64.0 + pick(2)
            hit = (pick(3) == group_index.astype(jnp.float32)) & (lane < steps)
            coded = (game * steps + lane).astype(jnp.float32) * 262144.0 + number
            low = jnp.minimum(low, jnp.min(jnp.where(hit, coded, 1e9), axis=1, keepdims=True))
            high = jnp.maximum(high, jnp.max(jnp.where(hit, coded, -1.0), axis=1, keepdims=True))
        sender = out_chip * CORES + lax.rem(core + turn, CORES)
        for k, (coded, there) in enumerate(((low, high >= 0), (high, high > low))):
            number = (coded.astype(jnp.int32) & 262143).astype(jnp.float32)
            value = jnp.where(there, number, -1.0)
            ids = ids + jnp.where(out_lane == sender * capacity + k, value, 0.0)
    ids_ref[...] = jnp.sum(ids, axis=0, keepdims=True).astype(jnp.int32)


def attend_kernel(
    lengths_ref,
    mine_ref,
    placed_ref,
    shard0_ref,
    shard1_ref,
    shard2_ref,
    shard3_ref,
    packed_ref,
):
    shards = (shard0_ref, shard1_ref, shard2_ref, shard3_ref)
    count, _, rounds, games, block, _ = shard0_ref.shape
    rows = mine_ref.shape[0]
    steps = rows // games
    heads = mine_ref.shape[1] // HEAD - 2
    n_tp = count * len(shards)
    factor = 1.0 / math.sqrt(HEAD)
    mine = mine_ref[...].astype(jnp.float32)
    spot = lax.broadcasted_iota(jnp.int32, (1, count * rounds * block), 1)
    tp_index = lax.axis_index("tp")
    positions = []
    for shift in range(len(shards)):
        across = lax.rem(lax.rem(tp_index, len(shards)) - shift + len(shards), len(shards))
        down = (tp_index // len(shards) - spot // (rounds * block) + count) % count
        tp = down * len(shards) + across
        positions.append((spot // block % rounds * n_tp + tp) * block + spot % block)
    contract = (((1,), (1,)), ((), ()))
    games_out = []
    for game in range(games):
        band = mine[game * steps : (game + 1) * steps]
        queries = jnp.concatenate(
            [band[:, h * HEAD : (h + 1) * HEAD] for h in range(heads)], axis=0
        ).astype(jnp.bfloat16)
        new_keys = band[:, heads * HEAD : (heads + 1) * HEAD].astype(jnp.bfloat16)
        new_values = band[:, (heads + 1) * HEAD :].astype(jnp.bfloat16)
        new_scores = factor * lax.dot_general(
            queries, new_keys, contract, preferred_element_type=jnp.float32
        )
        later = lax.broadcasted_iota(jnp.int32, new_scores.shape, 1)
        step = lax.broadcasted_iota(jnp.int32, new_scores.shape, 0) % steps
        new_valid = later <= step
        top = jnp.max(jnp.where(new_valid, new_scores, NEG_FILL), axis=1, keepdims=True)
        kept = []
        for shard_ref, position in zip(shards, positions):
            keys = shard_ref[:, 0, :, game].reshape(count * rounds * block, HEAD)
            scores = factor * lax.dot_general(
                queries, keys, contract, preferred_element_type=jnp.float32
            )
            scores = jnp.where(position < lengths_ref[game], scores, NEG_FILL)
            top = jnp.maximum(top, jnp.max(scores, axis=1, keepdims=True))
            kept.append(scores)
        weight = jnp.where(new_valid, jnp.exp(new_scores - top), 0.0).astype(jnp.bfloat16)
        total = jnp.sum(weight.astype(jnp.float32), axis=1, keepdims=True)
        mixed = jnp.dot(weight, new_values, preferred_element_type=jnp.float32)
        for shard_ref, position, scores in zip(shards, positions, kept):
            values = shard_ref[:, 1, :, game].reshape(count * rounds * block, HEAD)
            weight = jnp.where(
                position < lengths_ref[game], jnp.exp(scores - top), 0.0
            ).astype(jnp.bfloat16)
            total = total + jnp.sum(weight.astype(jnp.float32), axis=1, keepdims=True)
            mixed = mixed + jnp.dot(weight, values, preferred_element_type=jnp.float32)
        out = mixed / total
        games_out.append(
            jnp.concatenate([out[h * steps : (h + 1) * steps] for h in range(heads)], axis=1)
        )
    attended = jnp.concatenate(games_out, axis=0).astype(jnp.bfloat16)
    packed_ref[...] = jnp.dot(
        placed_ref[...], attended, preferred_element_type=jnp.float32
    ).astype(jnp.bfloat16)


def per_device(
    hidden,
    query_weight,
    key_value_weight,
    query_codes,
    query_scales,
    key_value_codes,
    key_value_scales,
    key_cache,
    value_cache,
    lengths,
    counts,
    learner,
    token_ids,
):
    games, steps, features = hidden.shape
    rows = games * steps
    n_group = lax.axis_size("group")
    n_tp = lax.axis_size("tp")
    chips = n_group // CORES
    across = n_tp // KV_HEADS
    same_core = [[CORES * u + k for u in range(chips)] for k in range(CORES)]
    swap = [(g, g ^ 1) for g in range(n_group)]
    turn = [
        ((CORES * u + k) * n_tp + t, (CORES * t + k) * n_tp + u)
        for u in range(chips)
        for k in range(CORES)
        for t in range(n_tp)
    ]
    wide = HEADS // n_tp * HEAD
    capacity = max(2, 2 * rows // n_group)
    rounds, _, _, block, _ = key_cache.shape
    pair_rows = key_value_codes.shape[1]
    bf16 = jnp.bfloat16

    def far(x):
        return pltpu.with_memory_space_constraint(x, pltpu.HBM)


    load, named = pl.pallas_call(
        load_kernel,
        out_shape=[
            jax.ShapeDtypeStruct((chips, 2 * TILE, 3 * LANES), bf16),
            jax.ShapeDtypeStruct((1, rows), jnp.int32),
        ],
        in_specs=[HBM] * 6,
        out_specs=[VMEM] * 2,
        scratch_shapes=[
            pltpu.SMEM((games,), jnp.int32),
            pltpu.VMEM((rows, features), bf16),
            pltpu.VMEM((pair_rows, 2 * KV_HEADS * HEAD), bf16),
            pltpu.VMEM((2 * KV_HEADS, pair_rows), jnp.float32),
            pltpu.VMEM((games, 1, steps), jnp.int32),
            pltpu.VMEM((games, steps), jnp.int32),
            pltpu.SemaphoreType.DMA((6,)),
        ],
        compiler_params=PARAMS,
        name="load",
    )(
        far(counts),
        far(hidden.reshape(rows, features)),
        far(key_value_codes[0]),
        far(key_value_scales[0].T),
        far(learner.transpose(0, 2, 1)),
        far(token_ids),
    )
    came = lax.all_to_all(
        load, "group", split_axis=0, concat_axis=0, tiled=True, axis_index_groups=same_core
    )

    piece = jax.ShapeDtypeStruct((2, rounds, games, block, HEAD), bf16)
    query_delta, *pieces = pl.pallas_call(
        pieces_kernel,
        out_shape=[jax.ShapeDtypeStruct(query_codes.shape, bf16)] + [piece] * KV_HEADS,
        in_specs=[HBM] * 4,
        out_specs=[VMEM] * (1 + KV_HEADS),
        scratch_shapes=[
            pltpu.VMEM(query_codes.shape, bf16),
            pltpu.VMEM((1, features), jnp.float32),
            pltpu.SemaphoreType.DMA((2,)),
            pltpu.SemaphoreType.DMA((2 * KV_HEADS,)),
        ],
        compiler_params=PARAMS,
        name="pieces",
    )(far(query_codes), far(query_scales.T), far(key_cache), far(value_cache))
    for shift in range(1, KV_HEADS):
        pairs = [(t, (t + shift * across) % n_tp) for t in range(n_tp)]
        pieces[shift] = lax.ppermute(pieces[shift], "tp", pairs)
    other = pl.pallas_call(
        swap_kernel,
        out_shape=jax.ShapeDtypeStruct((3 * chips * TILE + features, LANES), bf16),
        in_specs=[VMEM] * 2 + [ANY] * (KV_HEADS - 1),
        out_specs=VMEM,
        compiler_params=PARAMS,
        name="swap",
    )(came, query_delta, *pieces[1:])
    other = lax.ppermute(other, "group", swap)

    part = pl.pallas_call(
        part_kernel,
        out_shape=jax.ShapeDtypeStruct((chips, rows, wide + 2 * HEAD), jnp.float32),
        in_specs=[VMEM] * 3 + [HBM] * 2,
        out_specs=VMEM,
        scratch_shapes=[
            pltpu.VMEM((features, wide), bf16),
            pltpu.VMEM((features, HEAD), bf16),
            pltpu.VMEM((features, HEAD), bf16),
            pltpu.SemaphoreType.DMA((3,)),
        ],
        compiler_params=PARAMS,
        name="part",
    )(came, other, query_delta, far(query_weight), far(key_value_weight))
    parts = lax.all_to_all(part, "tp", split_axis=0, concat_axis=0, tiled=True)

    shard = pl.pallas_call(
        join_kernel,
        out_shape=jax.ShapeDtypeStruct((KV_HEADS,) + piece.shape, bf16),
        in_specs=[ANY] + [VMEM] * KV_HEADS,
        out_specs=VMEM,
        compiler_params=PARAMS,
        name="join",
    )(part, *pieces)
    shards = [shard]
    for shift in range(1, across):
        pairs = [(t, t // across * across + (t + shift) % across) for t in range(n_tp)]
        shards.append(lax.ppermute(shard, "tp", pairs))
    mine = jnp.sum(parts, axis=0).astype(bf16)
    mine = lax.ppermute(mine, ("group", "tp"), turn)

    placed, ids_back = pl.pallas_call(
        facts_kernel,
        out_shape=[
            jax.ShapeDtypeStruct((n_group * capacity, rows), bf16),
            jax.ShapeDtypeStruct((1, n_group * capacity), jnp.int32),
        ],
        in_specs=[ANY] + [VMEM] * 3,
        out_specs=[VMEM] * 2,
        compiler_params=PARAMS,
        name="facts",
    )(parts, named, came, other)

    packed = pl.pallas_call(
        attend_kernel,
        out_shape=jax.ShapeDtypeStruct((n_group * capacity, wide), bf16),
        in_specs=[SMEM] + [VMEM] * 6,
        out_specs=VMEM,
        compiler_params=PARAMS,
        name="attend",
    )(lengths, mine, placed, *shards)
    packed = packed.reshape(n_group, capacity, wide)
    rows_back = lax.all_to_all(packed, "group", split_axis=0, concat_axis=1, tiled=True)
    return (rows_back, ids_back)


def solution(mesh):
    placed = (
        P("group", None, "tp"),
        P("tp", None),
        P("tp", None),
        P("tp", "group"),
        P("tp", "group"),
        P("tp", "group", None),
        P("tp", "group", None),
        P(None, "tp", "group", None, None),
        P(None, "tp", "group", None, None),
        P("group"),
        P("group"),
        P("group", None, None),
        P("group", None),
    )
    return jax.shard_map(
        per_device,
        mesh=mesh,
        in_specs=placed,
        out_specs=(P("group", None, "tp"), P("group", None)),
        check_vma=False,
    )
```

time: 121 us -> 103 us (0.85)
  blocking collectives: 0 us -> 27.5 us
  starting transfers between devices: 72.9 us -> 47.6 us
  local copies, waits for them, and re-layouts: 12.5 us -> 0.66 us
  waiting for transfers between devices: 25.2 us -> 17.4 us
  other arithmetic: 2.76 us -> 0.04 us
  Pallas kernels: 5.51 us -> 7.86 us
    all_to_all x0 -> x1, blocking collectives: none -> 27.5 us  [per_device(): lax.all_to_all(packed, 'group', split_axis=0, concat_axis=1, tiled=True)]
    all_to_all x1 -> x0, starting transfers between devices: 27.5 us -> none  [per_device(): lax.all_to_all(packed, 'group', split_axis=0, concat_axis=1, tiled=True)]
    all_to_all x1 -> x0, waiting for transfers between devices: 11.3 us -> none  [per_device(): lax.all_to_all(packed, 'group', split_axis=0, concat_axis=1, tiled=True)]
    unnamed x28 -> x2, local copies, waits for them, and re-layouts: 9.92 us -> 0.01 us
    all_to_all x1, waiting for transfers between devices: 12.9 us -> 4.67 us  [per_device(): parts = lax.all_to_all(part, 'tp', split_axis=0, concat_axis=0, tiled=True)]
    ppermute x3, waiting for transfers between devices: 0.01 us -> 7.53 us  [per_device(): shards.append(lax.ppermute(shard, 'tp', pairs))]
    all_to_all x1, starting transfers between devices: 3.58 us -> 8.56 us  [per_device(): parts = lax.all_to_all(part, 'tp', split_axis=0, concat_axis=0, tiled=True)]
    ppermute x3, waiting for transfers between devices: 0.01 us -> 4.07 us  [per_device(): pieces[shift] = lax.ppermute(pieces[shift], 'tp', pairs)]
  transfers between devices with their start and end apart: 12 -> 10, of which waited for: 3 -> 5; matrix products, arithmetic and copies ran while one was open for 4% -> 0% of each run, Pallas kernels for 1% -> 2%
where the time goes in v3:
time: 103 us; the launch traced here: 102 us
  starting transfers between devices  47.6 us (46%)
  blocking collectives  27.5 us (27%)
  waiting for transfers between devices  17.4 us (17%)
  Pallas kernels  7.86 us (8%)
    all_to_all x1, blocking collectives, per_device(): lax.all_to_all(packed, 'group', split_axis=0, concat_axis=1, tiled=True)  27.5 us
    all_to_all x1, starting transfers between devices, per_device(): lax.all_to_all(load, 'group', split_axis=0, concat_axis=0, tiled=True, ax...  16.2 us
    ppermute x3, starting transfers between devices, per_device(): shards.append(lax.ppermute(shard, 'tp', pairs))  9.45 us
    ppermute x3, starting transfers between devices, per_device(): pieces[shift] = lax.ppermute(pieces[shift], 'tp', pairs)  9 us
    all_to_all x1, starting transfers between devices, per_device(): parts = lax.all_to_all(part, 'tp', split_axis=0, concat_axis=0, tiled=True)  8.56 us
    ppermute x3, waiting for transfers between devices, per_device(): shards.append(lax.ppermute(shard, 'tp', pairs))  7.53 us
    all_to_all x1, waiting for transfers between devices, per_device(): parts = lax.all_to_all(part, 'tp', split_axis=0, concat_axis=0, tiled=True)  4.67 us
    ppermute x3, waiting for transfers between devices, per_device(): pieces[shift] = lax.ppermute(pieces[shift], 'tp', pairs)  4.07 us
  transfers between devices with their start and end apart: 10, of which 5 were waited for; matrix products, arithmetic and copies ran while one was open for 0% of the time, Pallas kernels for 2%

profile of v3, /device:TPU:1, one launch (start us, length us, event | category | flops | bytes accessed | tf_op | source)
XLA Modules:
  0.0 101.9 jit_solution(3359599350423450498)
XLA Ops:
  0.6 1.7 %load.1 = (bf16[16,32,384]{2,1,0:T(8,128)(2,1)}, s32[1,16]{1,0:T(1,128)S(1)}) custom-call(s32[2]{0:T(128)} %counts_hbm.1, bf16[16,320]{1,0:T(8,128)(2,1)} %bitcast.10, bf16[10,1024]{1,0:T(8,128)(2,1)} %bitcast.9, f32[8,10]{1,0:T(8,128)} %bitcast.11, s32[2,1,8]{2,1,0:T(1,128)} %bitcast.13, s32[2,8]{1,0:T(2,128)} %ids_hbm.1), custom_call_target="tpu_custom_call" | custom-call | tf_op jit(solution)/shard_map/load/pallas_call | solution.py:376
  2.3 16.2 %all-to-all-start = ((bf16[16,32,384]{2,1,0:T(8,128)(2,1)}), bf16[16,32,384]{2,1,0:T(8,128)(2,1)S(1)}, u32[]{:S(2)}, u32[]{:S(2)}) async-start(bf16[16,32,384]{2,1,0:T(8,128)(2,1)} %get-tuple-element.11), calls=%async_computation | async-start | bytes 786432 | tf_op jit(solution)/shard_map/all_to_all | solution.py:403
  18.6 1.1 %pieces.1 = (bf16[320,128]{1,0:T(8,128)(2,1)S(1)}, bf16[2,4,2,16,128]{4,3,2,1,0:T(8,128)(2,1)S(1)}, bf16[2,4,2,16,128]{4,3,2,1,0:T(8,128)(2,1)S(1)}, bf16[2,4,2,...) custom-call(bf16[320,128]{1,0:T(8,128)(2,1)} %codes_hbm.1, f32[1,320]{1,0:T(1,128)} %bitcast.12, ...), custom_call_target="tpu_custom_call" | custom-call | tf_op jit(solution)/shard_map/pieces/pallas_call | solution.py:408
  19.7 2.3 %collective-permute-start = (bf16[2,4,2,16,128]{4,3,2,1,0:T(8,128)(2,1)S(1)}, bf16[2,4,2,16,128]{4,3,2,1,0:T(8,128)(2,1)S(1)}, u32[]{:S(2)}, u32[]{:S(2)}) collective-permute-start(bf16[2,4,2,16,128]{4,3,2,1,0:T(8,128)(2,1)S(1)} %get-tuple-element.13), channel_id=1, source_target_pairs={{0,4},{1,5},{2,6},{3,7},{4,8},{5,9},{6,10},{7,11},{8,12},{9,13},{1... | collective-permute-start | bytes 196616 | tf_op jit(solution)/shard_map/ppermute | solution.py:424
  22.0 2.4 %collective-permute-start.1 = (bf16[2,4,2,16,128]{4,3,2,1,0:T(8,128)(2,1)S(1)}, bf16[2,4,2,16,128]{4,3,2,1,0:T(8,128)(2,1)S(1)}, u32[]{:S(2)}, u32[]{:S(2)}) collective-permute-start(bf16[2,4,2,16,128]{4,3,2,1,0:T(8,128)(2,1)S(1)} %get-tuple-element.14), channel_id=1, source_target_pairs={{0,8},{1,9},{2,10},{3,11},{4,12},{5,13},{6,14},{7,15},{8,0},{9,1},... | collective-permute-start | bytes 196616 | tf_op jit(solution)/shard_map/ppermute | solution.py:424
  24.5 4.3 %collective-permute-start.2 = (bf16[2,4,2,16,128]{4,3,2,1,0:T(8,128)(2,1)S(1)}, bf16[2,4,2,16,128]{4,3,2,1,0:T(8,128)(2,1)S(1)}, u32[]{:S(2)}, u32[]{:S(2)}) collective-permute-start(bf16[2,4,2,16,128]{4,3,2,1,0:T(8,128)(2,1)S(1)} %get-tuple-element.15), channel_id=1, source_target_pairs={{0,12},{1,13},{2,14},{3,15},{4,0},{5,1},{6,2},{7,3},{8,4},{9,5},{1... | collective-permute-start | bytes 196616 | tf_op jit(solution)/shard_map/ppermute | solution.py:424
  28.8 4.1 %collective-permute-done.1.after2_ref.refs_2_ = bf16[2,4,2,16,128]{4,3,2,1,0:T(8,128)(2,1)S(1)} collective-permute-done((bf16[2,4,2,16,128]{4,3,2,1,0:T(8,128)(2,1)S(1)}, bf16[2,4,2,16,128]{4,3,2,1,0:T(8,128)(2,1)S(1)}, u32[]{:S(2)}, u32[]{:S(2)}) %collective-permute-start.1) | collective-permute-done | bytes 65568 | tf_op jit(solution)/shard_map/ppermute | solution.py:424
  32.8 0.0 collective-permute-done.2.after3_ref.refs_3_
  32.9 3.7 %collective-permute-start.3 = (bf16[1088,128]{1,0:T(8,128)(2,1)S(1)}, bf16[1088,128]{1,0:T(8,128)(2,1)S(1)}, u32[]{:S(2)}, u32[]{:S(2)}) collective-permute-start(bf16[1088,128]{1,0:T(8,128)(2,1)S(1)} %swap.1), channel_id=1, source_target_pairs={{0,16},{16,0},{32,48},{48,32},{64,80},{80,64},{96,112},{112,96},{1... | collective-permute-start | bytes 835592 | tf_op jit(solution)/shard_map/ppermute | solution.py:433
  36.5 1.2 %collective-permute-done.3.other_ref = bf16[1088,128]{1,0:T(8,128)(2,1)S(1)} collective-permute-done((bf16[1088,128]{1,0:T(8,128)(2,1)S(1)}, bf16[1088,128]{1,0:T(8,128)(2,1)S(1)}, u32[]{:S(2)}, u32[]{:S(2)}) %collective-permute-start.3) | collective-permute-done | bytes 278560 | tf_op jit(solution)/shard_map/ppermute | solution.py:433
  37.7 2.6 %part.1.after_ref = f32[16,16,512]{2,1,0:T(8,128)} custom-call(bf16[16,32,384]{2,1,0:T(8,128)(2,1)S(1)} %all-to-all-done.came_ref, bf16[1088,128]{1,0:T(8,128)(2,1)S(1)} %collective-permute-done.3.other_ref, bf16[320,128]{1,0:T(8,128)(2,1)S(1)} %get-tuple-element.12.query_ref.delta_ref, bf16[320,4096]{1,0:T(8,128)(2,1)} %query_hbm.1, bf16[320,1024]{1,0:T(8,128)(2,1)} %pair_hbm.1), custom_call_target="tpu_custom_call" | custom-call | tf_op jit(solution)/shard_map/part/pallas_call | solution.py:435
  40.3 0.0 copy-start
  40.4 8.6 %all-to-all-start.1 = ((f32[16,16,512]{2,1,0:T(8,128)}), f32[16,16,512]{2,1,0:T(8,128)S(1)}, u32[]{:S(2)}, u32[]{:S(2)}) async-start(f32[16,16,512]{2,1,0:T(8,128)} %part.1.after_ref), calls=%async_computation.1 | async-start | bytes 1048576 | tf_op jit(solution)/shard_map/all_to_all | solution.py:449
  49.0 4.5 %collective-permute-start.7 = (bf16[4,2,4,2,16,128]{5,4,3,2,1,0:T(8,128)(2,1)S(1)}, bf16[4,2,4,2,16,128]{5,4,3,2,1,0:T(8,128)(2,1)S(1)}, u32[]{:S(2)}, u32[]{:S(2)}) collective-permute-start(bf16[4,2,4,2,16,128]{5,4,3,2,1,0:T(8,128)(2,1)S(1)} %join.1.shard0_ref), channel_id=1, source_target_pairs={{0,3},{1,0},{2,1},{3,2},{4,7},{5,4},{6,5},{7,6},{8,11},{9,8},{10,9... | collective-permute-start | bytes 786440 | tf_op jit(solution)/shard_map/ppermute | solution.py:462
  53.4 2.5 %collective-permute-start.6 = (bf16[4,2,4,2,16,128]{5,4,3,2,1,0:T(8,128)(2,1)S(1)}, bf16[4,2,4,2,16,128]{5,4,3,2,1,0:T(8,128)(2,1)S(1)}, u32[]{:S(2)}, u32[]{:S(2)}) collective-permute-start(bf16[4,2,4,2,16,128]{5,4,3,2,1,0:T(8,128)(2,1)S(1)} %join.1.shard0_ref), channel_id=1, source_target_pairs={{0,2},{1,3},{2,0},{3,1},{4,6},{5,7},{6,4},{7,5},{8,10},{9,11},{10,... | collective-permute-start | bytes 786440 | tf_op jit(solution)/shard_map/ppermute | solution.py:462
  55.9 2.5 %collective-permute-start.5 = (bf16[4,2,4,2,16,128]{5,4,3,2,1,0:T(8,128)(2,1)S(1)}, bf16[4,2,4,2,16,128]{5,4,3,2,1,0:T(8,128)(2,1)S(1)}, u32[]{:S(2)}, u32[]{:S(2)}) collective-permute-start(bf16[4,2,4,2,16,128]{5,4,3,2,1,0:T(8,128)(2,1)S(1)} %join.1.shard0_ref), channel_id=1, source_target_pairs={{0,1},{1,2},{2,3},{3,0},{4,5},{5,6},{6,7},{7,4},{8,9},{9,10},{10,1... | collective-permute-start | bytes 786440 | tf_op jit(solution)/shard_map/ppermute | solution.py:462
  58.4 4.7 %all-to-all-done.1.after_ref = f32[16,16,512]{2,1,0:T(8,128)S(1)} async-done(((f32[16,16,512]{2,1,0:T(8,128)}), f32[16,16,512]{2,1,0:T(8,128)S(1)}, u32[]{:S(2)}, u32[]{:S(2)}) %all-to-all-start.1) | async-done | bytes 524320 | tf_op jit(solution)/shard_map/all_to_all | solution.py:449
  63.1 0.7 collective-permute-start.4
  63.8 0.9 facts.1
  64.7 0.6 collective-permute-done.6.shard2_ref
  65.3 7.0 %collective-permute-done.5.shard1_ref = bf16[4,2,4,2,16,128]{5,4,3,2,1,0:T(8,128)(2,1)S(1)} collective-permute-done((bf16[4,2,4,2,16,128]{5,4,3,2,1,0:T(8,128)(2,1)S(1)}, bf16[4,2,4,2,16,128]{5,4,3,2,1,0:T(8,128)(2,1)S(1)}, u32[]{:S(2)}, u32[]{:S(2)}) %collective-permute-start.5) | collective-permute-done | bytes 262176 | tf_op jit(solution)/shard_map/ppermute | solution.py:462
  72.3 1.4 %attend.1 = bf16[64,256]{1,0:T(8,128)(2,1)S(1)} custom-call(s32[2]{0:T(128)S(1)} %copy-done, bf16[16,512]{1,0:T(8,128)(2,1)S(1)} %collective-permute-done.4.mine_ref, bf16[64,16]{1,0:T(8,128)(2,1)S(1)} %get-tuple-element.17.placed_ref, bf16[4,2,4,2,16,128]{5,4,3,2,1,0:T(8,128)(2,1)S(1)} %join.1.shard0_ref, ...), custom_call_target="tpu_custom_call" | custom-call | tf_op jit(solution)/shard_map/attend/pallas_call | solution.py:478
  73.7 27.5 %all_to_all.22 = bf16[32,2,256]{2,1,0:T(2,128)(2,1)S(1)} all-to-all(bf16[32,2,256]{2,1,0:T(2,128)(2,1)S(1)} %reshape.14), channel_id=1, replica_groups=mesh['group'=32,'tp'=16] {'group'}, dimensions={0} | all-to-all | bytes 65536 | tf_op jit(solution)/shard_map/all_to_all | solution.py:487
  101.2 0.6 all_to_all.18
  (9 shorter events, 0.1 us)
Async XLA Ops:
  2.3 30.5 %all-to-all-start = ((bf16[16,32,384]{2,1,0:T(8,128)(2,1)}), bf16[16,32,384]{2,1,0:T(8,128)(2,1)S(1)}, u32[]{:S(2)}, u32[]{:S(2)}) async-start(bf16[16,32,384]{2,1,0:T(8,128)(2,1)} %get-tuple-element.11), calls=%async_computation | async-start | bytes 786432 | tf_op jit(solution)/shard_map/all_to_all | solution.py:403
  19.7 9.0 %collective-permute-start = (bf16[2,4,2,16,128]{4,3,2,1,0:T(8,128)(2,1)S(1)}, bf16[2,4,2,16,128]{4,3,2,1,0:T(8,128)(2,1)S(1)}, u32[]{:S(2)}, u32[]{:S(2)}) collective-permute-start(bf16[2,4,2,16,128]{4,3,2,1,0:T(8,128)(2,1)S(1)} %get-tuple-element.13), channel_id=1, source_target_pairs={{0,4},{1,5},{2,6},{3,7},{4,8},{5,9},{6,10},{7,11},{8,12},{9,13},{1... | collective-permute-start | bytes 196616 | tf_op jit(solution)/shard_map/ppermute | solution.py:424
  22.0 10.8 %collective-permute-start.1 = (bf16[2,4,2,16,128]{4,3,2,1,0:T(8,128)(2,1)S(1)}, bf16[2,4,2,16,128]{4,3,2,1,0:T(8,128)(2,1)S(1)}, u32[]{:S(2)}, u32[]{:S(2)}) collective-permute-start(bf16[2,4,2,16,128]{4,3,2,1,0:T(8,128)(2,1)S(1)} %get-tuple-element.14), channel_id=1, source_target_pairs={{0,8},{1,9},{2,10},{3,11},{4,12},{5,13},{6,14},{7,15},{8,0},{9,1},... | collective-permute-start | bytes 196616 | tf_op jit(solution)/shard_map/ppermute | solution.py:424
  24.5 8.4 %collective-permute-start.2 = (bf16[2,4,2,16,128]{4,3,2,1,0:T(8,128)(2,1)S(1)}, bf16[2,4,2,16,128]{4,3,2,1,0:T(8,128)(2,1)S(1)}, u32[]{:S(2)}, u32[]{:S(2)}) collective-permute-start(bf16[2,4,2,16,128]{4,3,2,1,0:T(8,128)(2,1)S(1)} %get-tuple-element.15), channel_id=1, source_target_pairs={{0,12},{1,13},{2,14},{3,15},{4,0},{5,1},{6,2},{7,3},{8,4},{9,5},{1... | collective-permute-start | bytes 196616 | tf_op jit(solution)/shard_map/ppermute | solution.py:424
  32.9 4.8 %collective-permute-start.3 = (bf16[1088,128]{1,0:T(8,128)(2,1)S(1)}, bf16[1088,128]{1,0:T(8,128)(2,1)S(1)}, u32[]{:S(2)}, u32[]{:S(2)}) collective-permute-start(bf16[1088,128]{1,0:T(8,128)(2,1)S(1)} %swap.1), channel_id=1, source_target_pairs={{0,16},{16,0},{32,48},{48,32},{64,80},{80,64},{96,112},{112,96},{1... | collective-permute-start | bytes 835592 | tf_op jit(solution)/shard_map/ppermute | solution.py:433
  40.3 31.9 %copy-start = (s32[2]{0:T(128)S(1)}, s32[2]{0:T(128)}, u32[]{:S(2)}) copy-start(s32[2]{0:T(128)} %lengths_ref.1) | copy-start | bytes 28
  40.4 22.7 %all-to-all-start.1 = ((f32[16,16,512]{2,1,0:T(8,128)}), f32[16,16,512]{2,1,0:T(8,128)S(1)}, u32[]{:S(2)}, u32[]{:S(2)}) async-start(f32[16,16,512]{2,1,0:T(8,128)} %part.1.after_ref), calls=%async_computation.1 | async-start | bytes 1048576 | tf_op jit(solution)/shard_map/all_to_all | solution.py:449
  49.0 15.8 %collective-permute-start.7 = (bf16[4,2,4,2,16,128]{5,4,3,2,1,0:T(8,128)(2,1)S(1)}, bf16[4,2,4,2,16,128]{5,4,3,2,1,0:T(8,128)(2,1)S(1)}, u32[]{:S(2)}, u32[]{:S(2)}) collective-permute-start(bf16[4,2,4,2,16,128]{5,4,3,2,1,0:T(8,128)(2,1)S(1)} %join.1.shard0_ref), channel_id=1, source_target_pairs={{0,3},{1,0},{2,1},{3,2},{4,7},{5,4},{6,5},{7,6},{8,11},{9,8},{10,9... | collective-permute-start | bytes 786440 | tf_op jit(solution)/shard_map/ppermute | solution.py:462
  53.4 11.9 %collective-permute-start.6 = (bf16[4,2,4,2,16,128]{5,4,3,2,1,0:T(8,128)(2,1)S(1)}, bf16[4,2,4,2,16,128]{5,4,3,2,1,0:T(8,128)(2,1)S(1)}, u32[]{:S(2)}, u32[]{:S(2)}) collective-permute-start(bf16[4,2,4,2,16,128]{5,4,3,2,1,0:T(8,128)(2,1)S(1)} %join.1.shard0_ref), channel_id=1, source_target_pairs={{0,2},{1,3},{2,0},{3,1},{4,6},{5,7},{6,4},{7,5},{8,10},{9,11},{10,... | collective-permute-start | bytes 786440 | tf_op jit(solution)/shard_map/ppermute | solution.py:462
  55.9 16.3 %collective-permute-start.5 = (bf16[4,2,4,2,16,128]{5,4,3,2,1,0:T(8,128)(2,1)S(1)}, bf16[4,2,4,2,16,128]{5,4,3,2,1,0:T(8,128)(2,1)S(1)}, u32[]{:S(2)}, u32[]{:S(2)}) collective-permute-start(bf16[4,2,4,2,16,128]{5,4,3,2,1,0:T(8,128)(2,1)S(1)} %join.1.shard0_ref), channel_id=1, source_target_pairs={{0,1},{1,2},{2,3},{3,0},{4,5},{5,6},{6,7},{7,4},{8,9},{9,10},{10,1... | collective-permute-start | bytes 786440 | tf_op jit(solution)/shard_map/ppermute | solution.py:462
  63.1 9.1 %collective-permute-start.4 = (bf16[16,512]{1,0:T(8,128)(2,1)S(1)}, bf16[16,512]{1,0:T(8,128)(2,1)S(1)}, u32[]{:S(2)}, u32[]{:S(2)}) collective-permute-start(bf16[16,512]{1,0:T(8,128)(2,1)S(1)} %reduce_sum.9), channel_id=1, source_target_pairs={{0,0},{1,32},{2,64},{3,96},{4,128},{5,160},{6,192},{7,224},{8,256}... | collective-permute-start | bytes 49160 | tf_op jit(solution)/shard_map/ppermute | solution.py:464

commit v4 on v3

v4 whole, which is shorter than its diff:
```python
import math

import jax
import jax.numpy as jnp
from jax import lax
from jax.experimental import pallas as pl
from jax.experimental.pallas import tpu as pltpu
from jax.sharding import PartitionSpec as P

HEADS = 32
KV_HEADS = 4
HEAD = 128
CORES = 2
SIDES = 2
LANES = 128


NEG_FILL = -1e30

VMEM = pl.BlockSpec(memory_space=pltpu.VMEM)
SMEM = pl.BlockSpec(memory_space=pltpu.SMEM)
HBM = pl.BlockSpec(memory_space=pltpu.HBM)
ANY = pl.BlockSpec(memory_space=pl.ANY)
PARAMS = pltpu.CompilerParams(vmem_limit_bytes=24 * 1024 * 1024)


def column(row):
    n = row.shape[1]
    across = lax.broadcasted_iota(jnp.int32, (n, n), 1)
    down = lax.broadcasted_iota(jnp.int32, (n, n), 0)
    return jnp.sum(jnp.where(across == down, row, jnp.zeros_like(row)), axis=1, keepdims=True)


def fetch(pairs, sems):
    copies = [
        pltpu.make_async_copy(source, target, sems.at[i]) for i, (source, target) in enumerate(pairs)
    ]
    for copy in copies:
        copy.start()
    return copies


def load_kernel(
    counts_hbm,
    hidden_hbm,
    codes_hbm,
    scales_hbm,
    learner_hbm,
    ids_hbm,
    load_ref,
    named_ref,
    counts_ref,
    hidden_ref,
    codes_ref,
    scales_ref,
    learner_ref,
    ids_ref,
    sems,
):
    copies = fetch(
        [
            (codes_hbm, codes_ref),
            (scales_hbm, scales_ref),
            (hidden_hbm, hidden_ref),
            (counts_hbm, counts_ref),
            (learner_hbm, learner_ref),
            (ids_hbm, ids_ref),
        ],
        sems,
    )
    peers = load_ref.shape[0]
    games, steps, features = hidden_ref.shape
    for copy in copies:
        copy.wait()
    inputs = jnp.concatenate(
        [hidden_ref[game].astype(jnp.float32) for game in range(games)], axis=1
    ).astype(jnp.bfloat16)
    load_ref[:, :, : games * features] = jnp.broadcast_to(inputs, (peers,) + inputs.shape)
    step = lax.broadcasted_iota(jnp.int32, (1, steps), 1)
    named = [
        jnp.where(step < counts_ref[game], learner_ref[game], -1) for game in range(games)
    ]
    named = jnp.concatenate(named, axis=1)
    named_ref[...] = named
    ids = jnp.concatenate([ids_ref[game : game + 1] for game in range(games)], axis=1)
    facts = jnp.concatenate([ids >> 12, (ids >> 6) & 63, ids & 63, named], axis=0)
    facts = jnp.concatenate(
        [facts.astype(jnp.float32), jnp.zeros((4, LANES - games * steps), jnp.float32)], axis=1
    )
    extra = codes_ref.shape[0] - steps
    blank = jnp.zeros((steps - 4 - extra, LANES), jnp.float32)
    for block in range(2 * KV_HEADS):
        scale = column(scales_ref[block : block + 1, :])
        delta = codes_ref[:, block * HEAD : (block + 1) * HEAD].astype(jnp.float32) * scale
        rest = jnp.concatenate([delta[steps:], blank, facts], axis=0)
        cell = jnp.concatenate([delta[:steps], rest], axis=1).astype(jnp.bfloat16)
        head, part = block % KV_HEADS, block // KV_HEADS
        for peer in range(part, peers, CORES):
            if peer * KV_HEADS // peers == head:
                load_ref[peer, :, games * features :] = cell


def pieces_kernel(
    codes_hbm,
    scales_hbm,
    key_hbm,
    value_hbm,
    delta_ref,
    piece0_ref,
    piece1_ref,
    piece2_ref,
    piece3_ref,
    codes_ref,
    scales_ref,
    sems,
    piece_sems,
):
    copies = fetch([(codes_hbm, codes_ref), (scales_hbm, scales_ref)], sems)
    own = lax.axis_index("tp") // (lax.axis_size("tp") // KV_HEADS)
    moves = []
    for shift, piece_ref in enumerate((piece0_ref, piece1_ref, piece2_ref, piece3_ref)):
        head = own ^ shift
        lanes = pl.ds(pl.multiple_of(head * HEAD, HEAD), HEAD)
        for part, cache_hbm in enumerate((key_hbm, value_hbm)):
            moves.append((cache_hbm.at[:, 0, :, :, lanes], piece_ref.at[part]))
    moves = fetch(moves, piece_sems)
    for copy in copies:
        copy.wait()
    scale = column(scales_ref[...])
    delta_ref[...] = (codes_ref[...].astype(jnp.float32) * scale).astype(jnp.bfloat16)
    for copy in moves:
        copy.wait()


def cells_of(came_ref, start, size):
    peers, steps, _ = came_ref.shape
    cell = came_ref[:, :, start : start + size].astype(jnp.float32)
    return cell.reshape(peers * steps, size).astype(jnp.bfloat16)


def swap_kernel(came_ref, after1_ref, after2_ref, after3_ref, out_ref):
    _, block, lanes = out_ref.shape
    width = came_ref.shape[2]
    for i in range(2):
        out_ref[i] = cells_of(came_ref, width - (2 - i) * lanes, lanes)


def dot(a, b):
    return jnp.dot(a, b, preferred_element_type=jnp.float32)


def part_kernel(
    came_ref,
    mine_ref,
    other_ref,
    query_hbm,
    pair_hbm,
    queries_ref,
    pairs_ref,
    spread_ref,
    weight_ref,
    sems,
):
    peers, steps, width = came_ref.shape
    features = weight_ref.shape[1]
    rows = queries_ref.shape[1]
    games = rows // steps
    block = peers * steps
    group_index = lax.axis_index("group")
    level = group_index // (SIDES * CORES)
    side, core = lax.rem(group_index // CORES, SIDES), lax.rem(group_index, CORES)
    head = level * KV_HEADS // (peers // CORES)
    pair_rows = features // (peers * SIDES)

    def columns(source, index):
        return source.at[:, pl.ds(pl.multiple_of(index * HEAD, HEAD), HEAD)]

    copies = fetch(
        [
            (columns(query_hbm, (level * SIDES + 0) * CORES + core), weight_ref.at[0]),
            (columns(query_hbm, (level * SIDES + 1) * CORES + core), weight_ref.at[1]),
            (columns(pair_hbm, core * KV_HEADS + head), weight_ref.at[2]),
        ],
        sems,
    )
    inputs = jnp.concatenate(
        [cells_of(came_ref, game * features, features) for game in range(games)], axis=0
    )
    spot = lax.broadcasted_iota(jnp.int32, (1, 2 * block), 1)
    feature = lax.broadcasted_iota(jnp.int32, (features, 2 * block), 0)
    peer, step = spot % block // steps, spot % steps
    offset = jnp.where(spot < block, step, step + steps)
    spreads = []
    for turn in range(SIDES):
        owner = (peer // CORES * SIDES + (side ^ turn)) * CORES + peer % CORES
        source = jnp.where(offset < pair_rows, owner * pair_rows + offset, -1)
        spread = (feature == source).astype(jnp.float32).astype(jnp.bfloat16)
        spreads.append(dot(inputs, spread).astype(jnp.bfloat16))
    spread_ref[...] = spreads[1]
    pairs = dot(spreads[0][:, :block], cells_of(came_ref, width - 2 * LANES, LANES))
    pairs = pairs + dot(spreads[0][:, block:], cells_of(came_ref, width - LANES, LANES))
    mine, other = mine_ref[...], other_ref[...]
    first = dot(inputs, jnp.where(side == 0, mine, other))
    second = dot(inputs, jnp.where(side == 0, other, mine))
    for copy in copies:
        copy.wait()

    def put(ref, i, sums):
        for game in range(games):
            ref[:, game * steps : (game + 1) * steps, i * HEAD : (i + 1) * HEAD] = sums[
                game * block : (game + 1) * block
            ].reshape(peers, steps, HEAD)

    put(queries_ref, 0, first + dot(inputs, weight_ref[0]))
    put(queries_ref, 1, second + dot(inputs, weight_ref[1]))
    put(pairs_ref, 0, pairs + dot(inputs, weight_ref[2]))


def whole_kernel(queries_ref, pairs_ref, spread_ref, other_ref, after_ref, part_ref):
    peers, rows, wide = queries_ref.shape
    block = spread_ref.shape[1] // 2
    games = spread_ref.shape[0] // block
    steps = rows // games
    part_ref[:, :, :wide] = queries_ref[...]
    pairs = dot(spread_ref[:, :block], other_ref[0]) + dot(spread_ref[:, block:], other_ref[1])
    for game in range(games):
        band = slice(game * steps, (game + 1) * steps)
        part_ref[:, band, wide:] = pairs_ref[:, band, :] + pairs[
            game * block : (game + 1) * block
        ].reshape(peers, steps, HEAD)


def sum_kernel(parts_ref, keep_ref, give_ref):
    core = lax.rem(lax.axis_index("group"), CORES)
    sums = jnp.sum(parts_ref[...], axis=0)
    heads = [sums[:, i * HEAD : (i + 1) * HEAD] for i in range(3)]
    keep_ref[:, :HEAD] = jnp.where(core == 0, heads[0], heads[1]).astype(jnp.bfloat16)
    give_ref[:, :HEAD] = jnp.where(core == 0, heads[1], heads[0]).astype(jnp.bfloat16)
    keep_ref[:, HEAD:] = heads[2].astype(jnp.bfloat16)
    give_ref[:, HEAD:] = heads[2].astype(jnp.bfloat16)


def join_kernel(after_ref, *refs):
    shard_ref = refs[-1]
    for shift, piece_ref in enumerate(refs[:-1]):
        shard_ref[shift] = piece_ref[...]


def facts_kernel(after_ref, named_ref, came_ref, other_ref, placed_ref, ids_ref):
    peers, steps, width = came_ref.shape
    slots, rows = placed_ref.shape
    group_index = lax.axis_index("group")
    side = lax.rem(group_index // CORES, SIDES)
    capacity = slots // (peers * SIDES)

    named = named_ref[...].astype(jnp.float32)
    before = lax.broadcasted_iota(jnp.int32, (rows, rows), 0) < lax.broadcasted_iota(
        jnp.int32, (rows, rows), 1
    )
    rank = jnp.sum(jnp.where((column(named) == named) & before, 1.0, 0.0), axis=0, keepdims=True)
    slot = jnp.where(named >= 0, named * capacity + rank, -1.0)
    index = lax.broadcasted_iota(jnp.int32, (slots, rows), 0).astype(jnp.float32)
    placed_ref[...] = jnp.where(index == slot, 1.0, 0.0).astype(jnp.bfloat16)

    own = came_ref[:, :, width - LANES :].astype(jnp.float32)
    other = other_ref[1].astype(jnp.float32).reshape(own.shape)
    kind = lax.broadcasted_iota(jnp.int32, own.shape, 1) - (steps - 4)
    lane = lax.broadcasted_iota(jnp.int32, (peers, LANES), 1)
    out_lane = lax.broadcasted_iota(jnp.int32, (peers, slots), 1)
    out_peer = lax.broadcasted_iota(jnp.int32, (peers, slots), 0)
    ids = jnp.zeros((peers, slots), jnp.float32)
    for turn, facts in enumerate((own, other)):

        def pick(i):
            return jnp.sum(jnp.where(kind == i, facts, 0.0), axis=1)

        number = pick(0) * 4096.0 + pick(1) * 64.0 + pick(2)
        hit = (pick(3) == group_index.astype(jnp.float32)) & (lane < rows)
        coded = lane.astype(jnp.float32) * 262144.0 + number
        low = jnp.min(jnp.where(hit, coded, 1e9), axis=1, keepdims=True)
        high = jnp.max(jnp.where(hit, coded, -1.0), axis=1, keepdims=True)
        sender = (out_peer // CORES * SIDES + (side ^ turn)) * CORES + out_peer % CORES
        for k, (coded, there) in enumerate(((low, high >= 0), (high, high > low))):
            number = (coded.astype(jnp.int32) & 262143).astype(jnp.float32)
            value = jnp.where(there, number, -1.0)
            ids = ids + jnp.where(out_lane == sender * capacity + k, value, 0.0)
    ids_ref[...] = jnp.sum(ids, axis=0, keepdims=True).astype(jnp.int32)


def attend_kernel(
    lengths_ref,
    mine_ref,
    placed_ref,
    shard0_ref,
    shard1_ref,
    shard2_ref,
    shard3_ref,
    packed_ref,
):
    shards = (shard0_ref, shard1_ref, shard2_ref, shard3_ref)
    count, _, rounds, games, block, _ = shard0_ref.shape
    rows = mine_ref.shape[0]
    steps = rows // games
    heads = CORES
    n_tp = count * len(shards)
    factor = 1.0 / math.sqrt(HEAD)
    mine = mine_ref[...].astype(jnp.float32)
    first, second = mine[:, : 2 * HEAD], mine[:, 2 * HEAD :]
    even = lax.rem(lax.axis_index("tp"), 2) == 0
    with_keys, with_values = jnp.where(even, first, second), jnp.where(even, second, first)
    spot = lax.broadcasted_iota(jnp.int32, (1, count * rounds * block), 1)
    tp_index = lax.axis_index("tp")
    positions = []
    for shift in range(len(shards)):
        across = lax.rem(tp_index, len(shards)) ^ shift
        down = (tp_index // len(shards)) ^ (spot // (rounds * block))
        tp = down * len(shards) + across
        positions.append((spot // block % rounds * n_tp + tp) * block + spot % block)
    contract = (((1,), (1,)), ((), ()))
    games_out = []
    for game in range(games):
        bands = [x[game * steps : (game + 1) * steps] for x in (with_keys, with_values)]
        queries = jnp.concatenate([band[:, :HEAD] for band in bands], axis=0).astype(jnp.bfloat16)
        new_keys, new_values = [band[:, HEAD:].astype(jnp.bfloat16) for band in bands]
        new_scores = factor * lax.dot_general(
            queries, new_keys, contract, preferred_element_type=jnp.float32
        )
        later = lax.broadcasted_iota(jnp.int32, new_scores.shape, 1)
        step = lax.broadcasted_iota(jnp.int32, new_scores.shape, 0) % steps
        new_valid = later <= step
        top = jnp.max(jnp.where(new_valid, new_scores, NEG_FILL), axis=1, keepdims=True)
        kept = []
        for shard_ref, position in zip(shards, positions):
            keys = shard_ref[:, 0, :, game].reshape(count * rounds * block, HEAD)
            scores = factor * lax.dot_general(
                queries, keys, contract, preferred_element_type=jnp.float32
            )
            scores = jnp.where(position < lengths_ref[game], scores, NEG_FILL)
            top = jnp.maximum(top, jnp.max(scores, axis=1, keepdims=True))
            kept.append(scores)
        weight = jnp.where(new_valid, jnp.exp(new_scores - top), 0.0).astype(jnp.bfloat16)
        total = jnp.sum(weight.astype(jnp.float32), axis=1, keepdims=True)
        mixed = jnp.dot(weight, new_values, preferred_element_type=jnp.float32)
        for shard_ref, position, scores in zip(shards, positions, kept):
            values = shard_ref[:, 1, :, game].reshape(count * rounds * block, HEAD)
            weight = jnp.where(
                position < lengths_ref[game], jnp.exp(scores - top), 0.0
            ).astype(jnp.bfloat16)
            total = total + jnp.sum(weight.astype(jnp.float32), axis=1, keepdims=True)
            mixed = mixed + jnp.dot(weight, values, preferred_element_type=jnp.float32)
        out = mixed / total
        games_out.append(
            jnp.concatenate([out[h * steps : (h + 1) * steps] for h in range(heads)], axis=1)
        )
    attended = jnp.concatenate(games_out, axis=0).astype(jnp.bfloat16)
    packed_ref[...] = jnp.dot(
        placed_ref[...], attended, preferred_element_type=jnp.float32
    ).astype(jnp.bfloat16)


def per_device(
    hidden,
    query_weight,
    key_value_weight,
    query_codes,
    query_scales,
    key_value_codes,
    key_value_scales,
    key_cache,
    value_cache,
    lengths,
    counts,
    learner,
    token_ids,
):
    games, steps, features = hidden.shape
    rows = games * steps
    n_group = lax.axis_size("group")
    n_tp = lax.axis_size("tp")
    peers = n_group // SIDES
    across = n_tp // KV_HEADS
    near = [
        [g for g in range(n_group) if g // CORES % SIDES == side] for side in range(SIDES)
    ]
    turn = []
    for g in range(n_group):
        level, side, core = g // (SIDES * CORES), g // CORES % SIDES, g % CORES
        for t in range(n_tp):
            to = (t // CORES * SIDES + side) * CORES + t % CORES
            turn.append((g * n_tp + t, to * n_tp + level * CORES + core))
    wide = HEADS // n_tp * HEAD
    capacity = max(2, 2 * rows // n_group)
    rounds, _, _, block, _ = key_cache.shape
    pair_rows = key_value_codes.shape[1]
    bf16 = jnp.bfloat16

    def far(x):
        return pltpu.with_memory_space_constraint(x, pltpu.HBM)


    def along(x, axis, shift):
        return lax.ppermute(x, axis, [(i, i ^ shift) for i in range(lax.axis_size(axis))])

    load, named = pl.pallas_call(
        load_kernel,
        out_shape=[
            jax.ShapeDtypeStruct((peers, steps, games * features + 2 * LANES), bf16),
            jax.ShapeDtypeStruct((1, rows), jnp.int32),
        ],
        in_specs=[HBM] * 6,
        out_specs=[VMEM] * 2,
        scratch_shapes=[
            pltpu.SMEM((games,), jnp.int32),
            pltpu.VMEM(hidden.shape, bf16),
            pltpu.VMEM((pair_rows, 2 * KV_HEADS * HEAD), bf16),
            pltpu.VMEM((2 * KV_HEADS, pair_rows), jnp.float32),
            pltpu.VMEM((games, 1, steps), jnp.int32),
            pltpu.VMEM((games, steps), jnp.int32),
            pltpu.SemaphoreType.DMA((6,)),
        ],
        compiler_params=PARAMS,
        name="load",
    )(
        far(counts),
        far(hidden),
        far(key_value_codes[0]),
        far(key_value_scales[0].T),
        far(learner.transpose(0, 2, 1)),
        far(token_ids),
    )
    came = lax.all_to_all(
        load, "group", split_axis=0, concat_axis=0, tiled=True, axis_index_groups=near
    )

    piece = jax.ShapeDtypeStruct((2, rounds, games, block, HEAD), bf16)
    query_delta, *pieces = pl.pallas_call(
        pieces_kernel,
        out_shape=[jax.ShapeDtypeStruct(query_codes.shape, bf16)] + [piece] * KV_HEADS,
        in_specs=[HBM] * 4,
        out_specs=[VMEM] * (1 + KV_HEADS),
        scratch_shapes=[
            pltpu.VMEM(query_codes.shape, bf16),
            pltpu.VMEM((1, features), jnp.float32),
            pltpu.SemaphoreType.DMA((2,)),
            pltpu.SemaphoreType.DMA((2 * KV_HEADS,)),
        ],
        compiler_params=PARAMS,
        name="pieces",
    )(far(query_codes), far(query_scales.T), far(key_cache), far(value_cache))
    for shift in range(1, KV_HEADS):
        pieces[shift] = along(pieces[shift], "tp", shift * across)
    query_other = along(query_delta, "group", CORES)
    rows_all = peers * steps
    other = pl.pallas_call(
        swap_kernel,
        out_shape=jax.ShapeDtypeStruct((2, rows_all, LANES), bf16),
        in_specs=[VMEM] + [ANY] * (KV_HEADS - 1),
        out_specs=VMEM,
        compiler_params=PARAMS,
        name="swap",
    )(came, *pieces[1:])
    other = along(other, "group", CORES)

    queries, pairs, spread = pl.pallas_call(
        part_kernel,
        out_shape=[
            jax.ShapeDtypeStruct((peers, rows, wide), jnp.float32),
            jax.ShapeDtypeStruct((peers, rows, HEAD), jnp.float32),
            jax.ShapeDtypeStruct((games * rows_all, 2 * rows_all), bf16),
        ],
        in_specs=[VMEM] * 3 + [HBM] * 2,
        out_specs=[VMEM] * 3,
        scratch_shapes=[
            pltpu.VMEM((3, features, HEAD), bf16),
            pltpu.SemaphoreType.DMA((3,)),
        ],
        compiler_params=PARAMS,
        name="part",
    )(came, query_delta, query_other, far(query_weight), far(key_value_weight))
    part = pl.pallas_call(
        whole_kernel,
        out_shape=jax.ShapeDtypeStruct((peers, rows, wide + HEAD), jnp.float32),
        in_specs=[VMEM] * 4 + [ANY],
        out_specs=VMEM,
        compiler_params=PARAMS,
        name="whole",
    )(queries, pairs, spread, other, pieces[1])
    parts = lax.all_to_all(part, "tp", split_axis=0, concat_axis=0, tiled=True)

    shard = pl.pallas_call(
        join_kernel,
        out_shape=jax.ShapeDtypeStruct((KV_HEADS,) + piece.shape, bf16),
        in_specs=[ANY] + [VMEM] * KV_HEADS,
        out_specs=VMEM,
        compiler_params=PARAMS,
        name="join",
    )(part, *pieces)
    shards = [shard]
    for shift in range(1, across):
        shards.append(along(shard, "tp", shift))
    keep, give = pl.pallas_call(
        sum_kernel,
        out_shape=[jax.ShapeDtypeStruct((rows, 2 * HEAD), bf16)] * 2,
        in_specs=[VMEM],
        out_specs=[VMEM] * 2,
        compiler_params=PARAMS,
        name="sum",
    )(parts)
    got = along(give, "group", 1)
    mine = lax.ppermute(jnp.concatenate([keep, got], axis=1), ("group", "tp"), turn)

    placed, ids_back = pl.pallas_call(
        facts_kernel,
        out_shape=[
            jax.ShapeDtypeStruct((n_group * capacity, rows), bf16),
            jax.ShapeDtypeStruct((1, n_group * capacity), jnp.int32),
        ],
        in_specs=[ANY] + [VMEM] * 3,
        out_specs=[VMEM] * 2,
        compiler_params=PARAMS,
        name="facts",
    )(parts, named, came, other)

    packed = pl.pallas_call(
        attend_kernel,
        out_shape=jax.ShapeDtypeStruct((n_group * capacity, wide), bf16),
        in_specs=[SMEM] + [VMEM] * 6,
        out_specs=VMEM,
        compiler_params=PARAMS,
        name="attend",
    )(lengths, mine, placed, *shards)
    packed = packed.reshape(n_group, capacity, wide)
    rows_back = lax.all_to_all(packed, "group", split_axis=0, concat_axis=1, tiled=True)
    return (rows_back, ids_back)


def solution(mesh):
    placed = (
        P("group", None, "tp"),
        P("tp", None),
        P("tp", None),
        P("tp", "group"),
        P("tp", "group"),
        P("tp", "group", None),
        P("tp", "group", None),
        P(None, "tp", "group", None, None),
        P(None, "tp", "group", None, None),
        P("group"),
        P("group"),
        P("group", None, None),
        P("group", None),
    )
    return jax.shard_map(
        per_device,
        mesh=mesh,
        in_specs=placed,
        out_specs=(P("group", None, "tp"), P("group", None)),
        check_vma=False,
    )
```

time: 103 us -> 100 us (0.971)
  waiting for transfers between devices: 17.4 us -> 8.68 us
  starting transfers between devices: 47.6 us -> 52.9 us
  blocking collectives: 27.5 us -> 28.7 us
    ppermute x8 -> x10, starting transfers between devices: 22.8 us -> 36.7 us  [the longest x9 34.3 us: along(): lax.ppermute(x, axis, [(i, i ^ shift) for i in range(lax.axis_size(axis))])]
    ppermute x8 -> x10, waiting for transfers between devices: 12.8 us -> 7.68 us  [the longest x9 5.83 us: along(): lax.ppermute(x, axis, [(i, i ^ shift) for i in range(lax.axis_size(axis))])]
    all_to_all x1, starting transfers between devices: 16.2 us -> 11.8 us  [per_device(): lax.all_to_all(load, 'group', split_axis=0, concat_axis=0, tiled=True, ax...]
    all_to_all x1, starting transfers between devices: 8.56 us -> 4.33 us  [per_device(): parts = lax.all_to_all(part, 'tp', split_axis=0, concat_axis=0, tiled=True)]
    all_to_all x1, waiting for transfers between devices: 4.67 us -> 1 us  [per_device(): parts = lax.all_to_all(part, 'tp', split_axis=0, concat_axis=0, tiled=True)]
    all_to_all x1, blocking collectives: 27.5 us -> 28.7 us  [per_device(): lax.all_to_all(packed, 'group', split_axis=0, concat_axis=1, tiled=True)]
    pallas_call x3 -> x5, Pallas kernels: 4.37 us -> 4.35 us  [the longest x1 1.73 us: per_device(): pl.pallas_call(part_kernel, out_shape=[jax.ShapeDtypeStruct((peers, rows,...]
  transfers between devices with their start and end apart: 10 -> 12, of which waited for: 5 -> 4; matrix products, arithmetic and copies ran while one was open for 0% -> 0% of each run, Pallas kernels for 2% -> 4%
where the time goes in v4:
time: 100 us; the launch traced here: 99.5 us
  starting transfers between devices  52.9 us (53%)
  blocking collectives  28.7 us (29%)
  waiting for transfers between devices  8.68 us (9%)
  Pallas kernels  7.67 us (8%)
    ppermute x9, starting transfers between devices, along(): lax.ppermute(x, axis, [(i, i ^ shift) for i in range(lax.axis_size(axis))])  34.3 us
    all_to_all x1, blocking collectives, per_device(): lax.all_to_all(packed, 'group', split_axis=0, concat_axis=1, tiled=True)  28.7 us
    all_to_all x1, starting transfers between devices, per_device(): lax.all_to_all(load, 'group', split_axis=0, concat_axis=0, tiled=True, ax...  11.8 us
    ppermute x9, waiting for transfers between devices, along(): lax.ppermute(x, axis, [(i, i ^ shift) for i in range(lax.axis_size(axis))])  5.83 us
    all_to_all x1, starting transfers between devices, per_device(): parts = lax.all_to_all(part, 'tp', split_axis=0, concat_axis=0, tiled=True)  4.33 us
    ppermute x1, starting transfers between devices, per_device(): lax.ppermute(jnp.concatenate([keep, got], axis=1), ('group', 'tp'), turn)  2.4 us
  transfers between devices with their start and end apart: 12, of which 4 were waited for; matrix products, arithmetic and copies ran while one was open for 0% of the time, Pallas kernels for 4%

profile of v4, /device:TPU:1, one launch (start us, length us, event | category | flops | bytes accessed | tf_op | source)
XLA Modules:
  0.0 99.5 jit_solution(12810441686105954506)
XLA Ops:
  0.6 1.7 %load.1 = (bf16[16,8,896]{2,1,0:T(8,128)(2,1)}, s32[1,16]{1,0:T(1,128)S(1)}) custom-call(s32[2]{0:T(128)} %counts_hbm.1, bf16[2,8,320]{2,1,0:T(8,128)(2,1)} %hidden_hbm.1, bf16[10,1024]{1,0:T(8,128)(2,1)} %bitcast.8, f32[8,10]{1,0:T(8,128)} %bitcast.9, s32[2,1,8]{2,1,0:T(1,128)} %bitcast.11, s32[2,8]{1,0:T(2,128)} %ids_hbm.1), custom_call_target="tpu_custom_call" | custom-call | tf_op jit(solution)/shard_map/load/pallas_call | solution.py:404
  2.3 11.8 %all-to-all-start = ((bf16[16,8,896]{2,1,0:T(8,128)(2,1)}), bf16[16,8,896]{2,1,0:T(8,128)(2,1)S(1)}, u32[]{:S(2)}, u32[]{:S(2)}) async-start(bf16[16,8,896]{2,1,0:T(8,128)(2,1)} %get-tuple-element.16), calls=%async_computation | async-start | bytes 458752 | tf_op jit(solution)/shard_map/all_to_all | solution.py:431
  14.1 1.1 %pieces.1 = (bf16[320,128]{1,0:T(8,128)(2,1)S(1)}, bf16[2,4,2,16,128]{4,3,2,1,0:T(8,128)(2,1)S(1)}, bf16[2,4,2,16,128]{4,3,2,1,0:T(8,128)(2,1)S(1)}, bf16[2,4,2,...) custom-call(bf16[320,128]{1,0:T(8,128)(2,1)} %codes_hbm.1, f32[1,320]{1,0:T(1,128)} %bitcast.10, ...), custom_call_target="tpu_custom_call" | custom-call | tf_op jit(solution)/shard_map/pieces/pallas_call | solution.py:436
  15.3 3.2 %collective-permute-start.1 = (bf16[2,4,2,16,128]{4,3,2,1,0:T(8,128)(2,1)S(1)}, bf16[2,4,2,16,128]{4,3,2,1,0:T(8,128)(2,1)S(1)}, u32[]{:S(2)}, u32[]{:S(2)}) collective-permute-start(bf16[2,4,2,16,128]{4,3,2,1,0:T(8,128)(2,1)S(1)} %get-tuple-element.21), channel_id=1, source_target_pairs={{0,4},{1,5},{2,6},{3,7},{4,0},{5,1},{6,2},{7,3},{8,12},{9,13},{10,... | collective-permute-start | bytes 196616 | tf_op jit(solution)/shard_map/ppermute | solution.py:402
  18.5 4.2 %collective-permute-start.2 = (bf16[2,4,2,16,128]{4,3,2,1,0:T(8,128)(2,1)S(1)}, bf16[2,4,2,16,128]{4,3,2,1,0:T(8,128)(2,1)S(1)}, u32[]{:S(2)}, u32[]{:S(2)}) collective-permute-start(bf16[2,4,2,16,128]{4,3,2,1,0:T(8,128)(2,1)S(1)} %get-tuple-element.22), channel_id=1, source_target_pairs={{0,8},{1,9},{2,10},{3,11},{4,12},{5,13},{6,14},{7,15},{8,0},{9,1},... | collective-permute-start | bytes 196616 | tf_op jit(solution)/shard_map/ppermute | solution.py:402
  22.7 1.9 %collective-permute-start.3 = (bf16[2,4,2,16,128]{4,3,2,1,0:T(8,128)(2,1)S(1)}, bf16[2,4,2,16,128]{4,3,2,1,0:T(8,128)(2,1)S(1)}, u32[]{:S(2)}, u32[]{:S(2)}) collective-permute-start(bf16[2,4,2,16,128]{4,3,2,1,0:T(8,128)(2,1)S(1)} %get-tuple-element.23), channel_id=1, source_target_pairs={{0,12},{1,13},{2,14},{3,15},{4,8},{5,9},{6,10},{7,11},{8,4},{9,5},... | collective-permute-start | bytes 196616 | tf_op jit(solution)/shard_map/ppermute | solution.py:402
  24.7 7.4 %collective-permute-start = (bf16[320,128]{1,0:T(8,128)(2,1)S(1)}, bf16[320,128]{1,0:T(8,128)(2,1)S(1)}, u32[]{:S(2)}, u32[]{:S(2)}) collective-permute-start(bf16[320,128]{1,0:T(8,128)(2,1)S(1)} %get-tuple-element.17.mine_ref), channel_id=1, source_target_pairs={{0,32},{16,48},{32,0},{48,16},{64,96},{80,112},{96,64},{112,80},{1... | collective-permute-start | bytes 245768 | tf_op jit(solution)/shard_map/ppermute | solution.py:402
  32.1 2.3 %collective-permute-start.4 = (bf16[2,128,128]{2,1,0:T(8,128)(2,1)S(1)}, bf16[2,128,128]{2,1,0:T(8,128)(2,1)S(1)}, u32[]{:S(2)}, u32[]{:S(2)}) collective-permute-start(bf16[2,128,128]{2,1,0:T(8,128)(2,1)S(1)} %swap.1), channel_id=1, source_target_pairs={{0,32},{16,48},{32,0},{48,16},{64,96},{80,112},{96,64},{112,80},{1... | collective-permute-start | bytes 196616 | tf_op jit(solution)/shard_map/ppermute | solution.py:402
  34.4 1.7 %part.1 = (f32[16,16,256]{2,1,0:T(8,128)S(1)}, f32[16,16,128]{2,1,0:T(8,128)S(1)}, bf16[256,256]{1,0:T(8,128)(2,1)S(1)}) custom-call(bf16[16,8,896]{2,1,0:T(8,128)(2,1)S(1)} %all-to-all-done.came_ref, bf16[320,128]{1,0:T(8,128)(2,1)S(1)} %get-tuple-element.17.mine_ref, bf16[320,128]{1,0:T(8,128)(2,1)S(1)} %collective-permute-done.other_ref, ...), custom_call_target="tpu_custom_call" | custom-call | tf_op jit(solution)/shard_map/part/pallas_call | solution.py:464
  36.2 5.0 %collective-permute-done.4.other_ref = bf16[2,128,128]{2,1,0:T(8,128)(2,1)S(1)} collective-permute-done((bf16[2,128,128]{2,1,0:T(8,128)(2,1)S(1)}, bf16[2,128,128]{2,1,0:T(8,128)(2,1)S(1)}, u32[]{:S(2)}, u32[]{:S(2)}) %collective-permute-start.4) | collective-permute-done | bytes 65568 | tf_op jit(solution)/shard_map/ppermute | solution.py:402
  41.2 0.9 whole.1.after_ref
  42.1 4.3 %all-to-all-start.1 = ((f32[16,16,384]{2,1,0:T(8,128)}), f32[16,16,384]{2,1,0:T(8,128)S(1)}, u32[]{:S(2)}, u32[]{:S(2)}) async-start(f32[16,16,384]{2,1,0:T(8,128)} %whole.1.after_ref), calls=%async_computation.1 | async-start | bytes 786432 | tf_op jit(solution)/shard_map/all_to_all | solution.py:488
  46.5 4.5 %collective-permute-start.9 = (bf16[4,2,4,2,16,128]{5,4,3,2,1,0:T(8,128)(2,1)S(1)}, bf16[4,2,4,2,16,128]{5,4,3,2,1,0:T(8,128)(2,1)S(1)}, u32[]{:S(2)}, u32[]{:S(2)}) collective-permute-start(bf16[4,2,4,2,16,128]{5,4,3,2,1,0:T(8,128)(2,1)S(1)} %join.1.shard0_ref), channel_id=1, source_target_pairs={{0,3},{1,2},{2,1},{3,0},{4,7},{5,6},{6,5},{7,4},{8,11},{9,10},{10,... | collective-permute-start | bytes 786440 | tf_op jit(solution)/shard_map/ppermute | solution.py:402
  51.0 2.5 %collective-permute-start.8 = (bf16[4,2,4,2,16,128]{5,4,3,2,1,0:T(8,128)(2,1)S(1)}, bf16[4,2,4,2,16,128]{5,4,3,2,1,0:T(8,128)(2,1)S(1)}, u32[]{:S(2)}, u32[]{:S(2)}) collective-permute-start(bf16[4,2,4,2,16,128]{5,4,3,2,1,0:T(8,128)(2,1)S(1)} %join.1.shard0_ref), channel_id=1, source_target_pairs={{0,2},{1,3},{2,0},{3,1},{4,6},{5,7},{6,4},{7,5},{8,10},{9,11},{10,... | collective-permute-start | bytes 786440 | tf_op jit(solution)/shard_map/ppermute | solution.py:402
  53.5 2.0 %collective-permute-start.7 = (bf16[4,2,4,2,16,128]{5,4,3,2,1,0:T(8,128)(2,1)S(1)}, bf16[4,2,4,2,16,128]{5,4,3,2,1,0:T(8,128)(2,1)S(1)}, u32[]{:S(2)}, u32[]{:S(2)}) collective-permute-start(bf16[4,2,4,2,16,128]{5,4,3,2,1,0:T(8,128)(2,1)S(1)} %join.1.shard0_ref), channel_id=1, source_target_pairs={{0,1},{1,0},{2,3},{3,2},{4,5},{5,4},{6,7},{7,6},{8,9},{9,8},{10,11... | collective-permute-start | bytes 786440 | tf_op jit(solution)/shard_map/ppermute | solution.py:402
  55.5 1.0 %all-to-all-done.1.parts_ref.after_ref = f32[16,16,384]{2,1,0:T(8,128)S(1)} async-done(((f32[16,16,384]{2,1,0:T(8,128)}), f32[16,16,384]{2,1,0:T(8,128)S(1)}, u32[]{:S(2)}, u32[]{:S(2)}) %all-to-all-start.1) | async-done | bytes 393248 | tf_op jit(solution)/shard_map/all_to_all | solution.py:488
  56.5 6.3 %collective-permute-start.5 = (bf16[16,256]{1,0:T(8,128)(2,1)S(1)}, bf16[16,256]{1,0:T(8,128)(2,1)S(1)}, u32[]{:S(2)}, u32[]{:S(2)}) collective-permute-start(bf16[16,256]{1,0:T(8,128)(2,1)S(1)} %get-tuple-element.25), channel_id=1, source_target_pairs={{0,16},{16,0},{32,48},{48,32},{64,80},{80,64},{96,112},{112,96},{1... | collective-permute-start | bytes 24584 | tf_op jit(solution)/shard_map/ppermute | solution.py:402
  62.8 0.8 collective-permute-done.5
  63.6 2.4 %collective-permute-start.6 = (bf16[16,512]{1,0:T(8,128)(2,1)S(1)}, bf16[16,512]{1,0:T(8,128)(2,1)S(1)}, u32[]{:S(2)}, u32[]{:S(2)}) collective-permute-start(bf16[16,512]{1,0:T(8,128)(2,1)S(1)} %pad_maximum_fusion), channel_id=1, source_target_pairs={{0,0},{1,16},{2,64},{3,80},{4,128},{5,144},{6,192},{7,208},{8,256}... | collective-permute-start | bytes 49160 | tf_op jit(solution)/shard_map/ppermute | solution.py:510
  66.0 0.8 facts.1
  66.8 1.9 %collective-permute-done.6.mine_ref = bf16[16,512]{1,0:T(8,128)(2,1)S(1)} collective-permute-done((bf16[16,512]{1,0:T(8,128)(2,1)S(1)}, bf16[16,512]{1,0:T(8,128)(2,1)S(1)}, u32[]{:S(2)}, u32[]{:S(2)}) %collective-permute-start.6) | collective-permute-done | bytes 16416 | tf_op jit(solution)/shard_map/ppermute | solution.py:510
  68.6 1.4 %attend.1 = bf16[64,256]{1,0:T(8,128)(2,1)S(1)} custom-call(s32[2]{0:T(128)S(1)} %copy-done, bf16[16,512]{1,0:T(8,128)(2,1)S(1)} %collective-permute-done.6.mine_ref, bf16[64,16]{1,0:T(8,128)(2,1)S(1)} %get-tuple-element.27.placed_ref, bf16[4,2,4,2,16,128]{5,4,3,2,1,0:T(8,128)(2,1)S(1)} %join.1.shard0_ref, ...), custom_call_target="tpu_custom_call" | custom-call | tf_op jit(solution)/shard_map/attend/pallas_call | solution.py:524
  70.1 28.7 %all_to_all.22 = bf16[32,2,256]{2,1,0:T(2,128)(2,1)S(1)} all-to-all(bf16[32,2,256]{2,1,0:T(2,128)(2,1)S(1)} %reshape.10), channel_id=1, replica_groups=mesh['group'=32,'tp'=16] {'group'}, dimensions={0} | all-to-all | bytes 65536 | tf_op jit(solution)/shard_map/all_to_all | solution.py:533
  98.8 0.6 all_to_all.18
  (15 shorter events, 0.1 us)
Async XLA Ops:
  2.3 29.8 %all-to-all-start = ((bf16[16,8,896]{2,1,0:T(8,128)(2,1)}), bf16[16,8,896]{2,1,0:T(8,128)(2,1)S(1)}, u32[]{:S(2)}, u32[]{:S(2)}) async-start(bf16[16,8,896]{2,1,0:T(8,128)(2,1)} %get-tuple-element.16), calls=%async_computation | async-start | bytes 458752 | tf_op jit(solution)/shard_map/all_to_all | solution.py:431
  15.3 16.8 %collective-permute-start.1 = (bf16[2,4,2,16,128]{4,3,2,1,0:T(8,128)(2,1)S(1)}, bf16[2,4,2,16,128]{4,3,2,1,0:T(8,128)(2,1)S(1)}, u32[]{:S(2)}, u32[]{:S(2)}) collective-permute-start(bf16[2,4,2,16,128]{4,3,2,1,0:T(8,128)(2,1)S(1)} %get-tuple-element.21), channel_id=1, source_target_pairs={{0,4},{1,5},{2,6},{3,7},{4,0},{5,1},{6,2},{7,3},{8,12},{9,13},{10,... | collective-permute-start | bytes 196616 | tf_op jit(solution)/shard_map/ppermute | solution.py:402
  18.5 13.6 %collective-permute-start.2 = (bf16[2,4,2,16,128]{4,3,2,1,0:T(8,128)(2,1)S(1)}, bf16[2,4,2,16,128]{4,3,2,1,0:T(8,128)(2,1)S(1)}, u32[]{:S(2)}, u32[]{:S(2)}) collective-permute-start(bf16[2,4,2,16,128]{4,3,2,1,0:T(8,128)(2,1)S(1)} %get-tuple-element.22), channel_id=1, source_target_pairs={{0,8},{1,9},{2,10},{3,11},{4,12},{5,13},{6,14},{7,15},{8,0},{9,1},... | collective-permute-start | bytes 196616 | tf_op jit(solution)/shard_map/ppermute | solution.py:402
  22.7 9.3 %collective-permute-start.3 = (bf16[2,4,2,16,128]{4,3,2,1,0:T(8,128)(2,1)S(1)}, bf16[2,4,2,16,128]{4,3,2,1,0:T(8,128)(2,1)S(1)}, u32[]{:S(2)}, u32[]{:S(2)}) collective-permute-start(bf16[2,4,2,16,128]{4,3,2,1,0:T(8,128)(2,1)S(1)} %get-tuple-element.23), channel_id=1, source_target_pairs={{0,12},{1,13},{2,14},{3,15},{4,8},{5,9},{6,10},{7,11},{8,4},{9,5},... | collective-permute-start | bytes 196616 | tf_op jit(solution)/shard_map/ppermute | solution.py:402
  24.7 9.8 %collective-permute-start = (bf16[320,128]{1,0:T(8,128)(2,1)S(1)}, bf16[320,128]{1,0:T(8,128)(2,1)S(1)}, u32[]{:S(2)}, u32[]{:S(2)}) collective-permute-start(bf16[320,128]{1,0:T(8,128)(2,1)S(1)} %get-tuple-element.17.mine_ref), channel_id=1, source_target_pairs={{0,32},{16,48},{32,0},{48,16},{64,96},{80,112},{96,64},{112,80},{1... | collective-permute-start | bytes 245768 | tf_op jit(solution)/shard_map/ppermute | solution.py:402
  32.1 9.1 %collective-permute-start.4 = (bf16[2,128,128]{2,1,0:T(8,128)(2,1)S(1)}, bf16[2,128,128]{2,1,0:T(8,128)(2,1)S(1)}, u32[]{:S(2)}, u32[]{:S(2)}) collective-permute-start(bf16[2,128,128]{2,1,0:T(8,128)(2,1)S(1)} %swap.1), channel_id=1, source_target_pairs={{0,32},{16,48},{32,0},{48,16},{64,96},{80,112},{96,64},{112,80},{1... | collective-permute-start | bytes 196616 | tf_op jit(solution)/shard_map/ppermute | solution.py:402
  36.2 32.5 %copy-start = (s32[2]{0:T(128)S(1)}, s32[2]{0:T(128)}, u32[]{:S(2)}) copy-start(s32[2]{0:T(128)} %lengths_ref.1) | copy-start | bytes 28
  42.1 14.4 %all-to-all-start.1 = ((f32[16,16,384]{2,1,0:T(8,128)}), f32[16,16,384]{2,1,0:T(8,128)S(1)}, u32[]{:S(2)}, u32[]{:S(2)}) async-start(f32[16,16,384]{2,1,0:T(8,128)} %whole.1.after_ref), calls=%async_computation.1 | async-start | bytes 786432 | tf_op jit(solution)/shard_map/all_to_all | solution.py:488
  46.5 20.3 %collective-permute-start.9 = (bf16[4,2,4,2,16,128]{5,4,3,2,1,0:T(8,128)(2,1)S(1)}, bf16[4,2,4,2,16,128]{5,4,3,2,1,0:T(8,128)(2,1)S(1)}, u32[]{:S(2)}, u32[]{:S(2)}) collective-permute-start(bf16[4,2,4,2,16,128]{5,4,3,2,1,0:T(8,128)(2,1)S(1)} %join.1.shard0_ref), channel_id=1, source_target_pairs={{0,3},{1,2},{2,1},{3,0},{4,7},{5,6},{6,5},{7,4},{8,11},{9,10},{10,... | collective-permute-start | bytes 786440 | tf_op jit(solution)/shard_map/ppermute | solution.py:402
  51.0 15.8 %collective-permute-start.8 = (bf16[4,2,4,2,16,128]{5,4,3,2,1,0:T(8,128)(2,1)S(1)}, bf16[4,2,4,2,16,128]{5,4,3,2,1,0:T(8,128)(2,1)S(1)}, u32[]{:S(2)}, u32[]{:S(2)}) collective-permute-start(bf16[4,2,4,2,16,128]{5,4,3,2,1,0:T(8,128)(2,1)S(1)} %join.1.shard0_ref), channel_id=1, source_target_pairs={{0,2},{1,3},{2,0},{3,1},{4,6},{5,7},{6,4},{7,5},{8,10},{9,11},{10,... | collective-permute-start | bytes 786440 | tf_op jit(solution)/shard_map/ppermute | solution.py:402
  53.5 13.3 %collective-permute-start.7 = (bf16[4,2,4,2,16,128]{5,4,3,2,1,0:T(8,128)(2,1)S(1)}, bf16[4,2,4,2,16,128]{5,4,3,2,1,0:T(8,128)(2,1)S(1)}, u32[]{:S(2)}, u32[]{:S(2)}) collective-permute-start(bf16[4,2,4,2,16,128]{5,4,3,2,1,0:T(8,128)(2,1)S(1)} %join.1.shard0_ref), channel_id=1, source_target_pairs={{0,1},{1,0},{2,3},{3,2},{4,5},{5,4},{6,7},{7,6},{8,9},{9,8},{10,11... | collective-permute-start | bytes 786440 | tf_op jit(solution)/shard_map/ppermute | solution.py:402
  56.5 7.1 %collective-permute-start.5 = (bf16[16,256]{1,0:T(8,128)(2,1)S(1)}, bf16[16,256]{1,0:T(8,128)(2,1)S(1)}, u32[]{:S(2)}, u32[]{:S(2)}) collective-permute-start(bf16[16,256]{1,0:T(8,128)(2,1)S(1)} %get-tuple-element.25), channel_id=1, source_target_pairs={{0,16},{16,0},{32,48},{48,32},{64,80},{80,64},{96,112},{112,96},{1... | collective-permute-start | bytes 24584 | tf_op jit(solution)/shard_map/ppermute | solution.py:402
  63.6 5.0 %collective-permute-start.6 = (bf16[16,512]{1,0:T(8,128)(2,1)S(1)}, bf16[16,512]{1,0:T(8,128)(2,1)S(1)}, u32[]{:S(2)}, u32[]{:S(2)}) collective-permute-start(bf16[16,512]{1,0:T(8,128)(2,1)S(1)} %pad_maximum_fusion), channel_id=1, source_target_pairs={{0,0},{1,16},{2,64},{3,80},{4,128},{5,144},{6,192},{7,208},{8,256}... | collective-permute-start | bytes 49160 | tf_op jit(solution)/shard_map/ppermute | solution.py:510

commit v5 on v4

--- a/solution.py
+++ b/solution.py
@@ -138,7 +138,7 @@
     return cell.reshape(peers * steps, size).astype(jnp.bfloat16)
 
 
-def swap_kernel(came_ref, after1_ref, after2_ref, after3_ref, out_ref):
+def swap_kernel(came_ref, out_ref):
     _, block, lanes = out_ref.shape
     width = came_ref.shape[2]
     for i in range(2):
@@ -216,7 +216,7 @@
     put(pairs_ref, 0, pairs + dot(inputs, weight_ref[2]))
 
 
-def whole_kernel(queries_ref, pairs_ref, spread_ref, other_ref, after_ref, part_ref):
+def whole_kernel(queries_ref, pairs_ref, spread_ref, other_ref, after1_ref, after2_ref, after3_ref, part_ref):
     peers, rows, wide = queries_ref.shape
     block = spread_ref.shape[1] // 2
     games = spread_ref.shape[0] // block
@@ -353,9 +353,8 @@
             jnp.concatenate([out[h * steps : (h + 1) * steps] for h in range(heads)], axis=1)
         )
     attended = jnp.concatenate(games_out, axis=0).astype(jnp.bfloat16)
-    packed_ref[...] = jnp.dot(
-        placed_ref[...], attended, preferred_element_type=jnp.float32
-    ).astype(jnp.bfloat16)
+    packed = jnp.dot(placed_ref[...], attended, preferred_element_type=jnp.float32)
+    packed_ref[...] = packed.reshape(packed_ref.shape).astype(jnp.bfloat16)
 
 
 def per_device(
@@ -454,11 +453,11 @@
     other = pl.pallas_call(
         swap_kernel,
         out_shape=jax.ShapeDtypeStruct((2, rows_all, LANES), bf16),
-        in_specs=[VMEM] + [ANY] * (KV_HEADS - 1),
+        in_specs=[VMEM],
         out_specs=VMEM,
         compiler_params=PARAMS,
         name="swap",
-    )(came, *pieces[1:])
+    )(came)
     other = along(other, "group", CORES)
 
     queries, pairs, spread = pl.pallas_call(
@@ -480,11 +479,11 @@
     part = pl.pallas_call(
         whole_kernel,
         out_shape=jax.ShapeDtypeStruct((peers, rows, wide + HEAD), jnp.float32),
-        in_specs=[VMEM] * 4 + [ANY],
+        in_specs=[VMEM] * 4 + [ANY] * 3,
         out_specs=VMEM,
         compiler_params=PARAMS,
         name="whole",
-    )(queries, pairs, spread, other, pieces[1])
+    )(queries, pairs, spread, other, *pieces[1:])
     parts = lax.all_to_all(part, "tp", split_axis=0, concat_axis=0, tiled=True)
 
     shard = pl.pallas_call(
@@ -523,13 +522,12 @@
 
     packed = pl.pallas_call(
         attend_kernel,
-        out_shape=jax.ShapeDtypeStruct((n_group * capacity, wide), bf16),
+        out_shape=jax.ShapeDtypeStruct((n_group, capacity, wide), bf16),
         in_specs=[SMEM] + [VMEM] * 6,
         out_specs=VMEM,
         compiler_params=PARAMS,
         name="attend",
     )(lengths, mine, placed, *shards)
-    packed = packed.reshape(n_group, capacity, wide)
     rows_back = lax.all_to_all(packed, "group", split_axis=0, concat_axis=1, tiled=True)
     return (rows_back, ids_back)
 

time: 100 us -> 100 us (level)
  waiting for transfers between devices: 8.68 us -> 11.1 us
  blocking collectives: 28.7 us -> 26.6 us
    ppermute x9, starting transfers between devices: 34.3 us -> 31.7 us  [along(): lax.ppermute(x, axis, [(i, i ^ shift) for i in range(lax.axis_size(axis))])]
    all_to_all x1, blocking collectives: 28.7 us -> 26.6 us  [per_device(): lax.all_to_all(packed, 'group', split_axis=0, concat_axis=1, tiled=True)]
    all_to_all x1, starting transfers between devices: 4.33 us -> 6.44 us  [per_device(): parts = lax.all_to_all(part, 'tp', split_axis=0, concat_axis=0, tiled=True)]
    all_to_all x1, waiting for transfers between devices: 1 us -> 3.01 us  [per_device(): parts = lax.all_to_all(part, 'tp', split_axis=0, concat_axis=0, tiled=True)]
where the time goes in v5:
time: 100 us; the launch traced here: 99.2 us
  starting transfers between devices  52.4 us (52%)
  blocking collectives  26.6 us (27%)
  waiting for transfers between devices  11.1 us (11%)
  Pallas kernels  7.69 us (8%)
    ppermute x9, starting transfers between devices, along(): lax.ppermute(x, axis, [(i, i ^ shift) for i in range(lax.axis_size(axis))])  31.7 us
    all_to_all x1, blocking collectives, per_device(): lax.all_to_all(packed, 'group', split_axis=0, concat_axis=1, tiled=True)  26.6 us
    all_to_all x1, starting transfers between devices, per_device(): lax.all_to_all(load, 'group', split_axis=0, concat_axis=0, tiled=True, ax...  11.8 us
    all_to_all x1, starting transfers between devices, per_device(): parts = lax.all_to_all(part, 'tp', split_axis=0, concat_axis=0, tiled=True)  6.44 us
    ppermute x9, waiting for transfers between devices, along(): lax.ppermute(x, axis, [(i, i ^ shift) for i in range(lax.axis_size(axis))])  6.03 us
    all_to_all x1, waiting for transfers between devices, per_device(): parts = lax.all_to_all(part, 'tp', split_axis=0, concat_axis=0, tiled=True)  3.01 us
    ppermute x1, starting transfers between devices, per_device(): lax.ppermute(jnp.concatenate([keep, got], axis=1), ('group', 'tp'), turn)  2.4 us
    ppermute x1, waiting for transfers between devices, per_device(): lax.ppermute(jnp.concatenate([keep, got], axis=1), ('group', 'tp'), turn)  2.02 us
  transfers between devices with their start and end apart: 12, of which 4 were waited for; matrix products, arithmetic and copies ran while one was open for 0% of the time, Pallas kernels for 4%

profile of v5, /device:TPU:1, one launch (start us, length us, event | category | flops | bytes accessed | tf_op | source)
XLA Modules:
  0.0 99.2 jit_solution(16384205426999295681)
XLA Ops:
  0.6 1.7 %load.1 = (bf16[16,8,896]{2,1,0:T(8,128)(2,1)}, s32[1,16]{1,0:T(1,128)S(1)}) custom-call(s32[2]{0:T(128)} %counts_hbm.1, bf16[2,8,320]{2,1,0:T(8,128)(2,1)} %hidden_hbm.1, bf16[10,1024]{1,0:T(8,128)(2,1)} %bitcast.8, f32[8,10]{1,0:T(8,128)} %bitcast.9, s32[2,1,8]{2,1,0:T(1,128)} %bitcast.11, s32[2,8]{1,0:T(2,128)} %ids_hbm.1), custom_call_target="tpu_custom_call" | custom-call | tf_op jit(solution)/shard_map/load/pallas_call | solution.py:403
  2.3 11.8 %all-to-all-start = ((bf16[16,8,896]{2,1,0:T(8,128)(2,1)}), bf16[16,8,896]{2,1,0:T(8,128)(2,1)S(1)}, u32[]{:S(2)}, u32[]{:S(2)}) async-start(bf16[16,8,896]{2,1,0:T(8,128)(2,1)} %get-tuple-element.16), calls=%async_computation | async-start | bytes 458752 | tf_op jit(solution)/shard_map/all_to_all | solution.py:430
  14.1 1.1 %pieces.1 = (bf16[320,128]{1,0:T(8,128)(2,1)S(1)}, bf16[2,4,2,16,128]{4,3,2,1,0:T(8,128)(2,1)S(1)}, bf16[2,4,2,16,128]{4,3,2,1,0:T(8,128)(2,1)S(1)}, bf16[2,4,2,...) custom-call(bf16[320,128]{1,0:T(8,128)(2,1)} %codes_hbm.1, f32[1,320]{1,0:T(1,128)} %bitcast.10, ...), custom_call_target="tpu_custom_call" | custom-call | tf_op jit(solution)/shard_map/pieces/pallas_call | solution.py:435
  15.3 7.5 %collective-permute-start = (bf16[320,128]{1,0:T(8,128)(2,1)S(1)}, bf16[320,128]{1,0:T(8,128)(2,1)S(1)}, u32[]{:S(2)}, u32[]{:S(2)}) collective-permute-start(bf16[320,128]{1,0:T(8,128)(2,1)S(1)} %get-tuple-element.17.mine_ref), channel_id=1, source_target_pairs={{0,32},{16,48},{32,0},{48,16},{64,96},{80,112},{96,64},{112,80},{1... | collective-permute-start | bytes 245768 | tf_op jit(solution)/shard_map/ppermute | solution.py:401
  22.7 2.3 %collective-permute-start.2 = (bf16[2,4,2,16,128]{4,3,2,1,0:T(8,128)(2,1)S(1)}, bf16[2,4,2,16,128]{4,3,2,1,0:T(8,128)(2,1)S(1)}, u32[]{:S(2)}, u32[]{:S(2)}) collective-permute-start(bf16[2,4,2,16,128]{4,3,2,1,0:T(8,128)(2,1)S(1)} %get-tuple-element.21), channel_id=1, source_target_pairs={{0,4},{1,5},{2,6},{3,7},{4,0},{5,1},{6,2},{7,3},{8,12},{9,13},{10,... | collective-permute-start | bytes 196616 | tf_op jit(solution)/shard_map/ppermute | solution.py:401
  25.1 2.4 %collective-permute-start.3 = (bf16[2,4,2,16,128]{4,3,2,1,0:T(8,128)(2,1)S(1)}, bf16[2,4,2,16,128]{4,3,2,1,0:T(8,128)(2,1)S(1)}, u32[]{:S(2)}, u32[]{:S(2)}) collective-permute-start(bf16[2,4,2,16,128]{4,3,2,1,0:T(8,128)(2,1)S(1)} %get-tuple-element.22), channel_id=1, source_target_pairs={{0,8},{1,9},{2,10},{3,11},{4,12},{5,13},{6,14},{7,15},{8,0},{9,1},... | collective-permute-start | bytes 196616 | tf_op jit(solution)/shard_map/ppermute | solution.py:401
  27.5 4.5 %collective-permute-start.4 = (bf16[2,4,2,16,128]{4,3,2,1,0:T(8,128)(2,1)S(1)}, bf16[2,4,2,16,128]{4,3,2,1,0:T(8,128)(2,1)S(1)}, u32[]{:S(2)}, u32[]{:S(2)}) collective-permute-start(bf16[2,4,2,16,128]{4,3,2,1,0:T(8,128)(2,1)S(1)} %get-tuple-element.23), channel_id=1, source_target_pairs={{0,12},{1,13},{2,14},{3,15},{4,8},{5,9},{6,10},{7,11},{8,4},{9,5},... | collective-permute-start | bytes 196616 | tf_op jit(solution)/shard_map/ppermute | solution.py:401
  32.1 1.9 %collective-permute-start.1 = (bf16[2,128,128]{2,1,0:T(8,128)(2,1)S(1)}, bf16[2,128,128]{2,1,0:T(8,128)(2,1)S(1)}, u32[]{:S(2)}, u32[]{:S(2)}) collective-permute-start(bf16[2,128,128]{2,1,0:T(8,128)(2,1)S(1)} %swap.1), channel_id=1, source_target_pairs={{0,32},{16,48},{32,0},{48,16},{64,96},{80,112},{96,64},{112,80},{1... | collective-permute-start | bytes 196616 | tf_op jit(solution)/shard_map/ppermute | solution.py:401
  34.0 1.7 %part.1 = (f32[16,16,256]{2,1,0:T(8,128)S(1)}, f32[16,16,128]{2,1,0:T(8,128)S(1)}, bf16[256,256]{1,0:T(8,128)(2,1)S(1)}) custom-call(bf16[16,8,896]{2,1,0:T(8,128)(2,1)S(1)} %all-to-all-done.came_ref, bf16[320,128]{1,0:T(8,128)(2,1)S(1)} %get-tuple-element.17.mine_ref, bf16[320,128]{1,0:T(8,128)(2,1)S(1)} %collective-permute-done.other_ref, ...), custom_call_target="tpu_custom_call" | custom-call | tf_op jit(solution)/shard_map/part/pallas_call | solution.py:463
  35.8 5.2 %collective-permute-done.1.other_ref = bf16[2,128,128]{2,1,0:T(8,128)(2,1)S(1)} collective-permute-done((bf16[2,128,128]{2,1,0:T(8,128)(2,1)S(1)}, bf16[2,128,128]{2,1,0:T(8,128)(2,1)S(1)}, u32[]{:S(2)}, u32[]{:S(2)}) %collective-permute-start.1) | collective-permute-done | bytes 65568 | tf_op jit(solution)/shard_map/ppermute | solution.py:401
  41.0 0.9 whole.1.after_ref
  41.9 6.4 %all-to-all-start.1 = ((f32[16,16,384]{2,1,0:T(8,128)}), f32[16,16,384]{2,1,0:T(8,128)S(1)}, u32[]{:S(2)}, u32[]{:S(2)}) async-start(f32[16,16,384]{2,1,0:T(8,128)} %whole.1.after_ref), calls=%async_computation.1 | async-start | bytes 786432 | tf_op jit(solution)/shard_map/all_to_all | solution.py:487
  48.4 4.5 %collective-permute-start.9 = (bf16[4,2,4,2,16,128]{5,4,3,2,1,0:T(8,128)(2,1)S(1)}, bf16[4,2,4,2,16,128]{5,4,3,2,1,0:T(8,128)(2,1)S(1)}, u32[]{:S(2)}, u32[]{:S(2)}) collective-permute-start(bf16[4,2,4,2,16,128]{5,4,3,2,1,0:T(8,128)(2,1)S(1)} %join.1.shard0_ref), channel_id=1, source_target_pairs={{0,3},{1,2},{2,1},{3,0},{4,7},{5,6},{6,5},{7,4},{8,11},{9,10},{10,... | collective-permute-start | bytes 786440 | tf_op jit(solution)/shard_map/ppermute | solution.py:401
  52.9 2.5 %collective-permute-start.8 = (bf16[4,2,4,2,16,128]{5,4,3,2,1,0:T(8,128)(2,1)S(1)}, bf16[4,2,4,2,16,128]{5,4,3,2,1,0:T(8,128)(2,1)S(1)}, u32[]{:S(2)}, u32[]{:S(2)}) collective-permute-start(bf16[4,2,4,2,16,128]{5,4,3,2,1,0:T(8,128)(2,1)S(1)} %join.1.shard0_ref), channel_id=1, source_target_pairs={{0,2},{1,3},{2,0},{3,1},{4,6},{5,7},{6,4},{7,5},{8,10},{9,11},{10,... | collective-permute-start | bytes 786440 | tf_op jit(solution)/shard_map/ppermute | solution.py:401
  55.4 2.0 %collective-permute-start.7 = (bf16[4,2,4,2,16,128]{5,4,3,2,1,0:T(8,128)(2,1)S(1)}, bf16[4,2,4,2,16,128]{5,4,3,2,1,0:T(8,128)(2,1)S(1)}, u32[]{:S(2)}, u32[]{:S(2)}) collective-permute-start(bf16[4,2,4,2,16,128]{5,4,3,2,1,0:T(8,128)(2,1)S(1)} %join.1.shard0_ref), channel_id=1, source_target_pairs={{0,1},{1,0},{2,3},{3,2},{4,5},{5,4},{6,7},{7,6},{8,9},{9,8},{10,11... | collective-permute-start | bytes 786440 | tf_op jit(solution)/shard_map/ppermute | solution.py:401
  57.4 3.0 %all-to-all-done.1.parts_ref.after_ref = f32[16,16,384]{2,1,0:T(8,128)S(1)} async-done(((f32[16,16,384]{2,1,0:T(8,128)}), f32[16,16,384]{2,1,0:T(8,128)S(1)}, u32[]{:S(2)}, u32[]{:S(2)}) %all-to-all-start.1) | async-done | bytes 393248 | tf_op jit(solution)/shard_map/all_to_all | solution.py:487
  60.4 4.1 %collective-permute-start.5 = (bf16[16,256]{1,0:T(8,128)(2,1)S(1)}, bf16[16,256]{1,0:T(8,128)(2,1)S(1)}, u32[]{:S(2)}, u32[]{:S(2)}) collective-permute-start(bf16[16,256]{1,0:T(8,128)(2,1)S(1)} %get-tuple-element.25), channel_id=1, source_target_pairs={{0,16},{16,0},{32,48},{48,32},{64,80},{80,64},{96,112},{112,96},{1... | collective-permute-start | bytes 24584 | tf_op jit(solution)/shard_map/ppermute | solution.py:401
  64.5 0.8 collective-permute-done.5
  65.3 2.4 %collective-permute-start.6 = (bf16[16,512]{1,0:T(8,128)(2,1)S(1)}, bf16[16,512]{1,0:T(8,128)(2,1)S(1)}, u32[]{:S(2)}, u32[]{:S(2)}) collective-permute-start(bf16[16,512]{1,0:T(8,128)(2,1)S(1)} %pad_maximum_fusion), channel_id=1, source_target_pairs={{0,0},{1,16},{2,64},{3,80},{4,128},{5,144},{6,192},{7,208},{8,256}... | collective-permute-start | bytes 49160 | tf_op jit(solution)/shard_map/ppermute | solution.py:509
  67.8 0.8 facts.1
  68.5 2.0 %collective-permute-done.6.mine_ref = bf16[16,512]{1,0:T(8,128)(2,1)S(1)} collective-permute-done((bf16[16,512]{1,0:T(8,128)(2,1)S(1)}, bf16[16,512]{1,0:T(8,128)(2,1)S(1)}, u32[]{:S(2)}, u32[]{:S(2)}) %collective-permute-start.6) | collective-permute-done | bytes 16416 | tf_op jit(solution)/shard_map/ppermute | solution.py:509
  70.6 1.4 %attend.1 = bf16[32,2,256]{2,1,0:T(2,128)(2,1)S(1)} custom-call(s32[2]{0:T(128)S(1)} %copy-done, bf16[16,512]{1,0:T(8,128)(2,1)S(1)} %collective-permute-done.6.mine_ref, bf16[64,16]{1,0:T(8,128)(2,1)S(1)} %get-tuple-element.27.placed_ref, bf16[4,2,4,2,16,128]{5,4,3,2,1,0:T(8,128)(2,1)S(1)} %join.1.shard0_ref, ...), custom_call_target="tpu_custom_call" | custom-call | tf_op jit(solution)/shard_map/attend/pallas_call | solution.py:523
  72.0 26.6 %all_to_all.22 = bf16[32,2,256]{2,1,0:T(2,128)(2,1)S(1)} all-to-all(bf16[32,2,256]{2,1,0:T(2,128)(2,1)S(1)} %attend.1), channel_id=1, replica_groups=mesh['group'=32,'tp'=16] {'group'}, dimensions={0} | all-to-all | bytes 65536 | tf_op jit(solution)/shard_map/all_to_all | solution.py:531
  98.6 0.6 all_to_all.18
  (14 shorter events, 0.1 us)
Async XLA Ops:
  2.3 29.8 %all-to-all-start = ((bf16[16,8,896]{2,1,0:T(8,128)(2,1)}), bf16[16,8,896]{2,1,0:T(8,128)(2,1)S(1)}, u32[]{:S(2)}, u32[]{:S(2)}) async-start(bf16[16,8,896]{2,1,0:T(8,128)(2,1)} %get-tuple-element.16), calls=%async_computation | async-start | bytes 458752 | tf_op jit(solution)/shard_map/all_to_all | solution.py:430
  15.3 18.8 %collective-permute-start = (bf16[320,128]{1,0:T(8,128)(2,1)S(1)}, bf16[320,128]{1,0:T(8,128)(2,1)S(1)}, u32[]{:S(2)}, u32[]{:S(2)}) collective-permute-start(bf16[320,128]{1,0:T(8,128)(2,1)S(1)} %get-tuple-element.17.mine_ref), channel_id=1, source_target_pairs={{0,32},{16,48},{32,0},{48,16},{64,96},{80,112},{96,64},{112,80},{1... | collective-permute-start | bytes 245768 | tf_op jit(solution)/shard_map/ppermute | solution.py:401
  22.7 13.0 %collective-permute-start.2 = (bf16[2,4,2,16,128]{4,3,2,1,0:T(8,128)(2,1)S(1)}, bf16[2,4,2,16,128]{4,3,2,1,0:T(8,128)(2,1)S(1)}, u32[]{:S(2)}, u32[]{:S(2)}) collective-permute-start(bf16[2,4,2,16,128]{4,3,2,1,0:T(8,128)(2,1)S(1)} %get-tuple-element.21), channel_id=1, source_target_pairs={{0,4},{1,5},{2,6},{3,7},{4,0},{5,1},{6,2},{7,3},{8,12},{9,13},{10,... | collective-permute-start | bytes 196616 | tf_op jit(solution)/shard_map/ppermute | solution.py:401
  25.1 10.7 %collective-permute-start.3 = (bf16[2,4,2,16,128]{4,3,2,1,0:T(8,128)(2,1)S(1)}, bf16[2,4,2,16,128]{4,3,2,1,0:T(8,128)(2,1)S(1)}, u32[]{:S(2)}, u32[]{:S(2)}) collective-permute-start(bf16[2,4,2,16,128]{4,3,2,1,0:T(8,128)(2,1)S(1)} %get-tuple-element.22), channel_id=1, source_target_pairs={{0,8},{1,9},{2,10},{3,11},{4,12},{5,13},{6,14},{7,15},{8,0},{9,1},... | collective-permute-start | bytes 196616 | tf_op jit(solution)/shard_map/ppermute | solution.py:401
  27.5 8.3 %collective-permute-start.4 = (bf16[2,4,2,16,128]{4,3,2,1,0:T(8,128)(2,1)S(1)}, bf16[2,4,2,16,128]{4,3,2,1,0:T(8,128)(2,1)S(1)}, u32[]{:S(2)}, u32[]{:S(2)}) collective-permute-start(bf16[2,4,2,16,128]{4,3,2,1,0:T(8,128)(2,1)S(1)} %get-tuple-element.23), channel_id=1, source_target_pairs={{0,12},{1,13},{2,14},{3,15},{4,8},{5,9},{6,10},{7,11},{8,4},{9,5},... | collective-permute-start | bytes 196616 | tf_op jit(solution)/shard_map/ppermute | solution.py:401
  32.1 8.9 %collective-permute-start.1 = (bf16[2,128,128]{2,1,0:T(8,128)(2,1)S(1)}, bf16[2,128,128]{2,1,0:T(8,128)(2,1)S(1)}, u32[]{:S(2)}, u32[]{:S(2)}) collective-permute-start(bf16[2,128,128]{2,1,0:T(8,128)(2,1)S(1)} %swap.1), channel_id=1, source_target_pairs={{0,32},{16,48},{32,0},{48,16},{64,96},{80,112},{96,64},{112,80},{1... | collective-permute-start | bytes 196616 | tf_op jit(solution)/shard_map/ppermute | solution.py:401
  35.8 34.8 %copy-start = (s32[2]{0:T(128)S(1)}, s32[2]{0:T(128)}, u32[]{:S(2)}) copy-start(s32[2]{0:T(128)} %lengths_ref.1) | copy-start | bytes 28
  41.9 18.5 %all-to-all-start.1 = ((f32[16,16,384]{2,1,0:T(8,128)}), f32[16,16,384]{2,1,0:T(8,128)S(1)}, u32[]{:S(2)}, u32[]{:S(2)}) async-start(f32[16,16,384]{2,1,0:T(8,128)} %whole.1.after_ref), calls=%async_computation.1 | async-start | bytes 786432 | tf_op jit(solution)/shard_map/all_to_all | solution.py:487
  48.4 20.1 %collective-permute-start.9 = (bf16[4,2,4,2,16,128]{5,4,3,2,1,0:T(8,128)(2,1)S(1)}, bf16[4,2,4,2,16,128]{5,4,3,2,1,0:T(8,128)(2,1)S(1)}, u32[]{:S(2)}, u32[]{:S(2)}) collective-permute-start(bf16[4,2,4,2,16,128]{5,4,3,2,1,0:T(8,128)(2,1)S(1)} %join.1.shard0_ref), channel_id=1, source_target_pairs={{0,3},{1,2},{2,1},{3,0},{4,7},{5,6},{6,5},{7,4},{8,11},{9,10},{10,... | collective-permute-start | bytes 786440 | tf_op jit(solution)/shard_map/ppermute | solution.py:401
  52.9 15.6 %collective-permute-start.8 = (bf16[4,2,4,2,16,128]{5,4,3,2,1,0:T(8,128)(2,1)S(1)}, bf16[4,2,4,2,16,128]{5,4,3,2,1,0:T(8,128)(2,1)S(1)}, u32[]{:S(2)}, u32[]{:S(2)}) collective-permute-start(bf16[4,2,4,2,16,128]{5,4,3,2,1,0:T(8,128)(2,1)S(1)} %join.1.shard0_ref), channel_id=1, source_target_pairs={{0,2},{1,3},{2,0},{3,1},{4,6},{5,7},{6,4},{7,5},{8,10},{9,11},{10,... | collective-permute-start | bytes 786440 | tf_op jit(solution)/shard_map/ppermute | solution.py:401
  55.4 13.2 %collective-permute-start.7 = (bf16[4,2,4,2,16,128]{5,4,3,2,1,0:T(8,128)(2,1)S(1)}, bf16[4,2,4,2,16,128]{5,4,3,2,1,0:T(8,128)(2,1)S(1)}, u32[]{:S(2)}, u32[]{:S(2)}) collective-permute-start(bf16[4,2,4,2,16,128]{5,4,3,2,1,0:T(8,128)(2,1)S(1)} %join.1.shard0_ref), channel_id=1, source_target_pairs={{0,1},{1,0},{2,3},{3,2},{4,5},{5,4},{6,7},{7,6},{8,9},{9,8},{10,11... | collective-permute-start | bytes 786440 | tf_op jit(solution)/shard_map/ppermute | solution.py:401
  60.4 4.9 %collective-permute-start.5 = (bf16[16,256]{1,0:T(8,128)(2,1)S(1)}, bf16[16,256]{1,0:T(8,128)(2,1)S(1)}, u32[]{:S(2)}, u32[]{:S(2)}) collective-permute-start(bf16[16,256]{1,0:T(8,128)(2,1)S(1)} %get-tuple-element.25), channel_id=1, source_target_pairs={{0,16},{16,0},{32,48},{48,32},{64,80},{80,64},{96,112},{112,96},{1... | collective-permute-start | bytes 24584 | tf_op jit(solution)/shard_map/ppermute | solution.py:401
  65.3 5.2 %collective-permute-start.6 = (bf16[16,512]{1,0:T(8,128)(2,1)S(1)}, bf16[16,512]{1,0:T(8,128)(2,1)S(1)}, u32[]{:S(2)}, u32[]{:S(2)}) collective-permute-start(bf16[16,512]{1,0:T(8,128)(2,1)S(1)} %pad_maximum_fusion), channel_id=1, source_target_pairs={{0,0},{1,16},{2,64},{3,80},{4,128},{5,144},{6,192},{7,208},{8,256}... | collective-permute-start | bytes 49160 | tf_op jit(solution)/shard_map/ppermute | solution.py:509

commit v6 on v5

--- a/solution.py
+++ b/solution.py
@@ -22,6 +22,10 @@
 HBM = pl.BlockSpec(memory_space=pltpu.HBM)
 ANY = pl.BlockSpec(memory_space=pl.ANY)
 PARAMS = pltpu.CompilerParams(vmem_limit_bytes=24 * 1024 * 1024)
+
+
+def whole(shape):
+    return pl.BlockSpec(shape, lambda i: (0,) * len(shape))
 
 
 def column(row):
@@ -41,44 +45,18 @@
 
 
 def load_kernel(
-    counts_hbm,
-    hidden_hbm,
-    codes_hbm,
-    scales_hbm,
-    learner_hbm,
-    ids_hbm,
-    load_ref,
-    named_ref,
-    counts_ref,
-    hidden_ref,
-    codes_ref,
-    scales_ref,
-    learner_ref,
-    ids_ref,
-    sems,
+    counts_ref, hidden_ref, codes_ref, scales_ref, learner_ref, ids_ref, load_ref, named_ref
 ):
-    copies = fetch(
-        [
-            (codes_hbm, codes_ref),
-            (scales_hbm, scales_ref),
-            (hidden_hbm, hidden_ref),
-            (counts_hbm, counts_ref),
-            (learner_hbm, learner_ref),
-            (ids_hbm, ids_ref),
-        ],
-        sems,
-    )
     peers = load_ref.shape[0]
     games, steps, features = hidden_ref.shape
-    for copy in copies:
-        copy.wait()
     inputs = jnp.concatenate(
         [hidden_ref[game].astype(jnp.float32) for game in range(games)], axis=1
     ).astype(jnp.bfloat16)
     load_ref[:, :, : games * features] = jnp.broadcast_to(inputs, (peers,) + inputs.shape)
     step = lax.broadcasted_iota(jnp.int32, (1, steps), 1)
     named = [
-        jnp.where(step < counts_ref[game], learner_ref[game], -1) for game in range(games)
+        jnp.where(step < counts_ref[:, game : game + 1], learner_ref[game], -1)
+        for game in range(games)
     ]
     named = jnp.concatenate(named, axis=1)
     named_ref[...] = named
@@ -400,33 +378,26 @@
     def along(x, axis, shift):
         return lax.ppermute(x, axis, [(i, i ^ shift) for i in range(lax.axis_size(axis))])
 
+    operands = (
+        counts.reshape(1, games),
+        hidden,
+        key_value_codes[0],
+        key_value_scales[0].T,
+        learner.transpose(0, 2, 1),
+        token_ids,
+    )
     load, named = pl.pallas_call(
         load_kernel,
         out_shape=[
             jax.ShapeDtypeStruct((peers, steps, games * features + 2 * LANES), bf16),
             jax.ShapeDtypeStruct((1, rows), jnp.int32),
         ],
-        in_specs=[HBM] * 6,
-        out_specs=[VMEM] * 2,
-        scratch_shapes=[
-            pltpu.SMEM((games,), jnp.int32),
-            pltpu.VMEM(hidden.shape, bf16),
-            pltpu.VMEM((pair_rows, 2 * KV_HEADS * HEAD), bf16),
-            pltpu.VMEM((2 * KV_HEADS, pair_rows), jnp.float32),
-            pltpu.VMEM((games, 1, steps), jnp.int32),
-            pltpu.VMEM((games, steps), jnp.int32),
-            pltpu.SemaphoreType.DMA((6,)),
-        ],
+        grid=(1,),
+        in_specs=[whole(x.shape) for x in operands],
+        out_specs=[whole((peers, steps, games * features + 2 * LANES)), whole((1, rows))],
         compiler_params=PARAMS,
         name="load",
-    )(
-        far(counts),
-        far(hidden),
-        far(key_value_codes[0]),
-        far(key_value_scales[0].T),
-        far(learner.transpose(0, 2, 1)),
-        far(token_ids),
-    )
+    )(*[far(x) for x in operands])
     came = lax.all_to_all(
         load, "group", split_axis=0, concat_axis=0, tiled=True, axis_index_groups=near
     )

time: 100 us -> 100 us (level)
  no operation moved by 1% of the time
where the time goes in v6:
time: 100 us; the launch traced here: 99.2 us
  starting transfers between devices  52.4 us (52%)
  blocking collectives  26.6 us (27%)
  waiting for transfers between devices  11.1 us (11%)
  Pallas kernels  7.69 us (8%)
    ppermute x9, starting transfers between devices, along(): lax.ppermute(x, axis, [(i, i ^ shift) for i in range(lax.axis_size(axis))])  31.7 us
    all_to_all x1, blocking collectives, per_device(): lax.all_to_all(packed, 'group', split_axis=0, concat_axis=1, tiled=True)  26.6 us
    all_to_all x1, starting transfers between devices, per_device(): lax.all_to_all(load, 'group', split_axis=0, concat_axis=0, tiled=True, ax...  11.8 us
    all_to_all x1, starting transfers between devices, per_device(): parts = lax.all_to_all(part, 'tp', split_axis=0, concat_axis=0, tiled=True)  6.44 us
    ppermute x9, waiting for transfers between devices, along(): lax.ppermute(x, axis, [(i, i ^ shift) for i in range(lax.axis_size(axis))])  6.03 us
    all_to_all x1, waiting for transfers between devices, per_device(): parts = lax.all_to_all(part, 'tp', split_axis=0, concat_axis=0, tiled=True)  3.01 us
    ppermute x1, starting transfers between devices, per_device(): lax.ppermute(jnp.concatenate([keep, got], axis=1), ('group', 'tp'), turn)  2.4 us
    ppermute x1, waiting for transfers between devices, per_device(): lax.ppermute(jnp.concatenate([keep, got], axis=1), ('group', 'tp'), turn)  2.02 us
  transfers between devices with their start and end apart: 12, of which 4 were waited for; matrix products, arithmetic and copies ran while one was open for 0% of the time, Pallas kernels for 4%

profile of v6, /device:TPU:1, one launch (start us, length us, event | category | flops | bytes accessed | tf_op | source)
XLA Modules:
  0.0 99.2 jit_solution(18240144441872647218)
XLA Ops:
  0.6 1.6 %load.1 = (bf16[16,8,896]{2,1,0:T(8,128)(2,1)}, s32[1,16]{1,0:T(1,128)S(1)}) custom-call(s32[1,2]{1,0:T(1,128)} %bitcast.13, bf16[2,8,320]{2,1,0:T(8,128)(2,1)} %hidden_ref.1, bf16[10,1024]{1,0:T(8,128)(2,1)} %bitcast.9, f32[8,10]{1,0:T(8,128)} %bitcast.10, s32[2,1,8]{2,1,0:T(1,128)} %bitcast.12, s32[2,8]{1,0:T(2,128)} %ids_ref.1), custom_call_target="tpu_custom_call" | custom-call | tf_op jit(solution)/shard_map/load/pallas_call | solution.py:389
  2.3 11.8 %all-to-all-start = ((bf16[16,8,896]{2,1,0:T(8,128)(2,1)}), bf16[16,8,896]{2,1,0:T(8,128)(2,1)S(1)}, u32[]{:S(2)}, u32[]{:S(2)}) async-start(bf16[16,8,896]{2,1,0:T(8,128)(2,1)} %get-tuple-element.16), calls=%async_computation | async-start | bytes 458752 | tf_op jit(solution)/shard_map/all_to_all | solution.py:401
  14.1 1.1 %pieces.1 = (bf16[320,128]{1,0:T(8,128)(2,1)S(1)}, bf16[2,4,2,16,128]{4,3,2,1,0:T(8,128)(2,1)S(1)}, bf16[2,4,2,16,128]{4,3,2,1,0:T(8,128)(2,1)S(1)}, bf16[2,4,2,...) custom-call(bf16[320,128]{1,0:T(8,128)(2,1)} %codes_hbm.1, f32[1,320]{1,0:T(1,128)} %bitcast.11, ...), custom_call_target="tpu_custom_call" | custom-call | tf_op jit(solution)/shard_map/pieces/pallas_call | solution.py:406
  15.2 7.5 %collective-permute-start = (bf16[320,128]{1,0:T(8,128)(2,1)S(1)}, bf16[320,128]{1,0:T(8,128)(2,1)S(1)}, u32[]{:S(2)}, u32[]{:S(2)}) collective-permute-start(bf16[320,128]{1,0:T(8,128)(2,1)S(1)} %get-tuple-element.17.mine_ref), channel_id=1, source_target_pairs={{0,32},{16,48},{32,0},{48,16},{64,96},{80,112},{96,64},{112,80},{1... | collective-permute-start | bytes 245768 | tf_op jit(solution)/shard_map/ppermute | solution.py:379
  22.7 2.3 %collective-permute-start.2 = (bf16[2,4,2,16,128]{4,3,2,1,0:T(8,128)(2,1)S(1)}, bf16[2,4,2,16,128]{4,3,2,1,0:T(8,128)(2,1)S(1)}, u32[]{:S(2)}, u32[]{:S(2)}) collective-permute-start(bf16[2,4,2,16,128]{4,3,2,1,0:T(8,128)(2,1)S(1)} %get-tuple-element.21), channel_id=1, source_target_pairs={{0,4},{1,5},{2,6},{3,7},{4,0},{5,1},{6,2},{7,3},{8,12},{9,13},{10,... | collective-permute-start | bytes 196616 | tf_op jit(solution)/shard_map/ppermute | solution.py:379
  25.0 2.4 %collective-permute-start.3 = (bf16[2,4,2,16,128]{4,3,2,1,0:T(8,128)(2,1)S(1)}, bf16[2,4,2,16,128]{4,3,2,1,0:T(8,128)(2,1)S(1)}, u32[]{:S(2)}, u32[]{:S(2)}) collective-permute-start(bf16[2,4,2,16,128]{4,3,2,1,0:T(8,128)(2,1)S(1)} %get-tuple-element.22), channel_id=1, source_target_pairs={{0,8},{1,9},{2,10},{3,11},{4,12},{5,13},{6,14},{7,15},{8,0},{9,1},... | collective-permute-start | bytes 196616 | tf_op jit(solution)/shard_map/ppermute | solution.py:379
  27.5 4.5 %collective-permute-start.4 = (bf16[2,4,2,16,128]{4,3,2,1,0:T(8,128)(2,1)S(1)}, bf16[2,4,2,16,128]{4,3,2,1,0:T(8,128)(2,1)S(1)}, u32[]{:S(2)}, u32[]{:S(2)}) collective-permute-start(bf16[2,4,2,16,128]{4,3,2,1,0:T(8,128)(2,1)S(1)} %get-tuple-element.23), channel_id=1, source_target_pairs={{0,12},{1,13},{2,14},{3,15},{4,8},{5,9},{6,10},{7,11},{8,4},{9,5},... | collective-permute-start | bytes 196616 | tf_op jit(solution)/shard_map/ppermute | solution.py:379
  32.1 1.9 %collective-permute-start.1 = (bf16[2,128,128]{2,1,0:T(8,128)(2,1)S(1)}, bf16[2,128,128]{2,1,0:T(8,128)(2,1)S(1)}, u32[]{:S(2)}, u32[]{:S(2)}) collective-permute-start(bf16[2,128,128]{2,1,0:T(8,128)(2,1)S(1)} %swap.1), channel_id=1, source_target_pairs={{0,32},{16,48},{32,0},{48,16},{64,96},{80,112},{96,64},{112,80},{1... | collective-permute-start | bytes 196616 | tf_op jit(solution)/shard_map/ppermute | solution.py:379
  34.0 1.7 %part.1 = (f32[16,16,256]{2,1,0:T(8,128)S(1)}, f32[16,16,128]{2,1,0:T(8,128)S(1)}, bf16[256,256]{1,0:T(8,128)(2,1)S(1)}) custom-call(bf16[16,8,896]{2,1,0:T(8,128)(2,1)S(1)} %all-to-all-done.came_ref, bf16[320,128]{1,0:T(8,128)(2,1)S(1)} %get-tuple-element.17.mine_ref, bf16[320,128]{1,0:T(8,128)(2,1)S(1)} %collective-permute-done.other_ref, ...), custom_call_target="tpu_custom_call" | custom-call | tf_op jit(solution)/shard_map/part/pallas_call | solution.py:434
  35.8 5.2 %collective-permute-done.1.other_ref = bf16[2,128,128]{2,1,0:T(8,128)(2,1)S(1)} collective-permute-done((bf16[2,128,128]{2,1,0:T(8,128)(2,1)S(1)}, bf16[2,128,128]{2,1,0:T(8,128)(2,1)S(1)}, u32[]{:S(2)}, u32[]{:S(2)}) %collective-permute-start.1) | collective-permute-done | bytes 65568 | tf_op jit(solution)/shard_map/ppermute | solution.py:379
  41.0 0.9 whole.1.after_ref
  41.9 6.4 %all-to-all-start.1 = ((f32[16,16,384]{2,1,0:T(8,128)}), f32[16,16,384]{2,1,0:T(8,128)S(1)}, u32[]{:S(2)}, u32[]{:S(2)}) async-start(f32[16,16,384]{2,1,0:T(8,128)} %whole.1.after_ref), calls=%async_computation.1 | async-start | bytes 786432 | tf_op jit(solution)/shard_map/all_to_all | solution.py:458
  48.4 4.5 %collective-permute-start.9 = (bf16[4,2,4,2,16,128]{5,4,3,2,1,0:T(8,128)(2,1)S(1)}, bf16[4,2,4,2,16,128]{5,4,3,2,1,0:T(8,128)(2,1)S(1)}, u32[]{:S(2)}, u32[]{:S(2)}) collective-permute-start(bf16[4,2,4,2,16,128]{5,4,3,2,1,0:T(8,128)(2,1)S(1)} %join.1.shard0_ref), channel_id=1, source_target_pairs={{0,3},{1,2},{2,1},{3,0},{4,7},{5,6},{6,5},{7,4},{8,11},{9,10},{10,... | collective-permute-start | bytes 786440 | tf_op jit(solution)/shard_map/ppermute | solution.py:379
  52.9 2.5 %collective-permute-start.8 = (bf16[4,2,4,2,16,128]{5,4,3,2,1,0:T(8,128)(2,1)S(1)}, bf16[4,2,4,2,16,128]{5,4,3,2,1,0:T(8,128)(2,1)S(1)}, u32[]{:S(2)}, u32[]{:S(2)}) collective-permute-start(bf16[4,2,4,2,16,128]{5,4,3,2,1,0:T(8,128)(2,1)S(1)} %join.1.shard0_ref), channel_id=1, source_target_pairs={{0,2},{1,3},{2,0},{3,1},{4,6},{5,7},{6,4},{7,5},{8,10},{9,11},{10,... | collective-permute-start | bytes 786440 | tf_op jit(solution)/shard_map/ppermute | solution.py:379
  55.4 2.0 %collective-permute-start.7 = (bf16[4,2,4,2,16,128]{5,4,3,2,1,0:T(8,128)(2,1)S(1)}, bf16[4,2,4,2,16,128]{5,4,3,2,1,0:T(8,128)(2,1)S(1)}, u32[]{:S(2)}, u32[]{:S(2)}) collective-permute-start(bf16[4,2,4,2,16,128]{5,4,3,2,1,0:T(8,128)(2,1)S(1)} %join.1.shard0_ref), channel_id=1, source_target_pairs={{0,1},{1,0},{2,3},{3,2},{4,5},{5,4},{6,7},{7,6},{8,9},{9,8},{10,11... | collective-permute-start | bytes 786440 | tf_op jit(solution)/shard_map/ppermute | solution.py:379
  57.4 3.0 %all-to-all-done.1.parts_ref.after_ref = f32[16,16,384]{2,1,0:T(8,128)S(1)} async-done(((f32[16,16,384]{2,1,0:T(8,128)}), f32[16,16,384]{2,1,0:T(8,128)S(1)}, u32[]{:S(2)}, u32[]{:S(2)}) %all-to-all-start.1) | async-done | bytes 393248 | tf_op jit(solution)/shard_map/all_to_all | solution.py:458
  60.4 4.1 %collective-permute-start.5 = (bf16[16,256]{1,0:T(8,128)(2,1)S(1)}, bf16[16,256]{1,0:T(8,128)(2,1)S(1)}, u32[]{:S(2)}, u32[]{:S(2)}) collective-permute-start(bf16[16,256]{1,0:T(8,128)(2,1)S(1)} %get-tuple-element.25), channel_id=1, source_target_pairs={{0,16},{16,0},{32,48},{48,32},{64,80},{80,64},{96,112},{112,96},{1... | collective-permute-start | bytes 24584 | tf_op jit(solution)/shard_map/ppermute | solution.py:379
  64.5 0.8 collective-permute-done.5
  65.3 2.4 %collective-permute-start.6 = (bf16[16,512]{1,0:T(8,128)(2,1)S(1)}, bf16[16,512]{1,0:T(8,128)(2,1)S(1)}, u32[]{:S(2)}, u32[]{:S(2)}) collective-permute-start(bf16[16,512]{1,0:T(8,128)(2,1)S(1)} %pad_maximum_fusion), channel_id=1, source_target_pairs={{0,0},{1,16},{2,64},{3,80},{4,128},{5,144},{6,192},{7,208},{8,256}... | collective-permute-start | bytes 49160 | tf_op jit(solution)/shard_map/ppermute | solution.py:480
  67.7 0.8 facts.1
  68.5 2.0 %collective-permute-done.6.mine_ref = bf16[16,512]{1,0:T(8,128)(2,1)S(1)} collective-permute-done((bf16[16,512]{1,0:T(8,128)(2,1)S(1)}, bf16[16,512]{1,0:T(8,128)(2,1)S(1)}, u32[]{:S(2)}, u32[]{:S(2)}) %collective-permute-start.6) | collective-permute-done | bytes 16416 | tf_op jit(solution)/shard_map/ppermute | solution.py:480
  70.5 1.4 %attend.1 = bf16[32,2,256]{2,1,0:T(2,128)(2,1)S(1)} custom-call(s32[2]{0:T(128)S(1)} %copy-done, bf16[16,512]{1,0:T(8,128)(2,1)S(1)} %collective-permute-done.6.mine_ref, bf16[64,16]{1,0:T(8,128)(2,1)S(1)} %get-tuple-element.27.placed_ref, bf16[4,2,4,2,16,128]{5,4,3,2,1,0:T(8,128)(2,1)S(1)} %join.1.shard0_ref, ...), custom_call_target="tpu_custom_call" | custom-call | tf_op jit(solution)/shard_map/attend/pallas_call | solution.py:494
  72.0 26.6 %all_to_all.22 = bf16[32,2,256]{2,1,0:T(2,128)(2,1)S(1)} all-to-all(bf16[32,2,256]{2,1,0:T(2,128)(2,1)S(1)} %attend.1), channel_id=1, replica_groups=mesh['group'=32,'tp'=16] {'group'}, dimensions={0} | all-to-all | bytes 65536 | tf_op jit(solution)/shard_map/all_to_all | solution.py:502
  98.6 0.6 all_to_all.18
  (14 shorter events, 0.1 us)
Async XLA Ops:
  2.3 29.7 %all-to-all-start = ((bf16[16,8,896]{2,1,0:T(8,128)(2,1)}), bf16[16,8,896]{2,1,0:T(8,128)(2,1)S(1)}, u32[]{:S(2)}, u32[]{:S(2)}) async-start(bf16[16,8,896]{2,1,0:T(8,128)(2,1)} %get-tuple-element.16), calls=%async_computation | async-start | bytes 458752 | tf_op jit(solution)/shard_map/all_to_all | solution.py:401
  15.2 18.8 %collective-permute-start = (bf16[320,128]{1,0:T(8,128)(2,1)S(1)}, bf16[320,128]{1,0:T(8,128)(2,1)S(1)}, u32[]{:S(2)}, u32[]{:S(2)}) collective-permute-start(bf16[320,128]{1,0:T(8,128)(2,1)S(1)} %get-tuple-element.17.mine_ref), channel_id=1, source_target_pairs={{0,32},{16,48},{32,0},{48,16},{64,96},{80,112},{96,64},{112,80},{1... | collective-permute-start | bytes 245768 | tf_op jit(solution)/shard_map/ppermute | solution.py:379
  22.7 13.0 %collective-permute-start.2 = (bf16[2,4,2,16,128]{4,3,2,1,0:T(8,128)(2,1)S(1)}, bf16[2,4,2,16,128]{4,3,2,1,0:T(8,128)(2,1)S(1)}, u32[]{:S(2)}, u32[]{:S(2)}) collective-permute-start(bf16[2,4,2,16,128]{4,3,2,1,0:T(8,128)(2,1)S(1)} %get-tuple-element.21), channel_id=1, source_target_pairs={{0,4},{1,5},{2,6},{3,7},{4,0},{5,1},{6,2},{7,3},{8,12},{9,13},{10,... | collective-permute-start | bytes 196616 | tf_op jit(solution)/shard_map/ppermute | solution.py:379
  25.0 10.7 %collective-permute-start.3 = (bf16[2,4,2,16,128]{4,3,2,1,0:T(8,128)(2,1)S(1)}, bf16[2,4,2,16,128]{4,3,2,1,0:T(8,128)(2,1)S(1)}, u32[]{:S(2)}, u32[]{:S(2)}) collective-permute-start(bf16[2,4,2,16,128]{4,3,2,1,0:T(8,128)(2,1)S(1)} %get-tuple-element.22), channel_id=1, source_target_pairs={{0,8},{1,9},{2,10},{3,11},{4,12},{5,13},{6,14},{7,15},{8,0},{9,1},... | collective-permute-start | bytes 196616 | tf_op jit(solution)/shard_map/ppermute | solution.py:379
  27.5 8.3 %collective-permute-start.4 = (bf16[2,4,2,16,128]{4,3,2,1,0:T(8,128)(2,1)S(1)}, bf16[2,4,2,16,128]{4,3,2,1,0:T(8,128)(2,1)S(1)}, u32[]{:S(2)}, u32[]{:S(2)}) collective-permute-start(bf16[2,4,2,16,128]{4,3,2,1,0:T(8,128)(2,1)S(1)} %get-tuple-element.23), channel_id=1, source_target_pairs={{0,12},{1,13},{2,14},{3,15},{4,8},{5,9},{6,10},{7,11},{8,4},{9,5},... | collective-permute-start | bytes 196616 | tf_op jit(solution)/shard_map/ppermute | solution.py:379
  32.1 8.9 %collective-permute-start.1 = (bf16[2,128,128]{2,1,0:T(8,128)(2,1)S(1)}, bf16[2,128,128]{2,1,0:T(8,128)(2,1)S(1)}, u32[]{:S(2)}, u32[]{:S(2)}) collective-permute-start(bf16[2,128,128]{2,1,0:T(8,128)(2,1)S(1)} %swap.1), channel_id=1, source_target_pairs={{0,32},{16,48},{32,0},{48,16},{64,96},{80,112},{96,64},{112,80},{1... | collective-permute-start | bytes 196616 | tf_op jit(solution)/shard_map/ppermute | solution.py:379
  35.7 34.8 %copy-start = (s32[2]{0:T(128)S(1)}, s32[2]{0:T(128)}, u32[]{:S(2)}) copy-start(s32[2]{0:T(128)} %lengths_ref.1) | copy-start | bytes 28
  41.9 18.5 %all-to-all-start.1 = ((f32[16,16,384]{2,1,0:T(8,128)}), f32[16,16,384]{2,1,0:T(8,128)S(1)}, u32[]{:S(2)}, u32[]{:S(2)}) async-start(f32[16,16,384]{2,1,0:T(8,128)} %whole.1.after_ref), calls=%async_computation.1 | async-start | bytes 786432 | tf_op jit(solution)/shard_map/all_to_all | solution.py:458
  48.4 20.1 %collective-permute-start.9 = (bf16[4,2,4,2,16,128]{5,4,3,2,1,0:T(8,128)(2,1)S(1)}, bf16[4,2,4,2,16,128]{5,4,3,2,1,0:T(8,128)(2,1)S(1)}, u32[]{:S(2)}, u32[]{:S(2)}) collective-permute-start(bf16[4,2,4,2,16,128]{5,4,3,2,1,0:T(8,128)(2,1)S(1)} %join.1.shard0_ref), channel_id=1, source_target_pairs={{0,3},{1,2},{2,1},{3,0},{4,7},{5,6},{6,5},{7,4},{8,11},{9,10},{10,... | collective-permute-start | bytes 786440 | tf_op jit(solution)/shard_map/ppermute | solution.py:379
  52.9 15.6 %collective-permute-start.8 = (bf16[4,2,4,2,16,128]{5,4,3,2,1,0:T(8,128)(2,1)S(1)}, bf16[4,2,4,2,16,128]{5,4,3,2,1,0:T(8,128)(2,1)S(1)}, u32[]{:S(2)}, u32[]{:S(2)}) collective-permute-start(bf16[4,2,4,2,16,128]{5,4,3,2,1,0:T(8,128)(2,1)S(1)} %join.1.shard0_ref), channel_id=1, source_target_pairs={{0,2},{1,3},{2,0},{3,1},{4,6},{5,7},{6,4},{7,5},{8,10},{9,11},{10,... | collective-permute-start | bytes 786440 | tf_op jit(solution)/shard_map/ppermute | solution.py:379
  55.4 13.2 %collective-permute-start.7 = (bf16[4,2,4,2,16,128]{5,4,3,2,1,0:T(8,128)(2,1)S(1)}, bf16[4,2,4,2,16,128]{5,4,3,2,1,0:T(8,128)(2,1)S(1)}, u32[]{:S(2)}, u32[]{:S(2)}) collective-permute-start(bf16[4,2,4,2,16,128]{5,4,3,2,1,0:T(8,128)(2,1)S(1)} %join.1.shard0_ref), channel_id=1, source_target_pairs={{0,1},{1,0},{2,3},{3,2},{4,5},{5,4},{6,7},{7,6},{8,9},{9,8},{10,11... | collective-permute-start | bytes 786440 | tf_op jit(solution)/shard_map/ppermute | solution.py:379
  60.4 4.9 %collective-permute-start.5 = (bf16[16,256]{1,0:T(8,128)(2,1)S(1)}, bf16[16,256]{1,0:T(8,128)(2,1)S(1)}, u32[]{:S(2)}, u32[]{:S(2)}) collective-permute-start(bf16[16,256]{1,0:T(8,128)(2,1)S(1)} %get-tuple-element.25), channel_id=1, source_target_pairs={{0,16},{16,0},{32,48},{48,32},{64,80},{80,64},{96,112},{112,96},{1... | collective-permute-start | bytes 24584 | tf_op jit(solution)/shard_map/ppermute | solution.py:379
  65.3 5.2 %collective-permute-start.6 = (bf16[16,512]{1,0:T(8,128)(2,1)S(1)}, bf16[16,512]{1,0:T(8,128)(2,1)S(1)}, u32[]{:S(2)}, u32[]{:S(2)}) collective-permute-start(bf16[16,512]{1,0:T(8,128)(2,1)S(1)} %pad_maximum_fusion), channel_id=1, source_target_pairs={{0,0},{1,16},{2,64},{3,80},{4,128},{5,144},{6,192},{7,208},{8,256}... | collective-permute-start | bytes 49160 | tf_op jit(solution)/shard_map/ppermute | solution.py:480

commit v7 on v6

--- a/solution.py
+++ b/solution.py
@@ -116,7 +116,8 @@
     return cell.reshape(peers * steps, size).astype(jnp.bfloat16)
 
 
-def swap_kernel(came_ref, out_ref):
+def swap_kernel(came_ref, piece_ref, out_ref, next_ref):
+    next_ref[...] = piece_ref[...]
     _, block, lanes = out_ref.shape
     width = came_ref.shape[2]
     for i in range(2):
@@ -417,19 +418,20 @@
         compiler_params=PARAMS,
         name="pieces",
     )(far(query_codes), far(query_scales.T), far(key_cache), far(value_cache))
-    for shift in range(1, KV_HEADS):
+    for shift in range(2, KV_HEADS):
         pieces[shift] = along(pieces[shift], "tp", shift * across)
     query_other = along(query_delta, "group", CORES)
     rows_all = peers * steps
-    other = pl.pallas_call(
+    other, later = pl.pallas_call(
         swap_kernel,
-        out_shape=jax.ShapeDtypeStruct((2, rows_all, LANES), bf16),
-        in_specs=[VMEM],
-        out_specs=VMEM,
+        out_shape=[jax.ShapeDtypeStruct((2, rows_all, LANES), bf16), piece],
+        in_specs=[VMEM] * 2,
+        out_specs=[VMEM] * 2,
         compiler_params=PARAMS,
         name="swap",
-    )(came)
+    )(came, pieces[1])
     other = along(other, "group", CORES)
+    pieces[1] = along(later, "tp", across)
 
     queries, pairs, spread = pl.pallas_call(
         part_kernel,

time: 100 us -> 98.4 us (0.984)
  waiting for transfers between devices: 11.1 us -> 6.68 us
  blocking collectives: 26.6 us -> 28.3 us
  starting transfers between devices: 52.4 us -> 53.5 us
    ppermute x9, starting transfers between devices: 31.7 us -> 34.8 us  [along(): lax.ppermute(x, axis, [(i, i ^ shift) for i in range(lax.axis_size(axis))])]
    ppermute x9, waiting for transfers between devices: 6.03 us -> 3.59 us  [along(): lax.ppermute(x, axis, [(i, i ^ shift) for i in range(lax.axis_size(axis))])]
    all_to_all x1, starting transfers between devices: 6.44 us -> 4.53 us  [per_device(): parts = lax.all_to_all(part, 'tp', split_axis=0, concat_axis=0, tiled=True)]
    all_to_all x1, waiting for transfers between devices: 3.01 us -> 1.25 us  [per_device(): parts = lax.all_to_all(part, 'tp', split_axis=0, concat_axis=0, tiled=True)]
    all_to_all x1, blocking collectives: 26.6 us -> 28.3 us  [per_device(): lax.all_to_all(packed, 'group', split_axis=0, concat_axis=1, tiled=True)]
where the time goes in v7:
time: 98.4 us; the launch traced here: 97.7 us
  starting transfers between devices  53.5 us (54%)
  blocking collectives  28.3 us (29%)
  Pallas kernels  7.71 us (8%)
  waiting for transfers between devices  6.68 us (7%)
    ppermute x9, starting transfers between devices, along(): lax.ppermute(x, axis, [(i, i ^ shift) for i in range(lax.axis_size(axis))])  34.8 us
    all_to_all x1, blocking collectives, per_device(): lax.all_to_all(packed, 'group', split_axis=0, concat_axis=1, tiled=True)  28.3 us
    all_to_all x1, starting transfers between devices, per_device(): lax.all_to_all(load, 'group', split_axis=0, concat_axis=0, tiled=True, ax...  11.8 us
    all_to_all x1, starting transfers between devices, per_device(): parts = lax.all_to_all(part, 'tp', split_axis=0, concat_axis=0, tiled=True)  4.53 us
    ppermute x9, waiting for transfers between devices, along(): lax.ppermute(x, axis, [(i, i ^ shift) for i in range(lax.axis_size(axis))])  3.59 us
    ppermute x1, starting transfers between devices, per_device(): lax.ppermute(jnp.concatenate([keep, got], axis=1), ('group', 'tp'), turn)  2.41 us
  transfers between devices with their start and end apart: 12, of which 4 were waited for; matrix products, arithmetic and copies ran while one was open for 0% of the time, Pallas kernels for 4%

profile of v7, /device:TPU:1, one launch (start us, length us, event | category | flops | bytes accessed | tf_op | source)
XLA Modules:
  0.0 97.7 jit_solution(3293734340516261783)
XLA Ops:
  0.6 1.7 %load.1 = (bf16[16,8,896]{2,1,0:T(8,128)(2,1)}, s32[1,16]{1,0:T(1,128)S(1)}) custom-call(s32[1,2]{1,0:T(1,128)} %bitcast.13, bf16[2,8,320]{2,1,0:T(8,128)(2,1)} %hidden_ref.1, bf16[10,1024]{1,0:T(8,128)(2,1)} %bitcast.9, f32[8,10]{1,0:T(8,128)} %bitcast.10, s32[2,1,8]{2,1,0:T(1,128)} %bitcast.12, s32[2,8]{1,0:T(2,128)} %ids_ref.1), custom_call_target="tpu_custom_call" | custom-call | tf_op jit(solution)/shard_map/load/pallas_call | solution.py:390
  2.3 11.8 %all-to-all-start = ((bf16[16,8,896]{2,1,0:T(8,128)(2,1)}), bf16[16,8,896]{2,1,0:T(8,128)(2,1)S(1)}, u32[]{:S(2)}, u32[]{:S(2)}) async-start(bf16[16,8,896]{2,1,0:T(8,128)(2,1)} %get-tuple-element.18), calls=%async_computation | async-start | bytes 458752 | tf_op jit(solution)/shard_map/all_to_all | solution.py:402
  14.1 1.1 %pieces.1 = (bf16[320,128]{1,0:T(8,128)(2,1)S(1)}, bf16[2,4,2,16,128]{4,3,2,1,0:T(8,128)(2,1)S(1)}, bf16[2,4,2,16,128]{4,3,2,1,0:T(8,128)(2,1)S(1)}, bf16[2,4,2,...) custom-call(bf16[320,128]{1,0:T(8,128)(2,1)} %codes_hbm.1, f32[1,320]{1,0:T(1,128)} %bitcast.11, ...), custom_call_target="tpu_custom_call" | custom-call | tf_op jit(solution)/shard_map/pieces/pallas_call | solution.py:407
  15.2 7.5 %collective-permute-start = (bf16[320,128]{1,0:T(8,128)(2,1)S(1)}, bf16[320,128]{1,0:T(8,128)(2,1)S(1)}, u32[]{:S(2)}, u32[]{:S(2)}) collective-permute-start(bf16[320,128]{1,0:T(8,128)(2,1)S(1)} %get-tuple-element.19.mine_ref), channel_id=1, source_target_pairs={{0,32},{16,48},{32,0},{48,16},{64,96},{80,112},{96,64},{112,80},{1... | collective-permute-start | bytes 245768 | tf_op jit(solution)/shard_map/ppermute | solution.py:380
  22.7 2.4 %collective-permute-start.3 = (bf16[2,4,2,16,128]{4,3,2,1,0:T(8,128)(2,1)S(1)}, bf16[2,4,2,16,128]{4,3,2,1,0:T(8,128)(2,1)S(1)}, u32[]{:S(2)}, u32[]{:S(2)}) collective-permute-start(bf16[2,4,2,16,128]{4,3,2,1,0:T(8,128)(2,1)S(1)} %get-tuple-element.26), channel_id=1, source_target_pairs={{0,8},{1,9},{2,10},{3,11},{4,12},{5,13},{6,14},{7,15},{8,0},{9,1},... | collective-permute-start | bytes 196616 | tf_op jit(solution)/shard_map/ppermute | solution.py:380
  25.2 3.9 %collective-permute-start.4 = (bf16[2,4,2,16,128]{4,3,2,1,0:T(8,128)(2,1)S(1)}, bf16[2,4,2,16,128]{4,3,2,1,0:T(8,128)(2,1)S(1)}, u32[]{:S(2)}, u32[]{:S(2)}) collective-permute-start(bf16[2,4,2,16,128]{4,3,2,1,0:T(8,128)(2,1)S(1)} %get-tuple-element.27), channel_id=1, source_target_pairs={{0,12},{1,13},{2,14},{3,15},{4,8},{5,9},{6,10},{7,11},{8,4},{9,5},... | collective-permute-start | bytes 196616 | tf_op jit(solution)/shard_map/ppermute | solution.py:380
  29.1 3.9 %collective-permute-start.1 = (bf16[2,128,128]{2,1,0:T(8,128)(2,1)S(1)}, bf16[2,128,128]{2,1,0:T(8,128)(2,1)S(1)}, u32[]{:S(2)}, u32[]{:S(2)}) collective-permute-start(bf16[2,128,128]{2,1,0:T(8,128)(2,1)S(1)} %get-tuple-element.24), channel_id=1, source_target_pairs={{0,32},{16,48},{32,0},{48,16},{64,96},{80,112},{96,64},{112,80},{1... | collective-permute-start | bytes 196616 | tf_op jit(solution)/shard_map/ppermute | solution.py:380
  33.0 2.3 %collective-permute-start.2 = (bf16[2,4,2,16,128]{4,3,2,1,0:T(8,128)(2,1)S(1)}, bf16[2,4,2,16,128]{4,3,2,1,0:T(8,128)(2,1)S(1)}, u32[]{:S(2)}, u32[]{:S(2)}) collective-permute-start(bf16[2,4,2,16,128]{4,3,2,1,0:T(8,128)(2,1)S(1)} %get-tuple-element.25), channel_id=1, source_target_pairs={{0,4},{1,5},{2,6},{3,7},{4,0},{5,1},{6,2},{7,3},{8,12},{9,13},{10,... | collective-permute-start | bytes 196616 | tf_op jit(solution)/shard_map/ppermute | solution.py:380
  35.3 1.7 %part.1 = (f32[16,16,256]{2,1,0:T(8,128)S(1)}, f32[16,16,128]{2,1,0:T(8,128)S(1)}, bf16[256,256]{1,0:T(8,128)(2,1)S(1)}) custom-call(bf16[16,8,896]{2,1,0:T(8,128)(2,1)S(1)} %all-to-all-done.came_ref, bf16[320,128]{1,0:T(8,128)(2,1)S(1)} %get-tuple-element.19.mine_ref, bf16[320,128]{1,0:T(8,128)(2,1)S(1)} %collective-permute-done.other_ref, ...), custom_call_target="tpu_custom_call" | custom-call | tf_op jit(solution)/shard_map/part/pallas_call | solution.py:436
  37.0 2.8 %collective-permute-done.1.other_ref = bf16[2,128,128]{2,1,0:T(8,128)(2,1)S(1)} collective-permute-done((bf16[2,128,128]{2,1,0:T(8,128)(2,1)S(1)}, bf16[2,128,128]{2,1,0:T(8,128)(2,1)S(1)}, u32[]{:S(2)}, u32[]{:S(2)}) %collective-permute-start.1) | collective-permute-done | bytes 65568 | tf_op jit(solution)/shard_map/ppermute | solution.py:380
  39.8 0.9 whole.1.after_ref
  40.7 4.5 %all-to-all-start.1 = ((f32[16,16,384]{2,1,0:T(8,128)}), f32[16,16,384]{2,1,0:T(8,128)S(1)}, u32[]{:S(2)}, u32[]{:S(2)}) async-start(f32[16,16,384]{2,1,0:T(8,128)} %whole.1.after_ref), calls=%async_computation.1 | async-start | bytes 786432 | tf_op jit(solution)/shard_map/all_to_all | solution.py:460
  45.3 4.5 %collective-permute-start.9 = (bf16[4,2,4,2,16,128]{5,4,3,2,1,0:T(8,128)(2,1)S(1)}, bf16[4,2,4,2,16,128]{5,4,3,2,1,0:T(8,128)(2,1)S(1)}, u32[]{:S(2)}, u32[]{:S(2)}) collective-permute-start(bf16[4,2,4,2,16,128]{5,4,3,2,1,0:T(8,128)(2,1)S(1)} %join.1.shard0_ref), channel_id=1, source_target_pairs={{0,3},{1,2},{2,1},{3,0},{4,7},{5,6},{6,5},{7,4},{8,11},{9,10},{10,... | collective-permute-start | bytes 786440 | tf_op jit(solution)/shard_map/ppermute | solution.py:380
  49.8 2.5 %collective-permute-start.8 = (bf16[4,2,4,2,16,128]{5,4,3,2,1,0:T(8,128)(2,1)S(1)}, bf16[4,2,4,2,16,128]{5,4,3,2,1,0:T(8,128)(2,1)S(1)}, u32[]{:S(2)}, u32[]{:S(2)}) collective-permute-start(bf16[4,2,4,2,16,128]{5,4,3,2,1,0:T(8,128)(2,1)S(1)} %join.1.shard0_ref), channel_id=1, source_target_pairs={{0,2},{1,3},{2,0},{3,1},{4,6},{5,7},{6,4},{7,5},{8,10},{9,11},{10,... | collective-permute-start | bytes 786440 | tf_op jit(solution)/shard_map/ppermute | solution.py:380
  52.3 2.0 %collective-permute-start.7 = (bf16[4,2,4,2,16,128]{5,4,3,2,1,0:T(8,128)(2,1)S(1)}, bf16[4,2,4,2,16,128]{5,4,3,2,1,0:T(8,128)(2,1)S(1)}, u32[]{:S(2)}, u32[]{:S(2)}) collective-permute-start(bf16[4,2,4,2,16,128]{5,4,3,2,1,0:T(8,128)(2,1)S(1)} %join.1.shard0_ref), channel_id=1, source_target_pairs={{0,1},{1,0},{2,3},{3,2},{4,5},{5,4},{6,7},{7,6},{8,9},{9,8},{10,11... | collective-permute-start | bytes 786440 | tf_op jit(solution)/shard_map/ppermute | solution.py:380
  54.3 1.2 %all-to-all-done.1.parts_ref.after_ref = f32[16,16,384]{2,1,0:T(8,128)S(1)} async-done(((f32[16,16,384]{2,1,0:T(8,128)}), f32[16,16,384]{2,1,0:T(8,128)S(1)}, u32[]{:S(2)}, u32[]{:S(2)}) %all-to-all-start.1) | async-done | bytes 393248 | tf_op jit(solution)/shard_map/all_to_all | solution.py:460
  55.6 5.8 %collective-permute-start.5 = (bf16[16,256]{1,0:T(8,128)(2,1)S(1)}, bf16[16,256]{1,0:T(8,128)(2,1)S(1)}, u32[]{:S(2)}, u32[]{:S(2)}) collective-permute-start(bf16[16,256]{1,0:T(8,128)(2,1)S(1)} %get-tuple-element.29), channel_id=1, source_target_pairs={{0,16},{16,0},{32,48},{48,32},{64,80},{80,64},{96,112},{112,96},{1... | collective-permute-start | bytes 24584 | tf_op jit(solution)/shard_map/ppermute | solution.py:380
  61.4 0.8 collective-permute-done.5
  62.2 2.4 %collective-permute-start.6 = (bf16[16,512]{1,0:T(8,128)(2,1)S(1)}, bf16[16,512]{1,0:T(8,128)(2,1)S(1)}, u32[]{:S(2)}, u32[]{:S(2)}) collective-permute-start(bf16[16,512]{1,0:T(8,128)(2,1)S(1)} %pad_maximum_fusion), channel_id=1, source_target_pairs={{0,0},{1,16},{2,64},{3,80},{4,128},{5,144},{6,192},{7,208},{8,256}... | collective-permute-start | bytes 49160 | tf_op jit(solution)/shard_map/ppermute | solution.py:482
  64.7 0.8 facts.1
  65.4 1.8 %collective-permute-done.6.mine_ref = bf16[16,512]{1,0:T(8,128)(2,1)S(1)} collective-permute-done((bf16[16,512]{1,0:T(8,128)(2,1)S(1)}, bf16[16,512]{1,0:T(8,128)(2,1)S(1)}, u32[]{:S(2)}, u32[]{:S(2)}) %collective-permute-start.6) | collective-permute-done | bytes 16416 | tf_op jit(solution)/shard_map/ppermute | solution.py:482
  67.3 1.4 %attend.1 = bf16[32,2,256]{2,1,0:T(2,128)(2,1)S(1)} custom-call(s32[2]{0:T(128)S(1)} %copy-done, bf16[16,512]{1,0:T(8,128)(2,1)S(1)} %collective-permute-done.6.mine_ref, bf16[64,16]{1,0:T(8,128)(2,1)S(1)} %get-tuple-element.31.placed_ref, bf16[4,2,4,2,16,128]{5,4,3,2,1,0:T(8,128)(2,1)S(1)} %join.1.shard0_ref, ...), custom_call_target="tpu_custom_call" | custom-call | tf_op jit(solution)/shard_map/attend/pallas_call | solution.py:496
  68.7 28.3 %all_to_all.22 = bf16[32,2,256]{2,1,0:T(2,128)(2,1)S(1)} all-to-all(bf16[32,2,256]{2,1,0:T(2,128)(2,1)S(1)} %attend.1), channel_id=1, replica_groups=mesh['group'=32,'tp'=16] {'group'}, dimensions={0} | all-to-all | bytes 65536 | tf_op jit(solution)/shard_map/all_to_all | solution.py:504
  97.0 0.6 all_to_all.18
  (14 shorter events, 0.1 us)
Async XLA Ops:
  2.3 26.8 %all-to-all-start = ((bf16[16,8,896]{2,1,0:T(8,128)(2,1)}), bf16[16,8,896]{2,1,0:T(8,128)(2,1)S(1)}, u32[]{:S(2)}, u32[]{:S(2)}) async-start(bf16[16,8,896]{2,1,0:T(8,128)(2,1)} %get-tuple-element.18), calls=%async_computation | async-start | bytes 458752 | tf_op jit(solution)/shard_map/all_to_all | solution.py:402
  15.2 20.0 %collective-permute-start = (bf16[320,128]{1,0:T(8,128)(2,1)S(1)}, bf16[320,128]{1,0:T(8,128)(2,1)S(1)}, u32[]{:S(2)}, u32[]{:S(2)}) collective-permute-start(bf16[320,128]{1,0:T(8,128)(2,1)S(1)} %get-tuple-element.19.mine_ref), channel_id=1, source_target_pairs={{0,32},{16,48},{32,0},{48,16},{64,96},{80,112},{96,64},{112,80},{1... | collective-permute-start | bytes 245768 | tf_op jit(solution)/shard_map/ppermute | solution.py:380
  22.7 14.3 %collective-permute-start.3 = (bf16[2,4,2,16,128]{4,3,2,1,0:T(8,128)(2,1)S(1)}, bf16[2,4,2,16,128]{4,3,2,1,0:T(8,128)(2,1)S(1)}, u32[]{:S(2)}, u32[]{:S(2)}) collective-permute-start(bf16[2,4,2,16,128]{4,3,2,1,0:T(8,128)(2,1)S(1)} %get-tuple-element.26), channel_id=1, source_target_pairs={{0,8},{1,9},{2,10},{3,11},{4,12},{5,13},{6,14},{7,15},{8,0},{9,1},... | collective-permute-start | bytes 196616 | tf_op jit(solution)/shard_map/ppermute | solution.py:380
  25.2 11.9 %collective-permute-start.4 = (bf16[2,4,2,16,128]{4,3,2,1,0:T(8,128)(2,1)S(1)}, bf16[2,4,2,16,128]{4,3,2,1,0:T(8,128)(2,1)S(1)}, u32[]{:S(2)}, u32[]{:S(2)}) collective-permute-start(bf16[2,4,2,16,128]{4,3,2,1,0:T(8,128)(2,1)S(1)} %get-tuple-element.27), channel_id=1, source_target_pairs={{0,12},{1,13},{2,14},{3,15},{4,8},{5,9},{6,10},{7,11},{8,4},{9,5},... | collective-permute-start | bytes 196616 | tf_op jit(solution)/shard_map/ppermute | solution.py:380
  29.1 10.7 %collective-permute-start.1 = (bf16[2,128,128]{2,1,0:T(8,128)(2,1)S(1)}, bf16[2,128,128]{2,1,0:T(8,128)(2,1)S(1)}, u32[]{:S(2)}, u32[]{:S(2)}) collective-permute-start(bf16[2,128,128]{2,1,0:T(8,128)(2,1)S(1)} %get-tuple-element.24), channel_id=1, source_target_pairs={{0,32},{16,48},{32,0},{48,16},{64,96},{80,112},{96,64},{112,80},{1... | collective-permute-start | bytes 196616 | tf_op jit(solution)/shard_map/ppermute | solution.py:380
  33.0 6.9 %collective-permute-start.2 = (bf16[2,4,2,16,128]{4,3,2,1,0:T(8,128)(2,1)S(1)}, bf16[2,4,2,16,128]{4,3,2,1,0:T(8,128)(2,1)S(1)}, u32[]{:S(2)}, u32[]{:S(2)}) collective-permute-start(bf16[2,4,2,16,128]{4,3,2,1,0:T(8,128)(2,1)S(1)} %get-tuple-element.25), channel_id=1, source_target_pairs={{0,4},{1,5},{2,6},{3,7},{4,0},{5,1},{6,2},{7,3},{8,12},{9,13},{10,... | collective-permute-start | bytes 196616 | tf_op jit(solution)/shard_map/ppermute | solution.py:380
  37.0 30.3 %copy-start = (s32[2]{0:T(128)S(1)}, s32[2]{0:T(128)}, u32[]{:S(2)}) copy-start(s32[2]{0:T(128)} %lengths_ref.1) | copy-start | bytes 28
  40.7 14.8 %all-to-all-start.1 = ((f32[16,16,384]{2,1,0:T(8,128)}), f32[16,16,384]{2,1,0:T(8,128)S(1)}, u32[]{:S(2)}, u32[]{:S(2)}) async-start(f32[16,16,384]{2,1,0:T(8,128)} %whole.1.after_ref), calls=%async_computation.1 | async-start | bytes 786432 | tf_op jit(solution)/shard_map/all_to_all | solution.py:460
  45.3 20.1 %collective-permute-start.9 = (bf16[4,2,4,2,16,128]{5,4,3,2,1,0:T(8,128)(2,1)S(1)}, bf16[4,2,4,2,16,128]{5,4,3,2,1,0:T(8,128)(2,1)S(1)}, u32[]{:S(2)}, u32[]{:S(2)}) collective-permute-start(bf16[4,2,4,2,16,128]{5,4,3,2,1,0:T(8,128)(2,1)S(1)} %join.1.shard0_ref), channel_id=1, source_target_pairs={{0,3},{1,2},{2,1},{3,0},{4,7},{5,6},{6,5},{7,4},{8,11},{9,10},{10,... | collective-permute-start | bytes 786440 | tf_op jit(solution)/shard_map/ppermute | solution.py:380
  49.8 15.6 %collective-permute-start.8 = (bf16[4,2,4,2,16,128]{5,4,3,2,1,0:T(8,128)(2,1)S(1)}, bf16[4,2,4,2,16,128]{5,4,3,2,1,0:T(8,128)(2,1)S(1)}, u32[]{:S(2)}, u32[]{:S(2)}) collective-permute-start(bf16[4,2,4,2,16,128]{5,4,3,2,1,0:T(8,128)(2,1)S(1)} %join.1.shard0_ref), channel_id=1, source_target_pairs={{0,2},{1,3},{2,0},{3,1},{4,6},{5,7},{6,4},{7,5},{8,10},{9,11},{10,... | collective-permute-start | bytes 786440 | tf_op jit(solution)/shard_map/ppermute | solution.py:380
  52.3 13.2 %collective-permute-start.7 = (bf16[4,2,4,2,16,128]{5,4,3,2,1,0:T(8,128)(2,1)S(1)}, bf16[4,2,4,2,16,128]{5,4,3,2,1,0:T(8,128)(2,1)S(1)}, u32[]{:S(2)}, u32[]{:S(2)}) collective-permute-start(bf16[4,2,4,2,16,128]{5,4,3,2,1,0:T(8,128)(2,1)S(1)} %join.1.shard0_ref), channel_id=1, source_target_pairs={{0,1},{1,0},{2,3},{3,2},{4,5},{5,4},{6,7},{7,6},{8,9},{9,8},{10,11... | collective-permute-start | bytes 786440 | tf_op jit(solution)/shard_map/ppermute | solution.py:380
  55.6 6.6 %collective-permute-start.5 = (bf16[16,256]{1,0:T(8,128)(2,1)S(1)}, bf16[16,256]{1,0:T(8,128)(2,1)S(1)}, u32[]{:S(2)}, u32[]{:S(2)}) collective-permute-start(bf16[16,256]{1,0:T(8,128)(2,1)S(1)} %get-tuple-element.29), channel_id=1, source_target_pairs={{0,16},{16,0},{32,48},{48,32},{64,80},{80,64},{96,112},{112,96},{1... | collective-permute-start | bytes 24584 | tf_op jit(solution)/shard_map/ppermute | solution.py:380
  62.2 5.0 %collective-permute-start.6 = (bf16[16,512]{1,0:T(8,128)(2,1)S(1)}, bf16[16,512]{1,0:T(8,128)(2,1)S(1)}, u32[]{:S(2)}, u32[]{:S(2)}) collective-permute-start(bf16[16,512]{1,0:T(8,128)(2,1)S(1)} %pad_maximum_fusion), channel_id=1, source_target_pairs={{0,0},{1,16},{2,64},{3,80},{4,128},{5,144},{6,192},{7,208},{8,256}... | collective-permute-start | bytes 49160 | tf_op jit(solution)/shard_map/ppermute | solution.py:482

commit v8 on v6

--- a/solution.py
+++ b/solution.py
@@ -116,7 +116,9 @@
     return cell.reshape(peers * steps, size).astype(jnp.bfloat16)
 
 
-def swap_kernel(came_ref, out_ref):
+def swap_kernel(came_ref, piece2_ref, piece1_ref, out_ref, next2_ref, next1_ref):
+    next2_ref[...] = piece2_ref[...]
+    next1_ref[...] = piece1_ref[...]
     _, block, lanes = out_ref.shape
     width = came_ref.shape[2]
     for i in range(2):
@@ -417,19 +419,20 @@
         compiler_params=PARAMS,
         name="pieces",
     )(far(query_codes), far(query_scales.T), far(key_cache), far(value_cache))
-    for shift in range(1, KV_HEADS):
-        pieces[shift] = along(pieces[shift], "tp", shift * across)
+    pieces[3] = along(pieces[3], "tp", 3 * across)
     query_other = along(query_delta, "group", CORES)
     rows_all = peers * steps
-    other = pl.pallas_call(
+    other, *later = pl.pallas_call(
         swap_kernel,
-        out_shape=jax.ShapeDtypeStruct((2, rows_all, LANES), bf16),
-        in_specs=[VMEM],
-        out_specs=VMEM,
+        out_shape=[jax.ShapeDtypeStruct((2, rows_all, LANES), bf16), piece, piece],
+        in_specs=[VMEM] * 3,
+        out_specs=[VMEM] * 3,
         compiler_params=PARAMS,
         name="swap",
-    )(came)
+    )(came, pieces[2], pieces[1])
     other = along(other, "group", CORES)
+    pieces[2] = along(later[0], "tp", 2 * across)
+    pieces[1] = along(later[1], "tp", across)
 
     queries, pairs, spread = pl.pallas_call(
         part_kernel,

time: 100 us -> 99 us (0.990)
  starting transfers between devices: 52.4 us -> 54.6 us
  blocking collectives: 26.6 us -> 24.6 us
  waiting for transfers between devices: 11.1 us -> 9.93 us
    ppermute x9, starting transfers between devices: 31.7 us -> 35.1 us  [along(): lax.ppermute(x, axis, [(i, i ^ shift) for i in range(lax.axis_size(axis))])]
    all_to_all x1, blocking collectives: 26.6 us -> 24.6 us  [per_device(): lax.all_to_all(packed, 'group', split_axis=0, concat_axis=1, tiled=True)]
    all_to_all x1, starting transfers between devices: 6.44 us -> 5.26 us  [per_device(): parts = lax.all_to_all(part, 'tp', split_axis=0, concat_axis=0, tiled=True)]
    ppermute x9, waiting for transfers between devices: 6.03 us -> 4.86 us  [along(): lax.ppermute(x, axis, [(i, i ^ shift) for i in range(lax.axis_size(axis))])]
  transfers between devices with their start and end apart: 12 -> 12, of which waited for: 4 -> 5; matrix products, arithmetic and copies ran while one was open for 0% -> 0% of each run, Pallas kernels for 4% -> 4%
where the time goes in v8:
time: 99 us; the launch traced here: 98.3 us
  starting transfers between devices  54.6 us (55%)
  blocking collectives  24.6 us (25%)
  waiting for transfers between devices  9.93 us (10%)
  Pallas kernels  7.72 us (8%)
    ppermute x9, starting transfers between devices, along(): lax.ppermute(x, axis, [(i, i ^ shift) for i in range(lax.axis_size(axis))])  35.1 us
    all_to_all x1, blocking collectives, per_device(): lax.all_to_all(packed, 'group', split_axis=0, concat_axis=1, tiled=True)  24.6 us
    all_to_all x1, starting transfers between devices, per_device(): lax.all_to_all(load, 'group', split_axis=0, concat_axis=0, tiled=True, ax...  11.8 us
    all_to_all x1, starting transfers between devices, per_device(): parts = lax.all_to_all(part, 'tp', split_axis=0, concat_axis=0, tiled=True)  5.26 us
    ppermute x9, waiting for transfers between devices, along(): lax.ppermute(x, axis, [(i, i ^ shift) for i in range(lax.axis_size(axis))])  4.86 us
    all_to_all x1, waiting for transfers between devices, per_device(): parts = lax.all_to_all(part, 'tp', split_axis=0, concat_axis=0, tiled=True)  2.85 us
    ppermute x1, starting transfers between devices, per_device(): lax.ppermute(jnp.concatenate([keep, got], axis=1), ('group', 'tp'), turn)  2.39 us
    ppermute x1, waiting for transfers between devices, per_device(): lax.ppermute(jnp.concatenate([keep, got], axis=1), ('group', 'tp'), turn)  2.03 us
  transfers between devices with their start and end apart: 12, of which 5 were waited for; matrix products, arithmetic and copies ran while one was open for 0% of the time, Pallas kernels for 4%

profile of v8, /device:TPU:1, one launch (start us, length us, event | category | flops | bytes accessed | tf_op | source)
XLA Modules:
  0.0 98.3 jit_solution(2728759422076319637)
XLA Ops:
  0.6 1.7 %load.1 = (bf16[16,8,896]{2,1,0:T(8,128)(2,1)}, s32[1,16]{1,0:T(1,128)S(1)}) custom-call(s32[1,2]{1,0:T(1,128)} %bitcast.13, bf16[2,8,320]{2,1,0:T(8,128)(2,1)} %hidden_ref.1, bf16[10,1024]{1,0:T(8,128)(2,1)} %bitcast.9, f32[8,10]{1,0:T(8,128)} %bitcast.10, s32[2,1,8]{2,1,0:T(1,128)} %bitcast.12, s32[2,8]{1,0:T(2,128)} %ids_ref.1), custom_call_target="tpu_custom_call" | custom-call | tf_op jit(solution)/shard_map/load/pallas_call | solution.py:391
  2.3 11.8 %all-to-all-start = ((bf16[16,8,896]{2,1,0:T(8,128)(2,1)}), bf16[16,8,896]{2,1,0:T(8,128)(2,1)S(1)}, u32[]{:S(2)}, u32[]{:S(2)}) async-start(bf16[16,8,896]{2,1,0:T(8,128)(2,1)} %get-tuple-element.19), calls=%async_computation | async-start | bytes 458752 | tf_op jit(solution)/shard_map/all_to_all | solution.py:403
  14.1 1.1 %pieces.1 = (bf16[320,128]{1,0:T(8,128)(2,1)S(1)}, bf16[2,4,2,16,128]{4,3,2,1,0:T(8,128)(2,1)S(1)}, bf16[2,4,2,16,128]{4,3,2,1,0:T(8,128)(2,1)S(1)}, bf16[2,4,2,...) custom-call(bf16[320,128]{1,0:T(8,128)(2,1)} %codes_hbm.1, f32[1,320]{1,0:T(1,128)} %bitcast.11, ...), custom_call_target="tpu_custom_call" | custom-call | tf_op jit(solution)/shard_map/pieces/pallas_call | solution.py:408
  15.2 7.5 %collective-permute-start = (bf16[320,128]{1,0:T(8,128)(2,1)S(1)}, bf16[320,128]{1,0:T(8,128)(2,1)S(1)}, u32[]{:S(2)}, u32[]{:S(2)}) collective-permute-start(bf16[320,128]{1,0:T(8,128)(2,1)S(1)} %get-tuple-element.20.mine_ref), channel_id=1, source_target_pairs={{0,32},{16,48},{32,0},{48,16},{64,96},{80,112},{96,64},{112,80},{1... | collective-permute-start | bytes 245768 | tf_op jit(solution)/shard_map/ppermute | solution.py:381
  22.7 2.5 %collective-permute-start.4 = (bf16[2,4,2,16,128]{4,3,2,1,0:T(8,128)(2,1)S(1)}, bf16[2,4,2,16,128]{4,3,2,1,0:T(8,128)(2,1)S(1)}, u32[]{:S(2)}, u32[]{:S(2)}) collective-permute-start(bf16[2,4,2,16,128]{4,3,2,1,0:T(8,128)(2,1)S(1)} %get-tuple-element.29), channel_id=1, source_target_pairs={{0,12},{1,13},{2,14},{3,15},{4,8},{5,9},{6,10},{7,11},{8,4},{9,5},... | collective-permute-start | bytes 196616 | tf_op jit(solution)/shard_map/ppermute | solution.py:381
  25.5 7.5 %collective-permute-start.1 = (bf16[2,128,128]{2,1,0:T(8,128)(2,1)S(1)}, bf16[2,128,128]{2,1,0:T(8,128)(2,1)S(1)}, u32[]{:S(2)}, u32[]{:S(2)}) collective-permute-start(bf16[2,128,128]{2,1,0:T(8,128)(2,1)S(1)} %get-tuple-element.26), channel_id=1, source_target_pairs={{0,32},{16,48},{32,0},{48,16},{64,96},{80,112},{96,64},{112,80},{1... | collective-permute-start | bytes 196616 | tf_op jit(solution)/shard_map/ppermute | solution.py:381
  33.0 2.3 %collective-permute-start.2 = (bf16[2,4,2,16,128]{4,3,2,1,0:T(8,128)(2,1)S(1)}, bf16[2,4,2,16,128]{4,3,2,1,0:T(8,128)(2,1)S(1)}, u32[]{:S(2)}, u32[]{:S(2)}) collective-permute-start(bf16[2,4,2,16,128]{4,3,2,1,0:T(8,128)(2,1)S(1)} %get-tuple-element.27), channel_id=1, source_target_pairs={{0,4},{1,5},{2,6},{3,7},{4,0},{5,1},{6,2},{7,3},{8,12},{9,13},{10,... | collective-permute-start | bytes 196616 | tf_op jit(solution)/shard_map/ppermute | solution.py:381
  35.3 2.1 %collective-permute-start.3 = (bf16[2,4,2,16,128]{4,3,2,1,0:T(8,128)(2,1)S(1)}, bf16[2,4,2,16,128]{4,3,2,1,0:T(8,128)(2,1)S(1)}, u32[]{:S(2)}, u32[]{:S(2)}) collective-permute-start(bf16[2,4,2,16,128]{4,3,2,1,0:T(8,128)(2,1)S(1)} %get-tuple-element.28), channel_id=1, source_target_pairs={{0,8},{1,9},{2,10},{3,11},{4,12},{5,13},{6,14},{7,15},{8,0},{9,1},... | collective-permute-start | bytes 196616 | tf_op jit(solution)/shard_map/ppermute | solution.py:381
  37.4 1.7 %part.1 = (f32[16,16,256]{2,1,0:T(8,128)S(1)}, f32[16,16,128]{2,1,0:T(8,128)S(1)}, bf16[256,256]{1,0:T(8,128)(2,1)S(1)}) custom-call(bf16[16,8,896]{2,1,0:T(8,128)(2,1)S(1)} %all-to-all-done.came_ref, bf16[320,128]{1,0:T(8,128)(2,1)S(1)} %get-tuple-element.20.mine_ref, bf16[320,128]{1,0:T(8,128)(2,1)S(1)} %collective-permute-done.other_ref, ...), custom_call_target="tpu_custom_call" | custom-call | tf_op jit(solution)/shard_map/part/pallas_call | solution.py:437
  39.2 4.0 %collective-permute-done.3.after2_ref.refs_2_ = bf16[2,4,2,16,128]{4,3,2,1,0:T(8,128)(2,1)S(1)} collective-permute-done((bf16[2,4,2,16,128]{4,3,2,1,0:T(8,128)(2,1)S(1)}, bf16[2,4,2,16,128]{4,3,2,1,0:T(8,128)(2,1)S(1)}, u32[]{:S(2)}, u32[]{:S(2)}) %collective-permute-start.3) | collective-permute-done | bytes 65568 | tf_op jit(solution)/shard_map/ppermute | solution.py:381
  43.2 0.9 whole.1.after_ref
  44.2 5.3 %all-to-all-start.1 = ((f32[16,16,384]{2,1,0:T(8,128)}), f32[16,16,384]{2,1,0:T(8,128)S(1)}, u32[]{:S(2)}, u32[]{:S(2)}) async-start(f32[16,16,384]{2,1,0:T(8,128)} %whole.1.after_ref), calls=%async_computation.1 | async-start | bytes 786432 | tf_op jit(solution)/shard_map/all_to_all | solution.py:461
  49.5 4.5 %collective-permute-start.9 = (bf16[4,2,4,2,16,128]{5,4,3,2,1,0:T(8,128)(2,1)S(1)}, bf16[4,2,4,2,16,128]{5,4,3,2,1,0:T(8,128)(2,1)S(1)}, u32[]{:S(2)}, u32[]{:S(2)}) collective-permute-start(bf16[4,2,4,2,16,128]{5,4,3,2,1,0:T(8,128)(2,1)S(1)} %join.1.shard0_ref), channel_id=1, source_target_pairs={{0,3},{1,2},{2,1},{3,0},{4,7},{5,6},{6,5},{7,4},{8,11},{9,10},{10,... | collective-permute-start | bytes 786440 | tf_op jit(solution)/shard_map/ppermute | solution.py:381
  54.0 2.5 %collective-permute-start.8 = (bf16[4,2,4,2,16,128]{5,4,3,2,1,0:T(8,128)(2,1)S(1)}, bf16[4,2,4,2,16,128]{5,4,3,2,1,0:T(8,128)(2,1)S(1)}, u32[]{:S(2)}, u32[]{:S(2)}) collective-permute-start(bf16[4,2,4,2,16,128]{5,4,3,2,1,0:T(8,128)(2,1)S(1)} %join.1.shard0_ref), channel_id=1, source_target_pairs={{0,2},{1,3},{2,0},{3,1},{4,6},{5,7},{6,4},{7,5},{8,10},{9,11},{10,... | collective-permute-start | bytes 786440 | tf_op jit(solution)/shard_map/ppermute | solution.py:381
  56.4 2.0 %collective-permute-start.7 = (bf16[4,2,4,2,16,128]{5,4,3,2,1,0:T(8,128)(2,1)S(1)}, bf16[4,2,4,2,16,128]{5,4,3,2,1,0:T(8,128)(2,1)S(1)}, u32[]{:S(2)}, u32[]{:S(2)}) collective-permute-start(bf16[4,2,4,2,16,128]{5,4,3,2,1,0:T(8,128)(2,1)S(1)} %join.1.shard0_ref), channel_id=1, source_target_pairs={{0,1},{1,0},{2,3},{3,2},{4,5},{5,4},{6,7},{7,6},{8,9},{9,8},{10,11... | collective-permute-start | bytes 786440 | tf_op jit(solution)/shard_map/ppermute | solution.py:381
  58.5 2.8 %all-to-all-done.1.parts_ref.after_ref = f32[16,16,384]{2,1,0:T(8,128)S(1)} async-done(((f32[16,16,384]{2,1,0:T(8,128)}), f32[16,16,384]{2,1,0:T(8,128)S(1)}, u32[]{:S(2)}, u32[]{:S(2)}) %all-to-all-start.1) | async-done | bytes 393248 | tf_op jit(solution)/shard_map/all_to_all | solution.py:461
  61.3 4.2 %collective-permute-start.5 = (bf16[16,256]{1,0:T(8,128)(2,1)S(1)}, bf16[16,256]{1,0:T(8,128)(2,1)S(1)}, u32[]{:S(2)}, u32[]{:S(2)}) collective-permute-start(bf16[16,256]{1,0:T(8,128)(2,1)S(1)} %get-tuple-element.31), channel_id=1, source_target_pairs={{0,16},{16,0},{32,48},{48,32},{64,80},{80,64},{96,112},{112,96},{1... | collective-permute-start | bytes 24584 | tf_op jit(solution)/shard_map/ppermute | solution.py:381
  65.6 0.8 collective-permute-done.5
  66.4 2.4 %collective-permute-start.6 = (bf16[16,512]{1,0:T(8,128)(2,1)S(1)}, bf16[16,512]{1,0:T(8,128)(2,1)S(1)}, u32[]{:S(2)}, u32[]{:S(2)}) collective-permute-start(bf16[16,512]{1,0:T(8,128)(2,1)S(1)} %pad_maximum_fusion), channel_id=1, source_target_pairs={{0,0},{1,16},{2,64},{3,80},{4,128},{5,144},{6,192},{7,208},{8,256}... | collective-permute-start | bytes 49160 | tf_op jit(solution)/shard_map/ppermute | solution.py:483
  68.8 0.8 facts.1
  69.6 2.0 %collective-permute-done.6.mine_ref = bf16[16,512]{1,0:T(8,128)(2,1)S(1)} collective-permute-done((bf16[16,512]{1,0:T(8,128)(2,1)S(1)}, bf16[16,512]{1,0:T(8,128)(2,1)S(1)}, u32[]{:S(2)}, u32[]{:S(2)}) %collective-permute-start.6) | collective-permute-done | bytes 16416 | tf_op jit(solution)/shard_map/ppermute | solution.py:483
  71.6 1.4 %attend.1 = bf16[32,2,256]{2,1,0:T(2,128)(2,1)S(1)} custom-call(s32[2]{0:T(128)S(1)} %copy-done, bf16[16,512]{1,0:T(8,128)(2,1)S(1)} %collective-permute-done.6.mine_ref, bf16[64,16]{1,0:T(8,128)(2,1)S(1)} %get-tuple-element.33.placed_ref, bf16[4,2,4,2,16,128]{5,4,3,2,1,0:T(8,128)(2,1)S(1)} %join.1.shard0_ref, ...), custom_call_target="tpu_custom_call" | custom-call | tf_op jit(solution)/shard_map/attend/pallas_call | solution.py:497
  73.0 24.6 %all_to_all.22 = bf16[32,2,256]{2,1,0:T(2,128)(2,1)S(1)} all-to-all(bf16[32,2,256]{2,1,0:T(2,128)(2,1)S(1)} %attend.1), channel_id=1, replica_groups=mesh['group'=32,'tp'=16] {'group'}, dimensions={0} | all-to-all | bytes 65536 | tf_op jit(solution)/shard_map/all_to_all | solution.py:505
  97.6 0.6 all_to_all.18
  (14 shorter events, 0.3 us)
Async XLA Ops:
  2.3 23.2 %all-to-all-start = ((bf16[16,8,896]{2,1,0:T(8,128)(2,1)}), bf16[16,8,896]{2,1,0:T(8,128)(2,1)S(1)}, u32[]{:S(2)}, u32[]{:S(2)}) async-start(bf16[16,8,896]{2,1,0:T(8,128)(2,1)} %get-tuple-element.19), calls=%async_computation | async-start | bytes 458752 | tf_op jit(solution)/shard_map/all_to_all | solution.py:403
  15.2 22.2 %collective-permute-start = (bf16[320,128]{1,0:T(8,128)(2,1)S(1)}, bf16[320,128]{1,0:T(8,128)(2,1)S(1)}, u32[]{:S(2)}, u32[]{:S(2)}) collective-permute-start(bf16[320,128]{1,0:T(8,128)(2,1)S(1)} %get-tuple-element.20.mine_ref), channel_id=1, source_target_pairs={{0,32},{16,48},{32,0},{48,16},{64,96},{80,112},{96,64},{112,80},{1... | collective-permute-start | bytes 245768 | tf_op jit(solution)/shard_map/ppermute | solution.py:381
  22.7 16.4 %collective-permute-start.4 = (bf16[2,4,2,16,128]{4,3,2,1,0:T(8,128)(2,1)S(1)}, bf16[2,4,2,16,128]{4,3,2,1,0:T(8,128)(2,1)S(1)}, u32[]{:S(2)}, u32[]{:S(2)}) collective-permute-start(bf16[2,4,2,16,128]{4,3,2,1,0:T(8,128)(2,1)S(1)} %get-tuple-element.29), channel_id=1, source_target_pairs={{0,12},{1,13},{2,14},{3,15},{4,8},{5,9},{6,10},{7,11},{8,4},{9,5},... | collective-permute-start | bytes 196616 | tf_op jit(solution)/shard_map/ppermute | solution.py:381
  25.5 13.7 %collective-permute-start.1 = (bf16[2,128,128]{2,1,0:T(8,128)(2,1)S(1)}, bf16[2,128,128]{2,1,0:T(8,128)(2,1)S(1)}, u32[]{:S(2)}, u32[]{:S(2)}) collective-permute-start(bf16[2,128,128]{2,1,0:T(8,128)(2,1)S(1)} %get-tuple-element.26), channel_id=1, source_target_pairs={{0,32},{16,48},{32,0},{48,16},{64,96},{80,112},{96,64},{112,80},{1... | collective-permute-start | bytes 196616 | tf_op jit(solution)/shard_map/ppermute | solution.py:381
  33.0 6.2 %collective-permute-start.2 = (bf16[2,4,2,16,128]{4,3,2,1,0:T(8,128)(2,1)S(1)}, bf16[2,4,2,16,128]{4,3,2,1,0:T(8,128)(2,1)S(1)}, u32[]{:S(2)}, u32[]{:S(2)}) collective-permute-start(bf16[2,4,2,16,128]{4,3,2,1,0:T(8,128)(2,1)S(1)} %get-tuple-element.27), channel_id=1, source_target_pairs={{0,4},{1,5},{2,6},{3,7},{4,0},{5,1},{6,2},{7,3},{8,12},{9,13},{10,... | collective-permute-start | bytes 196616 | tf_op jit(solution)/shard_map/ppermute | solution.py:381
  35.3 8.0 %collective-permute-start.3 = (bf16[2,4,2,16,128]{4,3,2,1,0:T(8,128)(2,1)S(1)}, bf16[2,4,2,16,128]{4,3,2,1,0:T(8,128)(2,1)S(1)}, u32[]{:S(2)}, u32[]{:S(2)}) collective-permute-start(bf16[2,4,2,16,128]{4,3,2,1,0:T(8,128)(2,1)S(1)} %get-tuple-element.28), channel_id=1, source_target_pairs={{0,8},{1,9},{2,10},{3,11},{4,12},{5,13},{6,14},{7,15},{8,0},{9,1},... | collective-permute-start | bytes 196616 | tf_op jit(solution)/shard_map/ppermute | solution.py:381
  39.2 32.4 %copy-start = (s32[2]{0:T(128)S(1)}, s32[2]{0:T(128)}, u32[]{:S(2)}) copy-start(s32[2]{0:T(128)} %lengths_ref.1) | copy-start | bytes 28
  44.2 17.2 %all-to-all-start.1 = ((f32[16,16,384]{2,1,0:T(8,128)}), f32[16,16,384]{2,1,0:T(8,128)S(1)}, u32[]{:S(2)}, u32[]{:S(2)}) async-start(f32[16,16,384]{2,1,0:T(8,128)} %whole.1.after_ref), calls=%async_computation.1 | async-start | bytes 786432 | tf_op jit(solution)/shard_map/all_to_all | solution.py:461
  49.5 20.1 %collective-permute-start.9 = (bf16[4,2,4,2,16,128]{5,4,3,2,1,0:T(8,128)(2,1)S(1)}, bf16[4,2,4,2,16,128]{5,4,3,2,1,0:T(8,128)(2,1)S(1)}, u32[]{:S(2)}, u32[]{:S(2)}) collective-permute-start(bf16[4,2,4,2,16,128]{5,4,3,2,1,0:T(8,128)(2,1)S(1)} %join.1.shard0_ref), channel_id=1, source_target_pairs={{0,3},{1,2},{2,1},{3,0},{4,7},{5,6},{6,5},{7,4},{8,11},{9,10},{10,... | collective-permute-start | bytes 786440 | tf_op jit(solution)/shard_map/ppermute | solution.py:381
  54.0 15.6 %collective-permute-start.8 = (bf16[4,2,4,2,16,128]{5,4,3,2,1,0:T(8,128)(2,1)S(1)}, bf16[4,2,4,2,16,128]{5,4,3,2,1,0:T(8,128)(2,1)S(1)}, u32[]{:S(2)}, u32[]{:S(2)}) collective-permute-start(bf16[4,2,4,2,16,128]{5,4,3,2,1,0:T(8,128)(2,1)S(1)} %join.1.shard0_ref), channel_id=1, source_target_pairs={{0,2},{1,3},{2,0},{3,1},{4,6},{5,7},{6,4},{7,5},{8,10},{9,11},{10,... | collective-permute-start | bytes 786440 | tf_op jit(solution)/shard_map/ppermute | solution.py:381
  56.4 13.1 %collective-permute-start.7 = (bf16[4,2,4,2,16,128]{5,4,3,2,1,0:T(8,128)(2,1)S(1)}, bf16[4,2,4,2,16,128]{5,4,3,2,1,0:T(8,128)(2,1)S(1)}, u32[]{:S(2)}, u32[]{:S(2)}) collective-permute-start(bf16[4,2,4,2,16,128]{5,4,3,2,1,0:T(8,128)(2,1)S(1)} %join.1.shard0_ref), channel_id=1, source_target_pairs={{0,1},{1,0},{2,3},{3,2},{4,5},{5,4},{6,7},{7,6},{8,9},{9,8},{10,11... | collective-permute-start | bytes 786440 | tf_op jit(solution)/shard_map/ppermute | solution.py:381
  61.3 5.0 %collective-permute-start.5 = (bf16[16,256]{1,0:T(8,128)(2,1)S(1)}, bf16[16,256]{1,0:T(8,128)(2,1)S(1)}, u32[]{:S(2)}, u32[]{:S(2)}) collective-permute-start(bf16[16,256]{1,0:T(8,128)(2,1)S(1)} %get-tuple-element.31), channel_id=1, source_target_pairs={{0,16},{16,0},{32,48},{48,32},{64,80},{80,64},{96,112},{112,96},{1... | collective-permute-start | bytes 24584 | tf_op jit(solution)/shard_map/ppermute | solution.py:381
  66.4 5.2 %collective-permute-start.6 = (bf16[16,512]{1,0:T(8,128)(2,1)S(1)}, bf16[16,512]{1,0:T(8,128)(2,1)S(1)}, u32[]{:S(2)}, u32[]{:S(2)}) collective-permute-start(bf16[16,512]{1,0:T(8,128)(2,1)S(1)} %pad_maximum_fusion), channel_id=1, source_target_pairs={{0,0},{1,16},{2,64},{3,80},{4,128},{5,144},{6,192},{7,208},{8,256}... | collective-permute-start | bytes 49160 | tf_op jit(solution)/shard_map/ppermute | solution.py:483

commit v9 on v7

--- a/solution.py
+++ b/solution.py
@@ -466,7 +466,7 @@
         out_specs=VMEM,
         compiler_params=PARAMS,
         name="join",
-    )(part, *pieces)
+    )(queries, *pieces)
     shards = [shard]
     for shift in range(1, across):
         shards.append(along(shard, "tp", shift))

time: 98.4 us -> 98.4 us (level)
  no operation moved by 1% of the time
where the time goes in v9:
time: 98.4 us; the launch traced here: 97.7 us
  starting transfers between devices  53.5 us (54%)
  blocking collectives  28.3 us (29%)
  Pallas kernels  7.71 us (8%)
  waiting for transfers between devices  6.68 us (7%)
    ppermute x9, starting transfers between devices, along(): lax.ppermute(x, axis, [(i, i ^ shift) for i in range(lax.axis_size(axis))])  34.8 us
    all_to_all x1, blocking collectives, per_device(): lax.all_to_all(packed, 'group', split_axis=0, concat_axis=1, tiled=True)  28.3 us
    all_to_all x1, starting transfers between devices, per_device(): lax.all_to_all(load, 'group', split_axis=0, concat_axis=0, tiled=True, ax...  11.8 us
    all_to_all x1, starting transfers between devices, per_device(): parts = lax.all_to_all(part, 'tp', split_axis=0, concat_axis=0, tiled=True)  4.53 us
    ppermute x9, waiting for transfers between devices, along(): lax.ppermute(x, axis, [(i, i ^ shift) for i in range(lax.axis_size(axis))])  3.59 us
    ppermute x1, starting transfers between devices, per_device(): lax.ppermute(jnp.concatenate([keep, got], axis=1), ('group', 'tp'), turn)  2.41 us
  transfers between devices with their start and end apart: 12, of which 4 were waited for; matrix products, arithmetic and copies ran while one was open for 0% of the time, Pallas kernels for 4%

profile of v9, /device:TPU:1, one launch (start us, length us, event | category | flops | bytes accessed | tf_op | source)
XLA Modules:
  0.0 97.7 jit_solution(16982231567045520946)
XLA Ops:
  0.6 1.7 %load.1 = (bf16[16,8,896]{2,1,0:T(8,128)(2,1)}, s32[1,16]{1,0:T(1,128)S(1)}) custom-call(s32[1,2]{1,0:T(1,128)} %bitcast.13, bf16[2,8,320]{2,1,0:T(8,128)(2,1)} %hidden_ref.1, bf16[10,1024]{1,0:T(8,128)(2,1)} %bitcast.9, f32[8,10]{1,0:T(8,128)} %bitcast.10, s32[2,1,8]{2,1,0:T(1,128)} %bitcast.12, s32[2,8]{1,0:T(2,128)} %ids_ref.1), custom_call_target="tpu_custom_call" | custom-call | tf_op jit(solution)/shard_map/load/pallas_call | solution.py:390
  2.3 11.8 %all-to-all-start = ((bf16[16,8,896]{2,1,0:T(8,128)(2,1)}), bf16[16,8,896]{2,1,0:T(8,128)(2,1)S(1)}, u32[]{:S(2)}, u32[]{:S(2)}) async-start(bf16[16,8,896]{2,1,0:T(8,128)(2,1)} %get-tuple-element.18), calls=%async_computation | async-start | bytes 458752 | tf_op jit(solution)/shard_map/all_to_all | solution.py:402
  14.1 1.1 %pieces.1 = (bf16[320,128]{1,0:T(8,128)(2,1)S(1)}, bf16[2,4,2,16,128]{4,3,2,1,0:T(8,128)(2,1)S(1)}, bf16[2,4,2,16,128]{4,3,2,1,0:T(8,128)(2,1)S(1)}, bf16[2,4,2,...) custom-call(bf16[320,128]{1,0:T(8,128)(2,1)} %codes_hbm.1, f32[1,320]{1,0:T(1,128)} %bitcast.11, ...), custom_call_target="tpu_custom_call" | custom-call | tf_op jit(solution)/shard_map/pieces/pallas_call | solution.py:407
  15.2 7.5 %collective-permute-start = (bf16[320,128]{1,0:T(8,128)(2,1)S(1)}, bf16[320,128]{1,0:T(8,128)(2,1)S(1)}, u32[]{:S(2)}, u32[]{:S(2)}) collective-permute-start(bf16[320,128]{1,0:T(8,128)(2,1)S(1)} %get-tuple-element.19.mine_ref), channel_id=1, source_target_pairs={{0,32},{16,48},{32,0},{48,16},{64,96},{80,112},{96,64},{112,80},{1... | collective-permute-start | bytes 245768 | tf_op jit(solution)/shard_map/ppermute | solution.py:380
  22.7 2.4 %collective-permute-start.3 = (bf16[2,4,2,16,128]{4,3,2,1,0:T(8,128)(2,1)S(1)}, bf16[2,4,2,16,128]{4,3,2,1,0:T(8,128)(2,1)S(1)}, u32[]{:S(2)}, u32[]{:S(2)}) collective-permute-start(bf16[2,4,2,16,128]{4,3,2,1,0:T(8,128)(2,1)S(1)} %get-tuple-element.26), channel_id=1, source_target_pairs={{0,8},{1,9},{2,10},{3,11},{4,12},{5,13},{6,14},{7,15},{8,0},{9,1},... | collective-permute-start | bytes 196616 | tf_op jit(solution)/shard_map/ppermute | solution.py:380
  25.2 3.9 %collective-permute-start.4 = (bf16[2,4,2,16,128]{4,3,2,1,0:T(8,128)(2,1)S(1)}, bf16[2,4,2,16,128]{4,3,2,1,0:T(8,128)(2,1)S(1)}, u32[]{:S(2)}, u32[]{:S(2)}) collective-permute-start(bf16[2,4,2,16,128]{4,3,2,1,0:T(8,128)(2,1)S(1)} %get-tuple-element.27), channel_id=1, source_target_pairs={{0,12},{1,13},{2,14},{3,15},{4,8},{5,9},{6,10},{7,11},{8,4},{9,5},... | collective-permute-start | bytes 196616 | tf_op jit(solution)/shard_map/ppermute | solution.py:380
  29.1 3.9 %collective-permute-start.1 = (bf16[2,128,128]{2,1,0:T(8,128)(2,1)S(1)}, bf16[2,128,128]{2,1,0:T(8,128)(2,1)S(1)}, u32[]{:S(2)}, u32[]{:S(2)}) collective-permute-start(bf16[2,128,128]{2,1,0:T(8,128)(2,1)S(1)} %get-tuple-element.24), channel_id=1, source_target_pairs={{0,32},{16,48},{32,0},{48,16},{64,96},{80,112},{96,64},{112,80},{1... | collective-permute-start | bytes 196616 | tf_op jit(solution)/shard_map/ppermute | solution.py:380
  33.0 2.3 %collective-permute-start.2 = (bf16[2,4,2,16,128]{4,3,2,1,0:T(8,128)(2,1)S(1)}, bf16[2,4,2,16,128]{4,3,2,1,0:T(8,128)(2,1)S(1)}, u32[]{:S(2)}, u32[]{:S(2)}) collective-permute-start(bf16[2,4,2,16,128]{4,3,2,1,0:T(8,128)(2,1)S(1)} %get-tuple-element.25), channel_id=1, source_target_pairs={{0,4},{1,5},{2,6},{3,7},{4,0},{5,1},{6,2},{7,3},{8,12},{9,13},{10,... | collective-permute-start | bytes 196616 | tf_op jit(solution)/shard_map/ppermute | solution.py:380
  35.3 1.7 %part.1 = (f32[16,16,256]{2,1,0:T(8,128)S(1)}, f32[16,16,128]{2,1,0:T(8,128)S(1)}, bf16[256,256]{1,0:T(8,128)(2,1)S(1)}) custom-call(bf16[16,8,896]{2,1,0:T(8,128)(2,1)S(1)} %all-to-all-done.came_ref, bf16[320,128]{1,0:T(8,128)(2,1)S(1)} %get-tuple-element.19.mine_ref, bf16[320,128]{1,0:T(8,128)(2,1)S(1)} %collective-permute-done.other_ref, ...), custom_call_target="tpu_custom_call" | custom-call | tf_op jit(solution)/shard_map/part/pallas_call | solution.py:436
  37.0 2.8 %collective-permute-done.1.other_ref = bf16[2,128,128]{2,1,0:T(8,128)(2,1)S(1)} collective-permute-done((bf16[2,128,128]{2,1,0:T(8,128)(2,1)S(1)}, bf16[2,128,128]{2,1,0:T(8,128)(2,1)S(1)}, u32[]{:S(2)}, u32[]{:S(2)}) %collective-permute-start.1) | collective-permute-done | bytes 65568 | tf_op jit(solution)/shard_map/ppermute | solution.py:380
  39.8 0.9 whole.1
  40.7 4.5 %all-to-all-start.1 = ((f32[16,16,384]{2,1,0:T(8,128)}), f32[16,16,384]{2,1,0:T(8,128)S(1)}, u32[]{:S(2)}, u32[]{:S(2)}) async-start(f32[16,16,384]{2,1,0:T(8,128)} %whole.1), calls=%async_computation.1 | async-start | bytes 786432 | tf_op jit(solution)/shard_map/all_to_all | solution.py:460
  45.3 4.5 %collective-permute-start.9 = (bf16[4,2,4,2,16,128]{5,4,3,2,1,0:T(8,128)(2,1)S(1)}, bf16[4,2,4,2,16,128]{5,4,3,2,1,0:T(8,128)(2,1)S(1)}, u32[]{:S(2)}, u32[]{:S(2)}) collective-permute-start(bf16[4,2,4,2,16,128]{5,4,3,2,1,0:T(8,128)(2,1)S(1)} %join.1.shard0_ref), channel_id=1, source_target_pairs={{0,3},{1,2},{2,1},{3,0},{4,7},{5,6},{6,5},{7,4},{8,11},{9,10},{10,... | collective-permute-start | bytes 786440 | tf_op jit(solution)/shard_map/ppermute | solution.py:380
  49.8 2.5 %collective-permute-start.8 = (bf16[4,2,4,2,16,128]{5,4,3,2,1,0:T(8,128)(2,1)S(1)}, bf16[4,2,4,2,16,128]{5,4,3,2,1,0:T(8,128)(2,1)S(1)}, u32[]{:S(2)}, u32[]{:S(2)}) collective-permute-start(bf16[4,2,4,2,16,128]{5,4,3,2,1,0:T(8,128)(2,1)S(1)} %join.1.shard0_ref), channel_id=1, source_target_pairs={{0,2},{1,3},{2,0},{3,1},{4,6},{5,7},{6,4},{7,5},{8,10},{9,11},{10,... | collective-permute-start | bytes 786440 | tf_op jit(solution)/shard_map/ppermute | solution.py:380
  52.3 2.0 %collective-permute-start.7 = (bf16[4,2,4,2,16,128]{5,4,3,2,1,0:T(8,128)(2,1)S(1)}, bf16[4,2,4,2,16,128]{5,4,3,2,1,0:T(8,128)(2,1)S(1)}, u32[]{:S(2)}, u32[]{:S(2)}) collective-permute-start(bf16[4,2,4,2,16,128]{5,4,3,2,1,0:T(8,128)(2,1)S(1)} %join.1.shard0_ref), channel_id=1, source_target_pairs={{0,1},{1,0},{2,3},{3,2},{4,5},{5,4},{6,7},{7,6},{8,9},{9,8},{10,11... | collective-permute-start | bytes 786440 | tf_op jit(solution)/shard_map/ppermute | solution.py:380
  54.3 1.2 %all-to-all-done.1.parts_ref.after_ref = f32[16,16,384]{2,1,0:T(8,128)S(1)} async-done(((f32[16,16,384]{2,1,0:T(8,128)}), f32[16,16,384]{2,1,0:T(8,128)S(1)}, u32[]{:S(2)}, u32[]{:S(2)}) %all-to-all-start.1) | async-done | bytes 393248 | tf_op jit(solution)/shard_map/all_to_all | solution.py:460
  55.6 5.8 %collective-permute-start.5 = (bf16[16,256]{1,0:T(8,128)(2,1)S(1)}, bf16[16,256]{1,0:T(8,128)(2,1)S(1)}, u32[]{:S(2)}, u32[]{:S(2)}) collective-permute-start(bf16[16,256]{1,0:T(8,128)(2,1)S(1)} %get-tuple-element.29), channel_id=1, source_target_pairs={{0,16},{16,0},{32,48},{48,32},{64,80},{80,64},{96,112},{112,96},{1... | collective-permute-start | bytes 24584 | tf_op jit(solution)/shard_map/ppermute | solution.py:380
  61.4 0.8 collective-permute-done.5
  62.2 2.4 %collective-permute-start.6 = (bf16[16,512]{1,0:T(8,128)(2,1)S(1)}, bf16[16,512]{1,0:T(8,128)(2,1)S(1)}, u32[]{:S(2)}, u32[]{:S(2)}) collective-permute-start(bf16[16,512]{1,0:T(8,128)(2,1)S(1)} %pad_maximum_fusion), channel_id=1, source_target_pairs={{0,0},{1,16},{2,64},{3,80},{4,128},{5,144},{6,192},{7,208},{8,256}... | collective-permute-start | bytes 49160 | tf_op jit(solution)/shard_map/ppermute | solution.py:482
  64.7 0.8 facts.1
  65.4 1.8 %collective-permute-done.6.mine_ref = bf16[16,512]{1,0:T(8,128)(2,1)S(1)} collective-permute-done((bf16[16,512]{1,0:T(8,128)(2,1)S(1)}, bf16[16,512]{1,0:T(8,128)(2,1)S(1)}, u32[]{:S(2)}, u32[]{:S(2)}) %collective-permute-start.6) | collective-permute-done | bytes 16416 | tf_op jit(solution)/shard_map/ppermute | solution.py:482
  67.3 1.4 %attend.1 = bf16[32,2,256]{2,1,0:T(2,128)(2,1)S(1)} custom-call(s32[2]{0:T(128)S(1)} %copy-done, bf16[16,512]{1,0:T(8,128)(2,1)S(1)} %collective-permute-done.6.mine_ref, bf16[64,16]{1,0:T(8,128)(2,1)S(1)} %get-tuple-element.31.placed_ref, bf16[4,2,4,2,16,128]{5,4,3,2,1,0:T(8,128)(2,1)S(1)} %join.1.shard0_ref, ...), custom_call_target="tpu_custom_call" | custom-call | tf_op jit(solution)/shard_map/attend/pallas_call | solution.py:496
  68.7 28.3 %all_to_all.22 = bf16[32,2,256]{2,1,0:T(2,128)(2,1)S(1)} all-to-all(bf16[32,2,256]{2,1,0:T(2,128)(2,1)S(1)} %attend.1), channel_id=1, replica_groups=mesh['group'=32,'tp'=16] {'group'}, dimensions={0} | all-to-all | bytes 65536 | tf_op jit(solution)/shard_map/all_to_all | solution.py:504
  97.0 0.6 all_to_all.18
  (14 shorter events, 0.1 us)
Async XLA Ops:
  2.3 26.8 %all-to-all-start = ((bf16[16,8,896]{2,1,0:T(8,128)(2,1)}), bf16[16,8,896]{2,1,0:T(8,128)(2,1)S(1)}, u32[]{:S(2)}, u32[]{:S(2)}) async-start(bf16[16,8,896]{2,1,0:T(8,128)(2,1)} %get-tuple-element.18), calls=%async_computation | async-start | bytes 458752 | tf_op jit(solution)/shard_map/all_to_all | solution.py:402
  15.2 20.0 %collective-permute-start = (bf16[320,128]{1,0:T(8,128)(2,1)S(1)}, bf16[320,128]{1,0:T(8,128)(2,1)S(1)}, u32[]{:S(2)}, u32[]{:S(2)}) collective-permute-start(bf16[320,128]{1,0:T(8,128)(2,1)S(1)} %get-tuple-element.19.mine_ref), channel_id=1, source_target_pairs={{0,32},{16,48},{32,0},{48,16},{64,96},{80,112},{96,64},{112,80},{1... | collective-permute-start | bytes 245768 | tf_op jit(solution)/shard_map/ppermute | solution.py:380
  22.7 14.3 %collective-permute-start.3 = (bf16[2,4,2,16,128]{4,3,2,1,0:T(8,128)(2,1)S(1)}, bf16[2,4,2,16,128]{4,3,2,1,0:T(8,128)(2,1)S(1)}, u32[]{:S(2)}, u32[]{:S(2)}) collective-permute-start(bf16[2,4,2,16,128]{4,3,2,1,0:T(8,128)(2,1)S(1)} %get-tuple-element.26), channel_id=1, source_target_pairs={{0,8},{1,9},{2,10},{3,11},{4,12},{5,13},{6,14},{7,15},{8,0},{9,1},... | collective-permute-start | bytes 196616 | tf_op jit(solution)/shard_map/ppermute | solution.py:380
  25.2 11.9 %collective-permute-start.4 = (bf16[2,4,2,16,128]{4,3,2,1,0:T(8,128)(2,1)S(1)}, bf16[2,4,2,16,128]{4,3,2,1,0:T(8,128)(2,1)S(1)}, u32[]{:S(2)}, u32[]{:S(2)}) collective-permute-start(bf16[2,4,2,16,128]{4,3,2,1,0:T(8,128)(2,1)S(1)} %get-tuple-element.27), channel_id=1, source_target_pairs={{0,12},{1,13},{2,14},{3,15},{4,8},{5,9},{6,10},{7,11},{8,4},{9,5},... | collective-permute-start | bytes 196616 | tf_op jit(solution)/shard_map/ppermute | solution.py:380
  29.1 10.7 %collective-permute-start.1 = (bf16[2,128,128]{2,1,0:T(8,128)(2,1)S(1)}, bf16[2,128,128]{2,1,0:T(8,128)(2,1)S(1)}, u32[]{:S(2)}, u32[]{:S(2)}) collective-permute-start(bf16[2,128,128]{2,1,0:T(8,128)(2,1)S(1)} %get-tuple-element.24), channel_id=1, source_target_pairs={{0,32},{16,48},{32,0},{48,16},{64,96},{80,112},{96,64},{112,80},{1... | collective-permute-start | bytes 196616 | tf_op jit(solution)/shard_map/ppermute | solution.py:380
  33.0 6.9 %collective-permute-start.2 = (bf16[2,4,2,16,128]{4,3,2,1,0:T(8,128)(2,1)S(1)}, bf16[2,4,2,16,128]{4,3,2,1,0:T(8,128)(2,1)S(1)}, u32[]{:S(2)}, u32[]{:S(2)}) collective-permute-start(bf16[2,4,2,16,128]{4,3,2,1,0:T(8,128)(2,1)S(1)} %get-tuple-element.25), channel_id=1, source_target_pairs={{0,4},{1,5},{2,6},{3,7},{4,0},{5,1},{6,2},{7,3},{8,12},{9,13},{10,... | collective-permute-start | bytes 196616 | tf_op jit(solution)/shard_map/ppermute | solution.py:380
  37.0 30.3 %copy-start = (s32[2]{0:T(128)S(1)}, s32[2]{0:T(128)}, u32[]{:S(2)}) copy-start(s32[2]{0:T(128)} %lengths_ref.1) | copy-start | bytes 28
  40.7 14.8 %all-to-all-start.1 = ((f32[16,16,384]{2,1,0:T(8,128)}), f32[16,16,384]{2,1,0:T(8,128)S(1)}, u32[]{:S(2)}, u32[]{:S(2)}) async-start(f32[16,16,384]{2,1,0:T(8,128)} %whole.1), calls=%async_computation.1 | async-start | bytes 786432 | tf_op jit(solution)/shard_map/all_to_all | solution.py:460
  45.3 20.1 %collective-permute-start.9 = (bf16[4,2,4,2,16,128]{5,4,3,2,1,0:T(8,128)(2,1)S(1)}, bf16[4,2,4,2,16,128]{5,4,3,2,1,0:T(8,128)(2,1)S(1)}, u32[]{:S(2)}, u32[]{:S(2)}) collective-permute-start(bf16[4,2,4,2,16,128]{5,4,3,2,1,0:T(8,128)(2,1)S(1)} %join.1.shard0_ref), channel_id=1, source_target_pairs={{0,3},{1,2},{2,1},{3,0},{4,7},{5,6},{6,5},{7,4},{8,11},{9,10},{10,... | collective-permute-start | bytes 786440 | tf_op jit(solution)/shard_map/ppermute | solution.py:380
  49.8 15.6 %collective-permute-start.8 = (bf16[4,2,4,2,16,128]{5,4,3,2,1,0:T(8,128)(2,1)S(1)}, bf16[4,2,4,2,16,128]{5,4,3,2,1,0:T(8,128)(2,1)S(1)}, u32[]{:S(2)}, u32[]{:S(2)}) collective-permute-start(bf16[4,2,4,2,16,128]{5,4,3,2,1,0:T(8,128)(2,1)S(1)} %join.1.shard0_ref), channel_id=1, source_target_pairs={{0,2},{1,3},{2,0},{3,1},{4,6},{5,7},{6,4},{7,5},{8,10},{9,11},{10,... | collective-permute-start | bytes 786440 | tf_op jit(solution)/shard_map/ppermute | solution.py:380
  52.3 13.2 %collective-permute-start.7 = (bf16[4,2,4,2,16,128]{5,4,3,2,1,0:T(8,128)(2,1)S(1)}, bf16[4,2,4,2,16,128]{5,4,3,2,1,0:T(8,128)(2,1)S(1)}, u32[]{:S(2)}, u32[]{:S(2)}) collective-permute-start(bf16[4,2,4,2,16,128]{5,4,3,2,1,0:T(8,128)(2,1)S(1)} %join.1.shard0_ref), channel_id=1, source_target_pairs={{0,1},{1,0},{2,3},{3,2},{4,5},{5,4},{6,7},{7,6},{8,9},{9,8},{10,11... | collective-permute-start | bytes 786440 | tf_op jit(solution)/shard_map/ppermute | solution.py:380
  55.6 6.6 %collective-permute-start.5 = (bf16[16,256]{1,0:T(8,128)(2,1)S(1)}, bf16[16,256]{1,0:T(8,128)(2,1)S(1)}, u32[]{:S(2)}, u32[]{:S(2)}) collective-permute-start(bf16[16,256]{1,0:T(8,128)(2,1)S(1)} %get-tuple-element.29), channel_id=1, source_target_pairs={{0,16},{16,0},{32,48},{48,32},{64,80},{80,64},{96,112},{112,96},{1... | collective-permute-start | bytes 24584 | tf_op jit(solution)/shard_map/ppermute | solution.py:380
  62.2 5.0 %collective-permute-start.6 = (bf16[16,512]{1,0:T(8,128)(2,1)S(1)}, bf16[16,512]{1,0:T(8,128)(2,1)S(1)}, u32[]{:S(2)}, u32[]{:S(2)}) collective-permute-start(bf16[16,512]{1,0:T(8,128)(2,1)S(1)} %pad_maximum_fusion), channel_id=1, source_target_pairs={{0,0},{1,16},{2,64},{3,80},{4,128},{5,144},{6,192},{7,208},{8,256}... | collective-permute-start | bytes 49160 | tf_op jit(solution)/shard_map/ppermute | solution.py:482
